TPU v7x, 256 devices: a whole 4x4x8 slice. The times are simulated.
256 devices in a mesh: role: 4 (over x_lo, core), rep: 8 (over y, x_hi), tp: 8 (over z).
Axes of the slice: x: 4 (x_hi: 2, x_lo: 2; x = x_hi * 2 + x_lo), y: 4, z: 8, core: 2. Of those that a mesh axis runs over, the one named last changes fastest.
Arguments:
- master: float32 [16384, 1024], P(('tp', 'role', 'rep')), may hold values from -6 to 6
- moment: float32 [16384, 1024], P(('tp', 'role', 'rep')), may hold values from -6 to 6
- second: float32 [16384, 1024], P(('tp', 'role', 'rep')), may hold values from 0.25 to 4
- gradient: float32 [16384, 1024], P(('tp', 'role', 'rep')), may hold values from -6 to 6
- step_count: int32 [1], replicated, may hold values from 1 to 8
- old_weights: bfloat16 [16384, 1024], P('tp'), may hold values from -0.046875 to 0.046875
- branch_rows: bfloat16 [16384, 16384], P(('role', 'rep'), 'tp'), may hold values from -6 to 6
- assignment: int32 [16384, 1], P(('role', 'rep')), may hold values from 0 to 31; in each aligned block of 512 rows (0 to 511, 512 to 1023, ...) at most 32 rows name the same one
Outputs:
- new_master: float32 [16384, 1024], P(('tp', 'role', 'rep'))
- new_moment: float32 [16384, 1024], P(('tp', 'role', 'rep'))
- new_second: float32 [16384, 1024], P(('tp', 'role', 'rep'))
- rollout_weights: bfloat16 [16384, 1024], P('tp')
- branch_keys: bfloat16 [32, 32, 32, 1024], P(('role', 'rep'), None, None, 'tp')
Inputs may be any that keep to these rules, and one draw needn't show every extreme that they name: `assignment`: in each aligned block of 512 rows (the rows that start on one replica) no replica is named by more than 32 rows; some replica is named by exactly 32 rows of some block.
All inputs are finite; a program needn't handle non-finite values.
Results may differ from a plain program's by a relative error of at most 0.001.
Values may be sent and summed in bfloat16 or wider, within the bound.
No kernel may reach another device: no remote copies, remote signals or barrier semaphores. Data moves between devices by JAX's collectives and lax.ppermute only.
A program may use at most 64 MiB of HBM per device.

v0:
```python
import jax
import jax.numpy as jnp
from jax import lax
from jax.sharding import PartitionSpec as P

learn_rate = 0.05
decay_rate = 0.1


def combine_width(partial_value):
    width = partial_value.shape[1] // lax.axis_size("tp")
    total = lax.psum(partial_value, "tp")
    result = lax.dynamic_slice_in_dim(total, lax.axis_index("tp") * width, width, 1)
    return result


def slot_matrix(assignment, replicas, slots_each):
    target = assignment[:, 0]
    targets = jnp.arange(replicas, dtype=jnp.int32)
    onehot = (target[:, None] == targets[None, :]).astype(jnp.int32)
    ranks = jnp.sum((jnp.cumsum(onehot, axis=0) - 1) * onehot, axis=1)
    position = target * slots_each + ranks
    places = jnp.arange(replicas * slots_each, dtype=jnp.int32)
    return (places[:, None] == position[None, :]).astype(jnp.bfloat16)


def local(master, moment, second, gradient, step_count, old_weights, branch_rows, assignment):
    steps_f = step_count[0].astype(jnp.float32)
    first_fix = 1.0 - jnp.power(jnp.float32(0.9), steps_f)
    second_fix = 1.0 - jnp.power(jnp.float32(0.95), steps_f)
    new_moment = 0.9 * moment + 0.1 * gradient
    new_second = 0.95 * second + 0.05 * gradient * gradient
    update = new_moment / first_fix / (jnp.sqrt(new_second / second_fix) + 1e-08)
    new_master = master - learn_rate * (update + decay_rate * master)
    rollout_weights = lax.all_gather(
        new_master.astype(jnp.bfloat16), ("role", "rep"), axis=0, tiled=True
    )
    replicas = lax.axis_size(("role", "rep"))
    rows_here = branch_rows.shape[0]
    slots_each = 2 * rows_here // replicas
    selector = slot_matrix(assignment, replicas, slots_each)
    placed = jnp.dot(selector, branch_rows, preferred_element_type=jnp.float32).astype(jnp.bfloat16)
    placed = placed.reshape(replicas, slots_each, branch_rows.shape[1])
    arrived = lax.all_to_all(placed, ("role", "rep"), split_axis=0, concat_axis=0, tiled=True)
    flat = arrived.reshape(replicas * slots_each, branch_rows.shape[1])
    partial_value = jnp.dot(flat, old_weights, preferred_element_type=jnp.float32)
    keys = combine_width(partial_value).astype(jnp.bfloat16)
    branch_keys = keys.reshape(1, replicas, slots_each, keys.shape[1])
    return (new_master, new_moment, new_second, rollout_weights, branch_keys)


def solution(mesh):
    placed = (
        P(("tp", "role", "rep"), None),
        P(("tp", "role", "rep"), None),
        P(("tp", "role", "rep"), None),
        P(("tp", "role", "rep"), None),
        P(),
        P("tp", None),
        P(("role", "rep"), "tp"),
        P(("role", "rep"), None),
    )
    return jax.shard_map(
        local,
        mesh=mesh,
        in_specs=placed,
        out_specs=(
            P(("tp", "role", "rep"), None),
            P(("tp", "role", "rep"), None),
            P(("tp", "role", "rep"), None),
            P("tp", None),
            P(("role", "rep"), None, None, "tp"),
        ),
        check_vma=False,
    )
```

profile of v0, /device:TPU:24, one launch (start us, length us, event | category | flops | bytes accessed | tf_op | source)
XLA Modules:
  0.0 194.3 jit_solution(15422282525727073729)
XLA Ops:
  7.2 0.0 copy-start
  7.2 0.8 fusion.4
  8.0 1.2 reduce-window.6
  9.2 0.2 slice_reduce_fusion
  9.4 0.8 fusion.3
  10.2 0.7 multiply_add_fusion.1
  10.9 0.0 copy-done
  10.9 4.3 %convolution_convert_fusion = bf16[1024,2048]{1,0:T(8,128)(2,1)} fusion(bf16[512,2048]{1,0:T(8,128)(2,1)S(1)} %copy-done, s32[512]{0:T(512)S(1)} %multiply_add_fusion.1), kind=kOutput, calls=%fused_computation | convolution fusion | flops 2150105088 | bytes 6293504 | tf_op jit(solution)/shard_map/dot_general | solution.py:42
  15.3 0.0 copy-start.1
  15.3 0.0 copy-start.2
  15.3 0.0 copy-start.3
  15.3 0.0 copy-start.4
  15.3 7.5 %all-to-all-start = ((bf16[32,32,2048]{2,1,0:T(8,128)(2,1)}), bf16[32,32,2048]{2,1,0:T(8,128)(2,1)}, u32[]{:S(2)}, u32[]{:S(2)}) async-start(bf16[32,32,2048]{2,1,0:T(8,128)(2,1)} %bitcast.25), calls=%async_computation | async-start | bytes 8388608 | tf_op jit(solution)/shard_map/all_to_all | solution.py:44
  22.8 0.0 all-gather.2.cloned.1.call-start
  23.6 0.0 copy-done.1
  23.6 0.0 copy-done.2
  23.6 0.0 copy-done.3
  23.6 0.0 copy-done.4
  23.6 1.0 fusion.5
  24.6 0.0 all-gather.2.cloned.1.call-update
  24.7 54.4 %all-to-all-done = bf16[32,32,2048]{2,1,0:T(8,128)(2,1)} async-done(((bf16[32,32,2048]{2,1,0:T(8,128)(2,1)}), bf16[32,32,2048]{2,1,0:T(8,128)(2,1)}, u32[]{:S(2)}, u32[]{:S(2)}) %all-to-all-start) | async-done | bytes 4194336 | tf_op jit(solution)/shard_map/all_to_all | solution.py:44
  79.1 10.0 %fusion.7 = f32[1024,1024]{1,0:T(8,128)} fusion(bf16[1024,2048]{1,0:T(8,128)(2,1)} %bitcast.6, bf16[2048,1024]{1,0:T(8,128)(2,1)} %param.13), kind=kOutput, calls=%fused_computation.18 | convolution fusion | flops 4294967296 | bytes 12582912 | tf_op jit(solution)/shard_map/dot_general | solution.py:46
  89.0 92.1 %all-reduce.1 = bf16[1024,1024]{1,0:T(8,128)(2,1)} all-reduce(f32[1024,1024]{1,0:T(8,128)} %fusion.7), channel_id=1, replica_groups=mesh['role'=4,'rep'=8,'tp'=8] {'tp'}, use_global_device_ids=true, to_apply=%region_3.4 | all-reduce | flops 1048576 | bytes 6291456 | tf_op jit(solution)/shard_map/psum | solution.py:12
  181.2 1.7 dynamic-slice_convert_fusion
  182.8 0.0 all-gather.2.cloned.1.call-done
  182.8 4.6 %copy.20 = bf16[2048,1024]{1,0:T(8,128)(2,1)} copy(bf16[2048,1024]{1,0:T(8,128)(2,1)} %all-gather.2.cloned.1.call-done) | data formatting | bytes 8388608
  (2 shorter events, 0.0 us)
Async XLA Ops:
  7.2 3.8 %copy-start = (bf16[512,2048]{1,0:T(8,128)(2,1)S(1)}, bf16[512,2048]{1,0:T(8,128)(2,1)}, u32[]{:S(2)}) copy-start(bf16[512,2048]{1,0:T(8,128)(2,1)} %param.14) | copy-start | bytes 6291460
  15.3 8.3 %copy-start.1 = (f32[64,1024]{1,0:T(8,128)S(1)}, f32[64,1024]{1,0:T(8,128)}, u32[]{:S(2)}) copy-start(f32[64,1024]{1,0:T(8,128)} %param.8) | copy-start | bytes 786436
  15.3 8.3 %copy-start.2 = (f32[64,1024]{1,0:T(8,128)S(1)}, f32[64,1024]{1,0:T(8,128)}, u32[]{:S(2)}) copy-start(f32[64,1024]{1,0:T(8,128)} %param.11) | copy-start | bytes 786436
  15.3 8.3 %copy-start.3 = (f32[64,1024]{1,0:T(8,128)S(1)}, f32[64,1024]{1,0:T(8,128)}, u32[]{:S(2)}) copy-start(f32[64,1024]{1,0:T(8,128)} %param.10) | copy-start | bytes 786436
  15.3 8.3 %copy-start.4 = (f32[64,1024]{1,0:T(8,128)S(1)}, f32[64,1024]{1,0:T(8,128)}, u32[]{:S(2)}) copy-start(f32[64,1024]{1,0:T(8,128)} %param.9) | copy-start | bytes 786436
  15.3 63.8 %all-to-all-start = ((bf16[32,32,2048]{2,1,0:T(8,128)(2,1)}), bf16[32,32,2048]{2,1,0:T(8,128)(2,1)}, u32[]{:S(2)}, u32[]{:S(2)}) async-start(bf16[32,32,2048]{2,1,0:T(8,128)(2,1)} %bitcast.25), calls=%async_computation | async-start | bytes 8388608 | tf_op jit(solution)/shard_map/all_to_all | solution.py:44
  22.8 160.0 %all-gather.2.cloned.1.call-start = ((), (), s32[]{:S(2)}) async-start(), calls=%async_computation.1 | async-start | bytes 4325376 | tf_op jit(solution)/shard_map/all_gather | solution.py:35
Sparse Core Ops, SparseCore 0:
  25.4 116.5 all-gather.1
where the time goes:
time: 195 us; the launch traced here: 194 us
  blocking collectives  92.1 us (47%)
  waiting for transfers between devices  54.4 us (28%)
  between operations  14.8 us (8%)
  matrix products  14.3 us (7%)
  starting transfers between devices  7.55 us (4%)
  local copies, waits for them, and re-layouts  6.56 us (3%)
  other arithmetic  4.54 us (2%)
    psum x1, blocking collectives, combine_width(): total = lax.psum(partial_value, 'tp')  92.1 us
    all_to_all x1, waiting for transfers between devices, local(): lax.all_to_all(placed, ('role', 'rep'), split_axis=0, concat_axis=0, tile...  54.4 us
    dot_general x1, matrix products, local(): jnp.dot(flat, old_weights, preferred_element_type=jnp.float32)  9.96 us
    all_to_all x1, starting transfers between devices, local(): lax.all_to_all(placed, ('role', 'rep'), split_axis=0, concat_axis=0, tile...  7.51 us
    unnamed x11, local copies, waits for them, and re-layouts  4.66 us
    dot_general x1, matrix products, local(): jnp.dot(selector, branch_rows, preferred_element_type=jnp.float32)  4.35 us
  transfers between devices with their start and end apart: 2, of which 1 were waited for; matrix products, arithmetic and copies ran while one was open for 7% of the time, Pallas kernels for 0%

commit v1 on v0

--- a/solution.py
+++ b/solution.py
@@ -5,13 +5,6 @@
 
 learn_rate = 0.05
 decay_rate = 0.1
-
-
-def combine_width(partial_value):
-    width = partial_value.shape[1] // lax.axis_size("tp")
-    total = lax.psum(partial_value, "tp")
-    result = lax.dynamic_slice_in_dim(total, lax.axis_index("tp") * width, width, 1)
-    return result
 
 
 def slot_matrix(assignment, replicas, slots_each):
@@ -39,13 +32,12 @@
     rows_here = branch_rows.shape[0]
     slots_each = 2 * rows_here // replicas
     selector = slot_matrix(assignment, replicas, slots_each)
-    placed = jnp.dot(selector, branch_rows, preferred_element_type=jnp.float32).astype(jnp.bfloat16)
-    placed = placed.reshape(replicas, slots_each, branch_rows.shape[1])
+    partial_value = jnp.dot(branch_rows, old_weights, preferred_element_type=jnp.float32)
+    keys = lax.psum_scatter(partial_value, "tp", scatter_dimension=1, tiled=True).astype(jnp.bfloat16)
+    placed = jnp.dot(selector, keys, preferred_element_type=jnp.float32).astype(jnp.bfloat16)
+    placed = placed.reshape(replicas, slots_each, keys.shape[1])
     arrived = lax.all_to_all(placed, ("role", "rep"), split_axis=0, concat_axis=0, tiled=True)
-    flat = arrived.reshape(replicas * slots_each, branch_rows.shape[1])
-    partial_value = jnp.dot(flat, old_weights, preferred_element_type=jnp.float32)
-    keys = combine_width(partial_value).astype(jnp.bfloat16)
-    branch_keys = keys.reshape(1, replicas, slots_each, keys.shape[1])
+    branch_keys = arrived.reshape(1, replicas, slots_each, keys.shape[1])
     return (new_master, new_moment, new_second, rollout_weights, branch_keys)
 
 

time: 195 us -> 126 us (0.65)
  the two profiles are of different devices: /device:TPU:24 before, /device:TPU:1 now
where the time goes in v1:
time: 126 us; the launch traced here: 125 us
  waiting for transfers between devices  70.8 us (56%)
  blocking collectives  21.2 us (17%)
  between operations  16.3 us (13%)
  local copies, waits for them, and re-layouts  7.43 us (6%)
  matrix products  7.26 us (6%)
  other arithmetic  2.36 us (2%)
    reduce_scatter x1, waiting for transfers between devices, local(): lax.psum_scatter(partial_value, 'tp', scatter_dimension=1, tiled=True)  37.9 us
    all_gather x1, waiting for transfers between devices, local(): lax.all_gather(new_master.astype(jnp.bfloat16), ('role', 'rep'), axis=0,...  32.9 us
    all_to_all x1, blocking collectives, local(): lax.all_to_all(placed, ('role', 'rep'), split_axis=0, concat_axis=0, tile...  21.2 us
    unnamed x14, local copies, waits for them, and re-layouts  7.2 us
    dot_general x1, matrix products, local(): jnp.dot(branch_rows, old_weights, preferred_element_type=jnp.float32)  5.84 us
  transfers between devices with their start and end apart: 2, of which 2 were waited for; matrix products, arithmetic and copies ran while one was open for 3% of the time, Pallas kernels for 0%

profile of v1, /device:TPU:1, one launch (start us, length us, event | category | flops | bytes accessed | tf_op | source)
XLA Modules:
  0.0 125.5 jit_solution(14629290608573552491)
XLA Ops:
  8.0 0.0 copy-start
  8.0 0.0 reduce-scatter.2.cloned.1.call-start
  8.1 1.5 %copy-done = bf16[512,2048]{1,0:T(8,128)(2,1)S(1)} copy-done((bf16[512,2048]{1,0:T(8,128)(2,1)S(1)}, bf16[512,2048]{1,0:T(8,128)(2,1)}, u32[]{:S(2)}) %copy-start) | copy-done | bytes 2097176
  9.6 5.8 %fusion.10 = f32[512,1024]{1,0:T(8,128)} fusion(bf16[512,2048]{1,0:T(8,128)(2,1)S(1)} %copy-done, bf16[2048,1024]{1,0:T(8,128)(2,1)} %param.13), kind=kOutput, calls=%fused_computation.19 | convolution fusion | flops 2147483648 | bytes 8388608 | tf_op jit(solution)/shard_map/dot_general | solution.py:35
  15.4 0.0 copy-start.1
  15.4 0.0 copy-start.2
  15.4 0.0 copy-start.3
  15.4 0.0 copy-start.4
  15.4 0.0 copy-start.5
  15.5 0.0 reduce-scatter.2.cloned.1.call-update
  15.5 0.0 all-gather.2.cloned.1.call-start
  16.3 0.0 copy-done.1
  16.4 0.1 copy-done.2
  16.5 0.1 copy-done.3
  16.6 0.1 copy-done.4
  16.6 1.0 fusion.8
  17.7 0.0 all-gather.2.cloned.1.call-update
  17.7 0.0 copy-done.5
  17.7 1.2 reduce-window.6
  18.9 0.2 slice_reduce_fusion
  19.2 0.1 fusion.6
  19.3 37.9 %reduce-scatter.2.cloned.1.call-done = f32[512,128]{1,0:T(8,128)} async-done(((f32[512,1024]{1,0:T(8,128)}), f32[512,128]{1,0:T(8,128)}) %reduce-scatter.2.cloned.1.call-update) | async-done | bytes 262160 | tf_op jit(solution)/shard_map/reduce_scatter | solution.py:36
  57.2 1.4 %fusion.1 = bf16[1024,128]{1,0:T(8,128)(2,1)S(1)} fusion(s32[512]{0:T(512)S(1)} %multiply_add_fusion.1, f32[512,128]{1,0:T(8,128)} %reduce-scatter.2.cloned.1.call-done), kind=kOutput, calls=%fused_computation.2 | convolution fusion | flops 134938624 | bytes 526336 | tf_op jit(solution)/shard_map/dot_general | solution.py:37
  58.6 21.2 %all_to_all.5 = bf16[32,32,128]{2,1,0:T(8,128)(2,1)S(1)} all-to-all(bf16[32,32,128]{2,1,0:T(8,128)(2,1)S(1)} %bitcast.24), channel_id=1, replica_groups=mesh['role'=4,'rep'=8,'tp'=8] {'role','rep'}, dimensions={0} | all-to-all | bytes 524288 | tf_op jit(solution)/shard_map/all_to_all | solution.py:39
  79.8 32.9 %all-gather.2.cloned.1.call-done = bf16[2048,1024]{1,0:T(8,128)(2,1)} async-done(((bf16[64,1024]{1,0:T(8,128)(2,1)}), bf16[2048,1024]{1,0:T(8,128)(2,1)}) %all-gather.2.cloned.1.call-update) | async-done | bytes 4194320 | tf_op jit(solution)/shard_map/all_gather | solution.py:28
  112.7 4.6 %copy.19 = bf16[2048,1024]{1,0:T(8,128)(2,1)} copy(bf16[2048,1024]{1,0:T(8,128)(2,1)} %all-gather.2.cloned.1.call-done) | data formatting | bytes 8388608
  117.4 0.7 copy.20
  (4 shorter events, 0.1 us)
Async XLA Ops:
  8.0 1.6 %copy-start = (bf16[512,2048]{1,0:T(8,128)(2,1)S(1)}, bf16[512,2048]{1,0:T(8,128)(2,1)}, u32[]{:S(2)}) copy-start(bf16[512,2048]{1,0:T(8,128)(2,1)} %param.14) | copy-start | bytes 6291460
  8.0 49.2 %reduce-scatter.2.cloned.1.call-start = ((), (), s32[]{:S(2)}) async-start(), calls=%async_computation.3 | async-start | bytes 2359296 | tf_op jit(solution)/shard_map/reduce_scatter | solution.py:36
  15.4 0.9 copy-start.1
  15.4 1.0 copy-start.2
  15.4 1.1 copy-start.3
  15.4 1.2 copy-start.4
  15.4 2.3 %copy-start.5 = (s32[512,1]{0,1:T(1,128)S(1)}, s32[512,1]{0,1:T(1,128)}, u32[]{:S(2)}) copy-start(s32[512,1]{0,1:T(1,128)} %param.15) | copy-start | bytes 6148
  15.5 97.2 %all-gather.2.cloned.1.call-start = ((), (), s32[]{:S(2)}) async-start(), calls=%async_computation.2 | async-start | bytes 4325376 | tf_op jit(solution)/shard_map/all_gather | solution.py:28
Sparse Core Ops, SparseCore 0:
  15.6 41.5 reduce-scatter.1
Sparse Core Ops, SparseCore 1:
  18.3 94.3 all-gather.1

commit v2 on v1

v2 whole, which is shorter than its diff:
```python
import functools

import jax
import jax.numpy as jnp
from jax import lax
from jax.experimental import pallas as pl
from jax.experimental.pallas import tpu as pltpu
from jax.sharding import Mesh
from jax.sharding import PartitionSpec as P

learn_rate = 0.05
decay_rate = 0.1

PLANE = ("xlo", "core", "y", "xhi")
CHIPS = ("xlo", "y", "xhi")
LEVELS = 32767.0
TAIL = 16


def coded(value):
    top = jnp.maximum(jnp.max(jnp.abs(value), axis=0, keepdims=True), 1.2e-38)
    power = jnp.ceil(jnp.log(top) * (256.0 / 0.6931471805599453) + 0.01)
    power = jnp.clip(power, -32256.0, 32256.0)
    scaled = value * jnp.exp2(power * (-1.0 / 256.0)) * LEVELS
    codes = jnp.clip(jnp.round(scaled), -LEVELS, LEVELS)
    tail = jnp.broadcast_to(power, (TAIL, value.shape[1]))
    return codes.astype(jnp.int32).astype(jnp.int16), tail.astype(jnp.int32).astype(jnp.int16)


def put_coded(ref, value):
    codes, tail = coded(value)
    rows = value.shape[0]
    ref[0:rows, :] = codes
    ref[rows : rows + TAIL, :] = tail


def take_coded(ref):
    rows = ref.shape[0] - TAIL
    power = ref[rows : rows + TAIL, :].astype(jnp.int32).astype(jnp.float32)[0:1, :]
    codes = ref[0:rows, :].astype(jnp.int32).astype(jnp.float32)
    return codes * (1.0 / LEVELS) * jnp.exp2(power * (1.0 / 256.0))


def product(rows_ref, columns_ref):
    return jnp.dot(rows_ref[...], columns_ref[...], preferred_element_type=jnp.float32)


def far_kernel(ids, x, wa, wb, wc, qa, qb, qc, qd):
    half = x.shape[0] // 2
    put_coded(qa, product(x, wa))
    put_coded(qb, product(x, wb))
    far = product(x, wc)
    put_coded(qc, far[:half])
    put_coded(qd, far[half:])


def near_kernel(ids, x, wa, wb, wc, wd, we, qa, qb, pc, pd, pe):
    put_coded(qa, product(x, wa))
    put_coded(qb, product(x, wb))
    pc[...] = product(x, wc)
    pd[...] = product(x, wd)
    pe[...] = product(x, we)


def products(kernel, x, w, ids, count, width, outs):
    rows, depth = x.shape
    whole = lambda g, ids: (0, 0)
    columns = [
        pl.BlockSpec((depth, width), functools.partial(lambda k, g, ids: (0, ids[k]), k))
        for k in range(count)
    ]
    return pl.pallas_call(
        kernel,
        out_shape=outs,
        grid_spec=pltpu.PrefetchScalarGridSpec(
            num_scalar_prefetch=1,
            grid=(1,),
            in_specs=[pl.BlockSpec((rows, depth), whole)] + columns,
            out_specs=[pl.BlockSpec(o.shape, whole) for o in outs],
        ),
        compiler_params=pltpu.CompilerParams(vmem_limit_bytes=40 * 2**20),
        cost_estimate=pl.CostEstimate(
            flops=2 * rows * depth * width * count,
            bytes_accessed=2 * depth * (rows + width * count),
            transcendentals=0,
        ),
    )(ids, x, *([w] * count))


def local_call(kernel, outs, *args, flops=0):
    return pl.pallas_call(
        kernel,
        out_shape=outs,
        compiler_params=pltpu.CompilerParams(vmem_limit_bytes=40 * 2**20),
        cost_estimate=pl.CostEstimate(flops=flops, bytes_accessed=2**20, transcendentals=0),
    )(*args)


def merge_kernel(own_a, next_a, far_a, own_b, next_b, far_b, qa, qb):
    half = own_a.shape[0] // 2
    total = own_a[...] + take_coded(next_a)
    total = jnp.concatenate([total[:half] + take_coded(far_a), total[half:]], axis=0)
    put_coded(qa, total)
    total = own_b[...] + take_coded(next_b)
    total = jnp.concatenate([total[:half], total[half:] + take_coded(far_b)], axis=0)
    put_coded(qb, total)


def selector_kernel(target_ref, out):
    places, rows = out.shape
    replicas = 32
    each = places // replicas
    target = target_ref[...]
    onehot = (lax.broadcasted_iota(jnp.int32, (replicas, rows), 0) == target).astype(jnp.float32)
    before = (
        lax.broadcasted_iota(jnp.int32, (rows, rows), 0)
        < lax.broadcasted_iota(jnp.int32, (rows, rows), 1)
    ).astype(jnp.bfloat16)
    ranks = jnp.dot(onehot.astype(jnp.bfloat16), before, preferred_element_type=jnp.float32)
    rank = jnp.sum(ranks * onehot, axis=0, keepdims=True).astype(jnp.int32)
    position = target * each + rank
    out[...] = (lax.broadcasted_iota(jnp.int32, (places, rows), 0) == position).astype(jnp.float32).astype(jnp.bfloat16)


def final_kernel(own, ra, rb, rc, rd, selector, out):
    keys = own[...] + take_coded(ra) + take_coded(rb) + take_coded(rc) + take_coded(rd)
    out[...] = jnp.dot(
        selector[...], keys.astype(jnp.bfloat16), preferred_element_type=jnp.float32
    ).astype(jnp.bfloat16)


def along_tp(value, step):
    size = lax.axis_size("tp")
    return lax.ppermute(value, "tp", [(i, (i + step) % size) for i in range(size)])


def local(master, moment, second, gradient, step_count, old_weights, branch_rows, assignment):
    steps_f = step_count[0].astype(jnp.float32)
    first_fix = 1.0 - jnp.power(jnp.float32(0.9), steps_f)
    second_fix = 1.0 - jnp.power(jnp.float32(0.95), steps_f)
    new_moment = 0.9 * moment + 0.1 * gradient
    new_second = 0.95 * second + 0.05 * gradient * gradient
    update = new_moment / first_fix / (jnp.sqrt(new_second / second_fix) + 1e-08)
    new_master = master - learn_rate * (update + decay_rate * master)

    rows, width = new_master.shape
    chips = lax.axis_size(CHIPS)
    fresh = new_master.astype(jnp.bfloat16)
    spread = jnp.broadcast_to(fresh[None], (chips, rows, width))
    mine = lax.all_to_all(spread, CHIPS, split_axis=0, concat_axis=0, tiled=True)
    other = lax.ppermute(mine, "core", [(0, 1), (1, 0)])
    core = lax.axis_index("core")
    pair = jnp.stack([jnp.where(core == 0, mine, other), jnp.where(core == 0, other, mine)])
    pair = pair.reshape(2, lax.axis_size("xlo"), -1, width)
    rollout_weights = jnp.swapaxes(pair, 0, 1).reshape(2 * chips * rows, width)

    size = lax.axis_size("tp")
    me = lax.axis_index("tp")
    count = branch_rows.shape[0]
    part = old_weights.shape[1] // size
    code = lambda n: jax.ShapeDtypeStruct((n + TAIL, part), jnp.int16)
    full = jax.ShapeDtypeStruct((count, part), jnp.float32)
    ids = lax.rem(me + jnp.array([3, 5, 4], jnp.int32), size)
    q3, q5, q4a, q4b = products(
        far_kernel, branch_rows, old_weights, ids, 3, part,
        [code(count), code(count), code(count // 2), code(count // 2)],
    )
    r3, r5 = along_tp(q3, 1), along_tp(q5, -1)
    r4a, r4b = along_tp(q4a, 2), along_tp(q4b, -2)
    ids = lax.rem(me + jnp.array([1, 7, 2, 6, 0], jnp.int32), size)
    q1, q7, p2, p6, p0 = products(
        near_kernel, branch_rows, old_weights, ids, 5, part,
        [code(count), code(count), full, full, full],
    )
    r1, r7 = along_tp(q1, 1), along_tp(q7, -1)
    q2, q6 = local_call(merge_kernel, [code(count), code(count)], p2, r3, r4a, p6, r5, r4b)
    r2, r6 = along_tp(q2, 2), along_tp(q6, -2)
    replicas = lax.axis_size(PLANE)
    slots_each = 2 * count // replicas
    places = replicas * slots_each
    selector = local_call(
        selector_kernel, jax.ShapeDtypeStruct((places, count), jnp.bfloat16), assignment.reshape(1, count)
    )
    placed = local_call(
        final_kernel, jax.ShapeDtypeStruct((places, part), jnp.bfloat16), p0, r1, r7, r2, r6, selector
    )
    placed = placed.reshape(replicas, slots_each, part)
    arrived = lax.all_to_all(placed, PLANE, split_axis=0, concat_axis=0, tiled=True)
    branch_keys = arrived.reshape(1, replicas, slots_each, part)
    return (new_master, new_moment, new_second, rollout_weights, branch_keys)


def solution(mesh):
    size = mesh.shape
    mesh = Mesh(
        mesh.devices.reshape(2, 2, 4, 2, size["tp"]), ("xlo", "core", "y", "xhi", "tp")
    )
    shard = P(("tp",) + PLANE, None)
    return jax.shard_map(
        local,
        mesh=mesh,
        in_specs=(shard, shard, shard, shard, P(), P("tp", None), P(PLANE, "tp"), P(PLANE, None)),
        out_specs=(shard, shard, shard, P("tp", None), P(PLANE, None, None, "tp")),
        check_vma=False,
    )
```

time: 126 us -> 92.2 us (0.73)
  waiting for transfers between devices: 70.8 us -> 15.6 us
  starting transfers between devices: 0.08 us -> 22.3 us
  between operations: 16.3 us -> 1.48 us
  blocking collectives: 21.2 us -> 33.7 us
  Pallas kernels: 0 us -> 8.69 us
  matrix products: 7.26 us -> 0 us
  other arithmetic: 2.36 us -> 7.06 us
  local copies, waits for them, and re-layouts: 7.43 us -> 3.16 us
    reduce_scatter x1 -> x0, waiting for transfers between devices: 37.9 us -> none  [local(): lax.psum_scatter(partial_value, 'tp', scatter_dimension=1, tiled=True)]
    all_gather x1 -> x0, waiting for transfers between devices: 32.9 us -> none  [local(): lax.all_gather(new_master.astype(jnp.bfloat16), ('role', 'rep'), axis=0,...]
    ppermute x0 -> x9, starting transfers between devices: none -> 16.1 us  [the longest x8 13.3 us: along_tp(): lax.ppermute(value, 'tp', [(i, (i + step) % size) for i in range(size)])]
    all_to_all x1, blocking collectives: 21.2 us -> 33.7 us  [local(): lax.all_to_all(spread, CHIPS, split_axis=0, concat_axis=0, tiled=True)]
    all_to_all x0 -> x1, waiting for transfers between devices: none -> 9.05 us  [local(): lax.all_to_all(placed, PLANE, split_axis=0, concat_axis=0, tiled=True)]
    pallas_call x0 -> x5, Pallas kernels: none -> 8.69 us  [the longest x2 6.48 us: products(): pl.pallas_call(kernel, out_shape=outs, grid_spec=pltpu.PrefetchScalarGrid...]
    dot_general x2 -> x0, matrix products: 7.26 us -> none  [the longest x1 5.84 us: local(): jnp.dot(branch_rows, old_weights, preferred_element_type=jnp.float32)]
    ppermute x0 -> x9, waiting for transfers between devices: none -> 6.51 us  [the longest x8 6.51 us: along_tp(): lax.ppermute(value, 'tp', [(i, (i + step) % size) for i in range(size)])]
  transfers between devices with their start and end apart: 2 -> 10, of which waited for: 2 -> 5; matrix products, arithmetic and copies ran while one was open for 3% -> 0% of each run, Pallas kernels for 0% -> 9%
where the time goes in v2:
time: 92.2 us; the launch traced here: 91.9 us
  blocking collectives  33.7 us (37%)
  starting transfers between devices  22.3 us (24%)
  waiting for transfers between devices  15.6 us (17%)
  Pallas kernels  8.69 us (9%)
  other arithmetic  7.06 us (8%)
  local copies, waits for them, and re-layouts  3.16 us (3%)
  between operations  1.48 us (2%)
    all_to_all x1, blocking collectives, local(): lax.all_to_all(spread, CHIPS, split_axis=0, concat_axis=0, tiled=True)  33.7 us
    ppermute x8, starting transfers between devices, along_tp(): lax.ppermute(value, 'tp', [(i, (i + step) % size) for i in range(size)])  13.3 us
    all_to_all x1, waiting for transfers between devices, local(): lax.all_to_all(placed, PLANE, split_axis=0, concat_axis=0, tiled=True)  9.05 us
    ppermute x8, waiting for transfers between devices, along_tp(): lax.ppermute(value, 'tp', [(i, (i + step) % size) for i in range(size)])  6.51 us
    pallas_call x2, Pallas kernels, products(): pl.pallas_call(kernel, out_shape=outs, grid_spec=pltpu.PrefetchScalarGrid...  6.48 us
    all_to_all x1, starting transfers between devices, local(): lax.all_to_all(placed, PLANE, split_axis=0, concat_axis=0, tiled=True)  6.17 us
    unnamed x13, local copies, waits for them, and re-layouts  2.91 us
    ppermute x1, starting transfers between devices, local(): other = lax.ppermute(mine, 'core', [(0, 1), (1, 0)])  2.84 us
  transfers between devices with their start and end apart: 10, of which 5 were waited for; matrix products, arithmetic and copies ran while one was open for 0% of the time, Pallas kernels for 9%

profile of v2, /device:TPU:1, one launch (start us, length us, event | category | flops | bytes accessed | tf_op | source)
XLA Modules:
  0.0 91.9 jit_solution(13243584625083101839)
XLA Ops:
  1.4 2.2 %fusion.3 = (bf16[64,1024]{1,0:T(8,128)(2,1)S(1)}, f32[64,1024]{1,0:T(8,128)}, f32[64,1024]{1,0:T(8,128)}, f32[64,1024]{1,0:T(8,128)}) fusion(f32[64,1024]{1,0:T(8,128)} %param.10, f32[]{:T(128)} %bitcast.1, f32[]{:T(128)} %bitcast, f32[64,1024]{1,0:T(8,128)} %param.13, f32[64,1024]{1,0:T(8,128)} %param.12, f32[64,1024]{1,0:T(8,128)} %param.11), kind=kLoop, calls=%fused_computation.13 | loop fusion | flops 1048576 | bytes 1966088 | tf_op jit(solution)/shard_map/convert_element_type | solution.py:148
  3.5 0.2 broadcast_in_dim.2
  3.8 0.0 copy-start.5
  3.8 0.0 copy-start.2
  3.8 33.7 %all_to_all.10 = bf16[16,64,1024]{2,1,0:T(8,128)(2,1)} all-to-all(bf16[16,64,1024]{2,1,0:T(8,128)(2,1)S(1)} %broadcast_in_dim.2), channel_id=1, replica_groups=mesh['xlo'=2,'core'=2,'y'=4,'xhi'=2,'tp'=8] {'xlo','y','xhi'}, dimensions={0} | all-to-all | bytes 4194304 | tf_op jit(solution)/shard_map/all_to_all | solution.py:150
  37.5 2.8 %collective-permute-start = (bf16[16,64,1024]{2,1,0:T(8,128)(2,1)}, bf16[16,64,1024]{2,1,0:T(8,128)(2,1)}, u32[]{:S(2)}, u32[]{:S(2)}) collective-permute-start(bf16[16,64,1024]{2,1,0:T(8,128)(2,1)} %all_to_all.10), channel_id=1, source_target_pairs={{0,64},{64,0},{1,65},{65,1},{2,66},{66,2},{3,67},{67,3},{4,68},{68... | collective-permute-start | bytes 6291464 | tf_op jit(solution)/shard_map/ppermute | solution.py:151
  40.3 0.0 copy-done.5
  40.3 0.0 copy-done.2
  40.3 0.0 copy-start
  40.4 2.2 %copy-done = bf16[2048,1024]{1,0:T(8,128)(2,1)S(1)} copy-done((bf16[2048,1024]{1,0:T(8,128)(2,1)S(1)}, bf16[2048,1024]{1,0:T(8,128)(2,1)}, u32[]{:S(2)}) %copy-start) | copy-done | bytes 4194328
  42.5 0.0 copy-start.4
  42.5 0.0 copy-start.1
  42.5 2.7 %shard_map.138 = (s16[528,128]{1,0:T(8,128)(2,1)S(1)}, s16[528,128]{1,0:T(8,128)(2,1)S(1)}, s16[272,128]{1,0:T(8,128)(2,1)S(1)}, s16[272,128]{1,0:T(8,128)(2,1)S(1)}) custom-call(s32[3]{0:T(128)S(1)} %compare_select_fusion.ids, bf16[512,2048]{1,0:T(8,128)(2,1)S(1)} %copy-done.2, bf16[2048,1024]{1,0:T(8,128)(2,1)S(1)} %copy-done, ...), custom_call_target="tpu_custom_call" | custom-call | flops 805306368 | bytes 3670016 | tf_op jit(solution)/shard_map/pallas_call | solution.py:72
  45.2 1.7 %collective-permute-start.3 = (s16[528,128]{1,0:T(8,128)(2,1)S(1)}, s16[528,128]{1,0:T(8,128)(2,1)S(1)}, u32[]{:S(2)}, u32[]{:S(2)}) collective-permute-start(s16[528,128]{1,0:T(8,128)(2,1)S(1)} %get-tuple-element.20), channel_id=1, source_target_pairs={{0,1},{1,2},{2,3},{3,4},{4,5},{5,6},{6,7},{7,0},{8,9},{9,10},{10,1... | collective-permute-start | bytes 405512 | tf_op jit(solution)/shard_map/ppermute | solution.py:134
  46.9 3.0 %collective-permute-start.4 = (s16[272,128]{1,0:T(8,128)(2,1)S(1)}, s16[272,128]{1,0:T(8,128)(2,1)S(1)}, u32[]{:S(2)}, u32[]{:S(2)}) collective-permute-start(s16[272,128]{1,0:T(8,128)(2,1)S(1)} %get-tuple-element.21), channel_id=1, source_target_pairs={{0,2},{1,3},{2,4},{3,5},{4,6},{5,7},{6,0},{7,1},{8,10},{9,11},{10,... | collective-permute-start | bytes 208904 | tf_op jit(solution)/shard_map/ppermute | solution.py:134
  49.9 1.1 %collective-permute-start.5 = (s16[528,128]{1,0:T(8,128)(2,1)S(1)}, s16[528,128]{1,0:T(8,128)(2,1)S(1)}, u32[]{:S(2)}, u32[]{:S(2)}) collective-permute-start(s16[528,128]{1,0:T(8,128)(2,1)S(1)} %get-tuple-element.23), channel_id=1, source_target_pairs={{0,7},{1,0},{2,1},{3,2},{4,3},{5,4},{6,5},{7,6},{8,15},{9,8},{10,9... | collective-permute-start | bytes 405512 | tf_op jit(solution)/shard_map/ppermute | solution.py:134
  51.1 2.3 %collective-permute-start.6 = (s16[272,128]{1,0:T(8,128)(2,1)S(1)}, s16[272,128]{1,0:T(8,128)(2,1)S(1)}, u32[]{:S(2)}, u32[]{:S(2)}) collective-permute-start(s16[272,128]{1,0:T(8,128)(2,1)S(1)} %get-tuple-element.24), channel_id=1, source_target_pairs={{0,6},{1,7},{2,0},{3,1},{4,2},{5,3},{6,4},{7,5},{8,14},{9,15},{10,... | collective-permute-start | bytes 208904 | tf_op jit(solution)/shard_map/ppermute | solution.py:134
  53.3 0.0 copy-done.4
  53.3 0.0 copy-done.1
  53.3 0.0 copy-start.3
  53.4 3.8 %shard_map.137 = (s16[528,128]{1,0:T(8,128)(2,1)S(1)}, s16[528,128]{1,0:T(8,128)(2,1)S(1)}, f32[512,128]{1,0:T(8,128)S(1)}, f32[512,128]{1,0:T(8,128)S(1)}, f32[512,128]{1,0:T(8,128)S(1)}) custom-call(s32[5]{0:T(128)S(1)} %compare_select_fusion.2.ids, bf16[512,2048]{1,0:T(8,128)(2,1)S(1)} %copy-done.2, bf16[2048,1024]{1,0:T(8,128)(2,1)S(1)} %copy-done.1, ...), custom_call_target="tpu_custom_call" | custom-call | flops 1342177280 | bytes 4718592 | tf_op jit(solution)/shard_map/pallas_call | solution.py:72
  57.2 0.7 collective-permute-done.4.far_a
  57.8 0.0 collective-permute-start.1
  57.8 1.1 %collective-permute-done.6.far_b = s16[272,128]{1,0:T(8,128)(2,1)S(1)} collective-permute-done((s16[272,128]{1,0:T(8,128)(2,1)S(1)}, s16[272,128]{1,0:T(8,128)(2,1)S(1)}, u32[]{:S(2)}, u32[]{:S(2)}) %collective-permute-start.6) | collective-permute-done | bytes 69664 | tf_op jit(solution)/shard_map/ppermute | solution.py:134
  59.0 1.5 %collective-permute-start.2 = (s16[528,128]{1,0:T(8,128)(2,1)S(1)}, s16[528,128]{1,0:T(8,128)(2,1)S(1)}, u32[]{:S(2)}, u32[]{:S(2)}) collective-permute-start(s16[528,128]{1,0:T(8,128)(2,1)S(1)} %get-tuple-element.18), channel_id=1, source_target_pairs={{0,7},{1,0},{2,1},{3,2},{4,3},{5,4},{6,5},{7,6},{8,15},{9,8},{10,9... | collective-permute-start | bytes 405512 | tf_op jit(solution)/shard_map/ppermute | solution.py:134
  60.5 0.0 collective-permute-done.3.next_a
  60.5 0.0 collective-permute-done.5.next_b
  60.5 0.3 shard_map.139
  60.8 1.5 %collective-permute-start.7 = (s16[528,128]{1,0:T(8,128)(2,1)S(1)}, s16[528,128]{1,0:T(8,128)(2,1)S(1)}, u32[]{:S(2)}, u32[]{:S(2)}) collective-permute-start(s16[528,128]{1,0:T(8,128)(2,1)S(1)} %get-tuple-element.25), channel_id=1, source_target_pairs={{0,2},{1,3},{2,4},{3,5},{4,6},{5,7},{6,0},{7,1},{8,10},{9,11},{10,... | collective-permute-start | bytes 405512 | tf_op jit(solution)/shard_map/ppermute | solution.py:134
  62.3 2.1 %collective-permute-start.8 = (s16[528,128]{1,0:T(8,128)(2,1)S(1)}, s16[528,128]{1,0:T(8,128)(2,1)S(1)}, u32[]{:S(2)}, u32[]{:S(2)}) collective-permute-start(s16[528,128]{1,0:T(8,128)(2,1)S(1)} %get-tuple-element.26), channel_id=1, source_target_pairs={{0,6},{1,7},{2,0},{3,1},{4,2},{5,3},{6,4},{7,5},{8,14},{9,15},{10,... | collective-permute-start | bytes 405512 | tf_op jit(solution)/shard_map/ppermute | solution.py:134
  64.5 0.0 copy-done.3
  64.5 0.6 shard_map.140.selector
  65.1 0.0 collective-permute-done.1.ra
  65.1 0.0 collective-permute-done.2.rb
  65.1 2.2 %collective-permute-done.7.rc = s16[528,128]{1,0:T(8,128)(2,1)S(1)} collective-permute-done((s16[528,128]{1,0:T(8,128)(2,1)S(1)}, s16[528,128]{1,0:T(8,128)(2,1)S(1)}, u32[]{:S(2)}, u32[]{:S(2)}) %collective-permute-start.7) | collective-permute-done | bytes 135200 | tf_op jit(solution)/shard_map/ppermute | solution.py:134
  67.3 2.5 %collective-permute-done.8.rd = s16[528,128]{1,0:T(8,128)(2,1)S(1)} collective-permute-done((s16[528,128]{1,0:T(8,128)(2,1)S(1)}, s16[528,128]{1,0:T(8,128)(2,1)S(1)}, u32[]{:S(2)}, u32[]{:S(2)}) %collective-permute-start.8) | collective-permute-done | bytes 135200 | tf_op jit(solution)/shard_map/ppermute | solution.py:134
  69.8 1.3 %shard_map.141 = bf16[1024,128]{1,0:T(8,128)(2,1)} custom-call(f32[512,128]{1,0:T(8,128)S(1)} %get-tuple-element.16.own, s16[528,128]{1,0:T(8,128)(2,1)S(1)} %collective-permute-done.1.ra, s16[528,128]{1,0:T(8,128)(2,1)S(1)} %collective-permute-done.2.rb, s16[528,128]{1,0:T(8,128)(2,1)S(1)} %collective-permute-done.7.rc, ...), custom_call_target="tpu_custom_call" | custom-call | bytes 1048576 | tf_op jit(solution)/shard_map/pallas_call | solution.py:91
  71.1 6.2 %all-to-all-start.1 = ((bf16[32,32,128]{2,1,0:T(8,128)(2,1)}), bf16[32,32,128]{2,1,0:T(8,128)(2,1)S(1)}, u32[]{:S(2)}, u32[]{:S(2)}) async-start(bf16[32,32,128]{2,1,0:T(8,128)(2,1)} %bitcast.7), calls=%async_computation.1 | async-start | bytes 524288 | tf_op jit(solution)/shard_map/all_to_all | solution.py:188
  77.3 9.1 %all-to-all-done.1 = bf16[32,32,128]{2,1,0:T(8,128)(2,1)S(1)} async-done(((bf16[32,32,128]{2,1,0:T(8,128)(2,1)}), bf16[32,32,128]{2,1,0:T(8,128)(2,1)S(1)}, u32[]{:S(2)}, u32[]{:S(2)}) %all-to-all-start.1) | async-done | bytes 262176 | tf_op jit(solution)/shard_map/all_to_all | solution.py:188
  86.3 0.0 collective-permute-done
  86.3 2.5 %broadcast_select_fusion.1 = (bf16[16,64,1024]{2,1,0:T(8,128)(2,1)S(1)}, bf16[16,64,1024]{2,1,0:T(8,128)(2,1)S(1)}) fusion(bf16[16,64,1024]{2,1,0:T(8,128)(2,1)} %all_to_all.10, bf16[16,64,1024]{2,1,0:T(8,128)(2,1)} %collective-permute-done, pred[]{:T(512)S(6)} %eq.4), kind=kLoop, calls=%fused_computation.2 | loop fusion | flops 2097152 | bytes 8388609 | tf_op jit(solution)/shard_map/jit(_where)/select_n | solution.py:153
  88.8 2.4 %pad_maximum_fusion = bf16[2,2,512,1024]{3,2,0,1:T(8,128)(2,1)} fusion(bf16[1,2,512,1024]{3,2,0,1:T(8,128)(2,1)S(1)} %bitcast.12, bf16[1,2,512,1024]{3,2,0,1:T(8,128)(2,1)S(1)} %bitcast.11), kind=kLoop, calls=%fused_computation | loop fusion | flops 2097152 | bytes 8388608 | tf_op jit(solution)/shard_map/stack | solution.py:153
  91.2 0.7 copy.17
  (2 shorter events, 0.0 us)
Async XLA Ops:
  3.8 36.5 %copy-start.5 = (s32[3]{0:T(128)S(1)}, s32[3]{0:T(128)}, u32[]{:S(2)}) copy-start(s32[3]{0:T(128)} %constant.43.clone) | copy-start | bytes 40
  3.8 36.5 %copy-start.2 = (bf16[512,2048]{1,0:T(8,128)(2,1)S(1)}, bf16[512,2048]{1,0:T(8,128)(2,1)}, u32[]{:S(2)}) copy-start(bf16[512,2048]{1,0:T(8,128)(2,1)} %x.3) | copy-start | bytes 6291460
  37.5 48.9 %collective-permute-start = (bf16[16,64,1024]{2,1,0:T(8,128)(2,1)}, bf16[16,64,1024]{2,1,0:T(8,128)(2,1)}, u32[]{:S(2)}, u32[]{:S(2)}) collective-permute-start(bf16[16,64,1024]{2,1,0:T(8,128)(2,1)} %all_to_all.10), channel_id=1, source_target_pairs={{0,64},{64,0},{1,65},{65,1},{2,66},{66,2},{3,67},{67,3},{4,68},{68... | collective-permute-start | bytes 6291464 | tf_op jit(solution)/shard_map/ppermute | solution.py:151
  40.3 2.2 %copy-start = (bf16[2048,1024]{1,0:T(8,128)(2,1)S(1)}, bf16[2048,1024]{1,0:T(8,128)(2,1)}, u32[]{:S(2)}) copy-start(bf16[2048,1024]{1,0:T(8,128)(2,1)} %wc.3) | copy-start | bytes 12582916
  42.5 10.8 %copy-start.4 = (s32[5]{0:T(128)S(1)}, s32[5]{0:T(128)}, u32[]{:S(2)}) copy-start(s32[5]{0:T(128)} %constant.44.clone) | copy-start | bytes 64
  42.5 10.8 %copy-start.1 = (bf16[2048,1024]{1,0:T(8,128)(2,1)S(1)}, bf16[2048,1024]{1,0:T(8,128)(2,1)}, u32[]{:S(2)}) copy-start(bf16[2048,1024]{1,0:T(8,128)(2,1)} %wc.3) | copy-start | bytes 12582916
  45.2 15.3 %collective-permute-start.3 = (s16[528,128]{1,0:T(8,128)(2,1)S(1)}, s16[528,128]{1,0:T(8,128)(2,1)S(1)}, u32[]{:S(2)}, u32[]{:S(2)}) collective-permute-start(s16[528,128]{1,0:T(8,128)(2,1)S(1)} %get-tuple-element.20), channel_id=1, source_target_pairs={{0,1},{1,2},{2,3},{3,4},{4,5},{5,6},{6,7},{7,0},{8,9},{9,10},{10,1... | collective-permute-start | bytes 405512 | tf_op jit(solution)/shard_map/ppermute | solution.py:134
  46.9 10.9 %collective-permute-start.4 = (s16[272,128]{1,0:T(8,128)(2,1)S(1)}, s16[272,128]{1,0:T(8,128)(2,1)S(1)}, u32[]{:S(2)}, u32[]{:S(2)}) collective-permute-start(s16[272,128]{1,0:T(8,128)(2,1)S(1)} %get-tuple-element.21), channel_id=1, source_target_pairs={{0,2},{1,3},{2,4},{3,5},{4,6},{5,7},{6,0},{7,1},{8,10},{9,11},{10,... | collective-permute-start | bytes 208904 | tf_op jit(solution)/shard_map/ppermute | solution.py:134
  49.9 10.6 %collective-permute-start.5 = (s16[528,128]{1,0:T(8,128)(2,1)S(1)}, s16[528,128]{1,0:T(8,128)(2,1)S(1)}, u32[]{:S(2)}, u32[]{:S(2)}) collective-permute-start(s16[528,128]{1,0:T(8,128)(2,1)S(1)} %get-tuple-element.23), channel_id=1, source_target_pairs={{0,7},{1,0},{2,1},{3,2},{4,3},{5,4},{6,5},{7,6},{8,15},{9,8},{10,9... | collective-permute-start | bytes 405512 | tf_op jit(solution)/shard_map/ppermute | solution.py:134
  51.1 7.9 %collective-permute-start.6 = (s16[272,128]{1,0:T(8,128)(2,1)S(1)}, s16[272,128]{1,0:T(8,128)(2,1)S(1)}, u32[]{:S(2)}, u32[]{:S(2)}) collective-permute-start(s16[272,128]{1,0:T(8,128)(2,1)S(1)} %get-tuple-element.24), channel_id=1, source_target_pairs={{0,6},{1,7},{2,0},{3,1},{4,2},{5,3},{6,4},{7,5},{8,14},{9,15},{10,... | collective-permute-start | bytes 208904 | tf_op jit(solution)/shard_map/ppermute | solution.py:134
  53.3 11.1 %copy-start.3 = (s32[512,1]{0,1:T(1,128)S(1)}, s32[512,1]{0,1:T(1,128)}, u32[]{:S(2)}) copy-start(s32[512,1]{0,1:T(1,128)} %param.17) | copy-start | bytes 6148
  57.8 7.3 %collective-permute-start.1 = (s16[528,128]{1,0:T(8,128)(2,1)S(1)}, s16[528,128]{1,0:T(8,128)(2,1)S(1)}, u32[]{:S(2)}, u32[]{:S(2)}) collective-permute-start(s16[528,128]{1,0:T(8,128)(2,1)S(1)} %get-tuple-element.17), channel_id=1, source_target_pairs={{0,1},{1,2},{2,3},{3,4},{4,5},{5,6},{6,7},{7,0},{8,9},{9,10},{10,1... | collective-permute-start | bytes 405512 | tf_op jit(solution)/shard_map/ppermute | solution.py:134
  59.0 6.1 %collective-permute-start.2 = (s16[528,128]{1,0:T(8,128)(2,1)S(1)}, s16[528,128]{1,0:T(8,128)(2,1)S(1)}, u32[]{:S(2)}, u32[]{:S(2)}) collective-permute-start(s16[528,128]{1,0:T(8,128)(2,1)S(1)} %get-tuple-element.18), channel_id=1, source_target_pairs={{0,7},{1,0},{2,1},{3,2},{4,3},{5,4},{6,5},{7,6},{8,15},{9,8},{10,9... | collective-permute-start | bytes 405512 | tf_op jit(solution)/shard_map/ppermute | solution.py:134
  60.8 6.5 %collective-permute-start.7 = (s16[528,128]{1,0:T(8,128)(2,1)S(1)}, s16[528,128]{1,0:T(8,128)(2,1)S(1)}, u32[]{:S(2)}, u32[]{:S(2)}) collective-permute-start(s16[528,128]{1,0:T(8,128)(2,1)S(1)} %get-tuple-element.25), channel_id=1, source_target_pairs={{0,2},{1,3},{2,4},{3,5},{4,6},{5,7},{6,0},{7,1},{8,10},{9,11},{10,... | collective-permute-start | bytes 405512 | tf_op jit(solution)/shard_map/ppermute | solution.py:134
  62.3 7.5 %collective-permute-start.8 = (s16[528,128]{1,0:T(8,128)(2,1)S(1)}, s16[528,128]{1,0:T(8,128)(2,1)S(1)}, u32[]{:S(2)}, u32[]{:S(2)}) collective-permute-start(s16[528,128]{1,0:T(8,128)(2,1)S(1)} %get-tuple-element.26), channel_id=1, source_target_pairs={{0,6},{1,7},{2,0},{3,1},{4,2},{5,3},{6,4},{7,5},{8,14},{9,15},{10,... | collective-permute-start | bytes 405512 | tf_op jit(solution)/shard_map/ppermute | solution.py:134
  71.1 15.2 %all-to-all-start.1 = ((bf16[32,32,128]{2,1,0:T(8,128)(2,1)}), bf16[32,32,128]{2,1,0:T(8,128)(2,1)S(1)}, u32[]{:S(2)}, u32[]{:S(2)}) async-start(bf16[32,32,128]{2,1,0:T(8,128)(2,1)} %bitcast.7), calls=%async_computation.1 | async-start | bytes 524288 | tf_op jit(solution)/shard_map/all_to_all | solution.py:188

commit v3 on v2

--- a/solution.py
+++ b/solution.py
@@ -129,6 +129,33 @@
     ).astype(jnp.bfloat16)
 
 
+def half_kernel(place, half, *refs):
+    out, sems = refs[-2:]
+    copies = [
+        pltpu.make_async_copy(half.at[i], out.at[i, place[0]], sems.at[i])
+        for i in range(half.shape[0])
+    ]
+    for copy in copies:
+        copy.start()
+    for copy in copies:
+        copy.wait()
+
+
+def set_half(place, half, pair=None):
+    anywhere = pl.BlockSpec(memory_space=pl.ANY)
+    lanes, rows, width = half.shape
+    args = (place, half) + (() if pair is None else (pair,))
+    return pl.pallas_call(
+        half_kernel,
+        out_shape=jax.ShapeDtypeStruct((lanes, 2, rows, width), half.dtype),
+        in_specs=[pl.BlockSpec(memory_space=pltpu.SMEM)] + [anywhere] * (len(args) - 1),
+        out_specs=anywhere,
+        scratch_shapes=[pltpu.SemaphoreType.DMA((lanes,))],
+        input_output_aliases={} if pair is None else {2: 0},
+        cost_estimate=pl.CostEstimate(flops=0, bytes_accessed=2 * half.size * 2, transcendentals=0),
+    )(*args)
+
+
 def along_tp(value, step):
     size = lax.axis_size("tp")
     return lax.ppermute(value, "tp", [(i, (i + step) % size) for i in range(size)])
@@ -148,12 +175,6 @@
     fresh = new_master.astype(jnp.bfloat16)
     spread = jnp.broadcast_to(fresh[None], (chips, rows, width))
     mine = lax.all_to_all(spread, CHIPS, split_axis=0, concat_axis=0, tiled=True)
-    other = lax.ppermute(mine, "core", [(0, 1), (1, 0)])
-    core = lax.axis_index("core")
-    pair = jnp.stack([jnp.where(core == 0, mine, other), jnp.where(core == 0, other, mine)])
-    pair = pair.reshape(2, lax.axis_size("xlo"), -1, width)
-    rollout_weights = jnp.swapaxes(pair, 0, 1).reshape(2 * chips * rows, width)
-
     size = lax.axis_size("tp")
     me = lax.axis_index("tp")
     count = branch_rows.shape[0]
@@ -184,9 +205,18 @@
     placed = local_call(
         final_kernel, jax.ShapeDtypeStruct((places, part), jnp.bfloat16), p0, r1, r7, r2, r6, selector
     )
+    placed, mine = lax.optimization_barrier((placed, mine))
     placed = placed.reshape(replicas, slots_each, part)
     arrived = lax.all_to_all(placed, PLANE, split_axis=0, concat_axis=0, tiled=True)
     branch_keys = arrived.reshape(1, replicas, slots_each, part)
+    other = lax.ppermute(mine, "core", [(0, 1), (1, 0)])
+    core = jnp.reshape(lax.axis_index("core"), (1,)).astype(jnp.int32)
+    lanes = lax.axis_size("xlo")
+    mine = mine.reshape(lanes, -1, width)
+    other = other.reshape(lanes, -1, width)
+    pair = set_half(core, mine)
+    pair = set_half(1 - core, other, pair)
+    rollout_weights = pair.reshape(2 * chips * rows, width)
     return (new_master, new_moment, new_second, rollout_weights, branch_keys)
 
 

time: 92.2 us -> 186 us (2.02)
  Pallas kernels: 8.69 us -> 138 us
  blocking collectives: 33.7 us -> 0 us
  starting transfers between devices: 22.3 us -> 33.3 us
  waiting for transfers between devices: 15.6 us -> 4.82 us
  other arithmetic: 7.06 us -> 2.19 us
  local copies, waits for them, and re-layouts: 3.16 us -> 5.81 us
    pallas_call x0 -> x2, Pallas kernels: none -> 129 us  [set_half(): pl.pallas_call(half_kernel, out_shape=jax.ShapeDtypeStruct((lanes, 2, row...]
    all_to_all x1 -> x0, blocking collectives: 33.7 us -> none  [local(): lax.all_to_all(spread, CHIPS, split_axis=0, concat_axis=0, tiled=True)]
    all_to_all x1, waiting for transfers between devices: 9.05 us -> 0.01 us  [local(): lax.all_to_all(placed, PLANE, split_axis=0, concat_axis=0, tiled=True)]
    all_to_all x0 -> x1, starting transfers between devices: none -> 7.77 us  [local(): lax.all_to_all(spread, CHIPS, split_axis=0, concat_axis=0, tiled=True)]
    select_n x1 -> x0, other arithmetic: 2.5 us -> none  [local(): jnp.where(core == 0, mine, other)]
    another operation x1 -> x0, other arithmetic: 2.38 us -> none  [local(): jnp.stack([jnp.where(core == 0, mine, other), jnp.where(core == 0, other,...]
    ppermute x8, waiting for transfers between devices: 6.51 us -> 4.53 us  [along_tp(): lax.ppermute(value, 'tp', [(i, (i + step) % size) for i in range(size)])]
    ppermute x8, starting transfers between devices: 13.3 us -> 15.2 us  [along_tp(): lax.ppermute(value, 'tp', [(i, (i + step) % size) for i in range(size)])]
  transfers between devices with their start and end apart: 10 -> 11, of which waited for: 5 -> 2; matrix products, arithmetic and copies ran while one was open for 0% -> 0% of each run, Pallas kernels for 9% -> 40%
where the time goes in v3:
time: 186 us
  Pallas kernels  138 us (74%)
  starting transfers between devices  33.3 us (18%)
  local copies, waits for them, and re-layouts  5.81 us (3%)
  waiting for transfers between devices  4.82 us (3%)
  other arithmetic  2.19 us (1%)
    pallas_call x2, Pallas kernels, set_half(): pl.pallas_call(half_kernel, out_shape=jax.ShapeDtypeStruct((lanes, 2, row...  129 us
    ppermute x8, starting transfers between devices, along_tp(): lax.ppermute(value, 'tp', [(i, (i + step) % size) for i in range(size)])  15.2 us
    all_to_all x1, starting transfers between devices, local(): lax.all_to_all(spread, CHIPS, split_axis=0, concat_axis=0, tiled=True)  7.77 us
    all_to_all x1, starting transfers between devices, local(): lax.all_to_all(placed, PLANE, split_axis=0, concat_axis=0, tiled=True)  7.33 us
    pallas_call x2, Pallas kernels, products(): pl.pallas_call(kernel, out_shape=outs, grid_spec=pltpu.PrefetchScalarGrid...  6.47 us
    ppermute x8, waiting for transfers between devices, along_tp(): lax.ppermute(value, 'tp', [(i, (i + step) % size) for i in range(size)])  4.53 us
    unnamed x15, local copies, waits for them, and re-layouts  4.23 us
  transfers between devices with their start and end apart: 11, of which 2 were waited for; matrix products, arithmetic and copies ran while one was open for 0% of the time, Pallas kernels for 40%

profile of v3, /device:TPU:1, one launch (start us, length us, event | category | flops | bytes accessed | tf_op | source)
XLA Modules:
  0.0 185.6 jit_solution(11787749172556927025)
XLA Ops:
  1.4 2.2 %fusion.3 = (bf16[64,1024]{1,0:T(8,128)(2,1)S(1)}, f32[64,1024]{1,0:T(8,128)}, f32[64,1024]{1,0:T(8,128)}, f32[64,1024]{1,0:T(8,128)}) fusion(f32[64,1024]{1,0:T(8,128)} %param.10, f32[]{:T(128)} %bitcast.1, f32[]{:T(128)} %bitcast, f32[64,1024]{1,0:T(8,128)} %param.13, f32[64,1024]{1,0:T(8,128)} %param.12, f32[64,1024]{1,0:T(8,128)} %param.11), kind=kLoop, calls=%fused_computation.10 | loop fusion | flops 1048576 | bytes 1966088 | tf_op jit(solution)/shard_map/convert_element_type | solution.py:175
  3.5 1.6 broadcast_in_dim.2
  5.1 0.0 copy-start.6
  5.1 0.0 copy-start.2
  5.1 7.8 %all-to-all-start = ((bf16[16,64,1024]{2,1,0:T(8,128)(2,1)}), bf16[16,64,1024]{2,1,0:T(8,128)(2,1)}, u32[]{:S(2)}, u32[]{:S(2)}) async-start(bf16[16,64,1024]{2,1,0:T(8,128)(2,1)} %broadcast_in_dim.2), calls=%async_computation | async-start | bytes 4194304 | tf_op jit(solution)/shard_map/all_to_all | solution.py:177
  12.9 0.0 copy-done.6
  12.9 0.0 copy-done.2
  12.9 0.0 copy-start
  12.9 2.2 %copy-done = bf16[2048,1024]{1,0:T(8,128)(2,1)S(1)} copy-done((bf16[2048,1024]{1,0:T(8,128)(2,1)S(1)}, bf16[2048,1024]{1,0:T(8,128)(2,1)}, u32[]{:S(2)}) %copy-start) | copy-done | bytes 4194328
  15.1 0.0 copy-start.5
  15.1 0.0 copy-start.1
  15.1 2.7 %shard_map.138 = (s16[528,128]{1,0:T(8,128)(2,1)S(1)}, s16[528,128]{1,0:T(8,128)(2,1)S(1)}, s16[272,128]{1,0:T(8,128)(2,1)S(1)}, s16[272,128]{1,0:T(8,128)(2,1)S(1)}) custom-call(s32[3]{0:T(128)S(1)} %compare_select_fusion.ids, bf16[512,2048]{1,0:T(8,128)(2,1)S(1)} %copy-done.2, bf16[2048,1024]{1,0:T(8,128)(2,1)S(1)} %copy-done, ...), custom_call_target="tpu_custom_call" | custom-call | flops 805306368 | bytes 3670016 | tf_op jit(solution)/shard_map/pallas_call | solution.py:72
  17.8 3.1 %collective-permute-start.3 = (s16[272,128]{1,0:T(8,128)(2,1)S(1)}, s16[272,128]{1,0:T(8,128)(2,1)S(1)}, u32[]{:S(2)}, u32[]{:S(2)}) collective-permute-start(s16[272,128]{1,0:T(8,128)(2,1)S(1)} %get-tuple-element.23), channel_id=1, source_target_pairs={{0,2},{1,3},{2,4},{3,5},{4,6},{5,7},{6,0},{7,1},{8,10},{9,11},{10,... | collective-permute-start | bytes 208904 | tf_op jit(solution)/shard_map/ppermute | solution.py:161
  20.9 3.1 %collective-permute-start.5 = (s16[272,128]{1,0:T(8,128)(2,1)S(1)}, s16[272,128]{1,0:T(8,128)(2,1)S(1)}, u32[]{:S(2)}, u32[]{:S(2)}) collective-permute-start(s16[272,128]{1,0:T(8,128)(2,1)S(1)} %get-tuple-element.26), channel_id=1, source_target_pairs={{0,6},{1,7},{2,0},{3,1},{4,2},{5,3},{6,4},{7,5},{8,14},{9,15},{10,... | collective-permute-start | bytes 208904 | tf_op jit(solution)/shard_map/ppermute | solution.py:161
  24.0 0.8 collective-permute-start.2
  24.8 1.9 %collective-permute-start.4 = (s16[528,128]{1,0:T(8,128)(2,1)S(1)}, s16[528,128]{1,0:T(8,128)(2,1)S(1)}, u32[]{:S(2)}, u32[]{:S(2)}) collective-permute-start(s16[528,128]{1,0:T(8,128)(2,1)S(1)} %get-tuple-element.25), channel_id=1, source_target_pairs={{0,7},{1,0},{2,1},{3,2},{4,3},{5,4},{6,5},{7,6},{8,15},{9,8},{10,9... | collective-permute-start | bytes 405512 | tf_op jit(solution)/shard_map/ppermute | solution.py:161
  26.7 0.0 copy-done.5
  26.7 0.0 copy-done.1
  26.7 0.0 copy-start.3
  26.7 3.8 %shard_map.137 = (s16[528,128]{1,0:T(8,128)(2,1)S(1)}, s16[528,128]{1,0:T(8,128)(2,1)S(1)}, f32[512,128]{1,0:T(8,128)S(1)}, f32[512,128]{1,0:T(8,128)S(1)}, f32[512,128]{1,0:T(8,128)S(1)}) custom-call(s32[5]{0:T(128)S(1)} %compare_select_fusion.2.ids, bf16[512,2048]{1,0:T(8,128)(2,1)S(1)} %copy-done.2, bf16[2048,1024]{1,0:T(8,128)(2,1)S(1)} %copy-done.1, ...), custom_call_target="tpu_custom_call" | custom-call | flops 1342177280 | bytes 4718592 | tf_op jit(solution)/shard_map/pallas_call | solution.py:72
  30.5 0.1 collective-permute-start
  30.6 0.0 collective-permute-done.3.far_a
  30.6 2.7 %collective-permute-start.1 = (s16[528,128]{1,0:T(8,128)(2,1)S(1)}, s16[528,128]{1,0:T(8,128)(2,1)S(1)}, u32[]{:S(2)}, u32[]{:S(2)}) collective-permute-start(s16[528,128]{1,0:T(8,128)(2,1)S(1)} %get-tuple-element.20), channel_id=1, source_target_pairs={{0,7},{1,0},{2,1},{3,2},{4,3},{5,4},{6,5},{7,6},{8,15},{9,8},{10,9... | collective-permute-start | bytes 405512 | tf_op jit(solution)/shard_map/ppermute | solution.py:161
  33.2 0.0 collective-permute-done.5.far_b
  33.3 0.0 collective-permute-done.2.next_a
  33.3 0.0 collective-permute-done.4.next_b
  33.3 0.3 shard_map.139
  33.5 0.1 collective-permute-start.6
  33.7 3.5 %collective-permute-start.7 = (s16[528,128]{1,0:T(8,128)(2,1)S(1)}, s16[528,128]{1,0:T(8,128)(2,1)S(1)}, u32[]{:S(2)}, u32[]{:S(2)}) collective-permute-start(s16[528,128]{1,0:T(8,128)(2,1)S(1)} %get-tuple-element.28), channel_id=1, source_target_pairs={{0,6},{1,7},{2,0},{3,1},{4,2},{5,3},{6,4},{7,5},{8,14},{9,15},{10,... | collective-permute-start | bytes 405512 | tf_op jit(solution)/shard_map/ppermute | solution.py:161
  37.2 0.0 copy-done.3
  37.2 0.6 shard_map.140.selector
  37.9 0.0 collective-permute-done.ra
  37.9 0.0 collective-permute-done.1.rb
  37.9 4.5 %collective-permute-done.6.rc = s16[528,128]{1,0:T(8,128)(2,1)S(1)} collective-permute-done((s16[528,128]{1,0:T(8,128)(2,1)S(1)}, s16[528,128]{1,0:T(8,128)(2,1)S(1)}, u32[]{:S(2)}, u32[]{:S(2)}) %collective-permute-start.6) | collective-permute-done | bytes 135200 | tf_op jit(solution)/shard_map/ppermute | solution.py:161
  42.4 0.0 collective-permute-done.7.rd
  42.4 1.3 shard_map.141
  43.7 0.3 all-to-all-done
  44.0 2.9 %collective-permute-start.8 = (bf16[16,64,1024]{2,1,0:T(8,128)(2,1)}, bf16[16,64,1024]{2,1,0:T(8,128)(2,1)S(1)}, u32[]{:S(2)}, u32[]{:S(2)}) collective-permute-start(bf16[16,64,1024]{2,1,0:T(8,128)(2,1)} %all-to-all-done), channel_id=1, source_target_pairs={{0,64},{64,0},{1,65},{65,1},{2,66},{66,2},{3,67},{67,3},{4,68},{68... | collective-permute-start | bytes 6291464 | tf_op jit(solution)/shard_map/ppermute | solution.py:212
  46.9 7.3 %all-to-all-start.1 = ((bf16[32,32,128]{2,1,0:T(8,128)(2,1)}), bf16[32,32,128]{2,1,0:T(8,128)(2,1)S(1)}, u32[]{:S(2)}, u32[]{:S(2)}) async-start(bf16[32,32,128]{2,1,0:T(8,128)(2,1)} %bitcast.7), calls=%async_computation.1 | async-start | bytes 524288 | tf_op jit(solution)/shard_map/all_to_all | solution.py:210
  54.3 64.6 %shard_map.142.refs_0_ = bf16[2,2,512,1024]{3,2,1,0:T(8,128)(2,1)} custom-call(s32[1]{0:T(128)} %bitcast.2.place, bf16[2,512,1024]{2,1,0:T(8,128)(2,1)} %bitcast.5.half), custom_call_target="tpu_custom_call" | custom-call | bytes 4194304 | tf_op jit(solution)/shard_map/pallas_call | solution.py:148
  118.9 0.0 all-to-all-done.1
  118.9 0.0 collective-permute-done.8
  118.9 0.0 copy-start.4
  118.9 1.3 copy-done.4
  120.3 64.6 %shard_map.143 = bf16[2,2,512,1024]{3,2,1,0:T(8,128)(2,1)} custom-call(s32[1]{0:T(128)S(6)} %sub.23.place, bf16[2,512,1024]{2,1,0:T(8,128)(2,1)} %bitcast.11, bf16[2,2,512,1024]{3,2,1,0:T(8,128)(2,1)} %shard_map.142.refs_0_), custom_call_target="tpu_custom_call", output_to_operand_aliasing={{}: (2, {})} | custom-call | bytes 4194304 | tf_op jit(solution)/shard_map/pallas_call | solution.py:148
  184.9 0.7 copy.19
  (2 shorter events, 0.0 us)
Async XLA Ops:
  5.1 7.8 %copy-start.6 = (s32[3]{0:T(128)S(1)}, s32[3]{0:T(128)}, u32[]{:S(2)}) copy-start(s32[3]{0:T(128)} %constant.44.clone) | copy-start | bytes 40
  5.1 7.8 %copy-start.2 = (bf16[512,2048]{1,0:T(8,128)(2,1)S(1)}, bf16[512,2048]{1,0:T(8,128)(2,1)}, u32[]{:S(2)}) copy-start(bf16[512,2048]{1,0:T(8,128)(2,1)} %x.3) | copy-start | bytes 6291460
  5.1 38.8 %all-to-all-start = ((bf16[16,64,1024]{2,1,0:T(8,128)(2,1)}), bf16[16,64,1024]{2,1,0:T(8,128)(2,1)}, u32[]{:S(2)}, u32[]{:S(2)}) async-start(bf16[16,64,1024]{2,1,0:T(8,128)(2,1)} %broadcast_in_dim.2), calls=%async_computation | async-start | bytes 4194304 | tf_op jit(solution)/shard_map/all_to_all | solution.py:177
  12.9 2.2 %copy-start = (bf16[2048,1024]{1,0:T(8,128)(2,1)S(1)}, bf16[2048,1024]{1,0:T(8,128)(2,1)}, u32[]{:S(2)}) copy-start(bf16[2048,1024]{1,0:T(8,128)(2,1)} %wc.3) | copy-start | bytes 12582916
  15.1 11.6 %copy-start.5 = (s32[5]{0:T(128)S(1)}, s32[5]{0:T(128)}, u32[]{:S(2)}) copy-start(s32[5]{0:T(128)} %constant.45.clone) | copy-start | bytes 64
  15.1 11.6 %copy-start.1 = (bf16[2048,1024]{1,0:T(8,128)(2,1)S(1)}, bf16[2048,1024]{1,0:T(8,128)(2,1)}, u32[]{:S(2)}) copy-start(bf16[2048,1024]{1,0:T(8,128)(2,1)} %wc.3) | copy-start | bytes 12582916
  17.8 12.8 %collective-permute-start.3 = (s16[272,128]{1,0:T(8,128)(2,1)S(1)}, s16[272,128]{1,0:T(8,128)(2,1)S(1)}, u32[]{:S(2)}, u32[]{:S(2)}) collective-permute-start(s16[272,128]{1,0:T(8,128)(2,1)S(1)} %get-tuple-element.23), channel_id=1, source_target_pairs={{0,2},{1,3},{2,4},{3,5},{4,6},{5,7},{6,0},{7,1},{8,10},{9,11},{10,... | collective-permute-start | bytes 208904 | tf_op jit(solution)/shard_map/ppermute | solution.py:161
  20.9 12.4 %collective-permute-start.5 = (s16[272,128]{1,0:T(8,128)(2,1)S(1)}, s16[272,128]{1,0:T(8,128)(2,1)S(1)}, u32[]{:S(2)}, u32[]{:S(2)}) collective-permute-start(s16[272,128]{1,0:T(8,128)(2,1)S(1)} %get-tuple-element.26), channel_id=1, source_target_pairs={{0,6},{1,7},{2,0},{3,1},{4,2},{5,3},{6,4},{7,5},{8,14},{9,15},{10,... | collective-permute-start | bytes 208904 | tf_op jit(solution)/shard_map/ppermute | solution.py:161
  24.0 9.3 %collective-permute-start.2 = (s16[528,128]{1,0:T(8,128)(2,1)S(1)}, s16[528,128]{1,0:T(8,128)(2,1)S(1)}, u32[]{:S(2)}, u32[]{:S(2)}) collective-permute-start(s16[528,128]{1,0:T(8,128)(2,1)S(1)} %get-tuple-element.22), channel_id=1, source_target_pairs={{0,1},{1,2},{2,3},{3,4},{4,5},{5,6},{6,7},{7,0},{8,9},{9,10},{10,1... | collective-permute-start | bytes 405512 | tf_op jit(solution)/shard_map/ppermute | solution.py:161
  24.8 8.5 %collective-permute-start.4 = (s16[528,128]{1,0:T(8,128)(2,1)S(1)}, s16[528,128]{1,0:T(8,128)(2,1)S(1)}, u32[]{:S(2)}, u32[]{:S(2)}) collective-permute-start(s16[528,128]{1,0:T(8,128)(2,1)S(1)} %get-tuple-element.25), channel_id=1, source_target_pairs={{0,7},{1,0},{2,1},{3,2},{4,3},{5,4},{6,5},{7,6},{8,15},{9,8},{10,9... | collective-permute-start | bytes 405512 | tf_op jit(solution)/shard_map/ppermute | solution.py:161
  26.7 10.5 %copy-start.3 = (s32[512,1]{0,1:T(1,128)S(1)}, s32[512,1]{0,1:T(1,128)}, u32[]{:S(2)}) copy-start(s32[512,1]{0,1:T(1,128)} %param.17) | copy-start | bytes 6148
  30.5 7.4 %collective-permute-start = (s16[528,128]{1,0:T(8,128)(2,1)S(1)}, s16[528,128]{1,0:T(8,128)(2,1)S(1)}, u32[]{:S(2)}, u32[]{:S(2)}) collective-permute-start(s16[528,128]{1,0:T(8,128)(2,1)S(1)} %get-tuple-element.19), channel_id=1, source_target_pairs={{0,1},{1,2},{2,3},{3,4},{4,5},{5,6},{6,7},{7,0},{8,9},{9,10},{10,1... | collective-permute-start | bytes 405512 | tf_op jit(solution)/shard_map/ppermute | solution.py:161
  30.6 7.3 %collective-permute-start.1 = (s16[528,128]{1,0:T(8,128)(2,1)S(1)}, s16[528,128]{1,0:T(8,128)(2,1)S(1)}, u32[]{:S(2)}, u32[]{:S(2)}) collective-permute-start(s16[528,128]{1,0:T(8,128)(2,1)S(1)} %get-tuple-element.20), channel_id=1, source_target_pairs={{0,7},{1,0},{2,1},{3,2},{4,3},{5,4},{6,5},{7,6},{8,15},{9,8},{10,9... | collective-permute-start | bytes 405512 | tf_op jit(solution)/shard_map/ppermute | solution.py:161
  33.5 8.8 %collective-permute-start.6 = (s16[528,128]{1,0:T(8,128)(2,1)S(1)}, s16[528,128]{1,0:T(8,128)(2,1)S(1)}, u32[]{:S(2)}, u32[]{:S(2)}) collective-permute-start(s16[528,128]{1,0:T(8,128)(2,1)S(1)} %get-tuple-element.27), channel_id=1, source_target_pairs={{0,2},{1,3},{2,4},{3,5},{4,6},{5,7},{6,0},{7,1},{8,10},{9,11},{10,... | collective-permute-start | bytes 405512 | tf_op jit(solution)/shard_map/ppermute | solution.py:161
  33.7 8.7 %collective-permute-start.7 = (s16[528,128]{1,0:T(8,128)(2,1)S(1)}, s16[528,128]{1,0:T(8,128)(2,1)S(1)}, u32[]{:S(2)}, u32[]{:S(2)}) collective-permute-start(s16[528,128]{1,0:T(8,128)(2,1)S(1)} %get-tuple-element.28), channel_id=1, source_target_pairs={{0,6},{1,7},{2,0},{3,1},{4,2},{5,3},{6,4},{7,5},{8,14},{9,15},{10,... | collective-permute-start | bytes 405512 | tf_op jit(solution)/shard_map/ppermute | solution.py:161
  44.0 75.0 %collective-permute-start.8 = (bf16[16,64,1024]{2,1,0:T(8,128)(2,1)}, bf16[16,64,1024]{2,1,0:T(8,128)(2,1)S(1)}, u32[]{:S(2)}, u32[]{:S(2)}) collective-permute-start(bf16[16,64,1024]{2,1,0:T(8,128)(2,1)} %all-to-all-done), channel_id=1, source_target_pairs={{0,64},{64,0},{1,65},{65,1},{2,66},{66,2},{3,67},{67,3},{4,68},{68... | collective-permute-start | bytes 6291464 | tf_op jit(solution)/shard_map/ppermute | solution.py:212
  46.9 72.0 %all-to-all-start.1 = ((bf16[32,32,128]{2,1,0:T(8,128)(2,1)}), bf16[32,32,128]{2,1,0:T(8,128)(2,1)S(1)}, u32[]{:S(2)}, u32[]{:S(2)}) async-start(bf16[32,32,128]{2,1,0:T(8,128)(2,1)} %bitcast.7), calls=%async_computation.1 | async-start | bytes 524288 | tf_op jit(solution)/shard_map/all_to_all | solution.py:210
  118.9 1.3 copy-start.4

commit v4 on v3

--- a/solution.py
+++ b/solution.py
@@ -130,29 +130,26 @@
 
 
 def half_kernel(place, half, *refs):
-    out, sems = refs[-2:]
-    copies = [
-        pltpu.make_async_copy(half.at[i], out.at[i, place[0]], sems.at[i])
-        for i in range(half.shape[0])
-    ]
-    for copy in copies:
-        copy.start()
-    for copy in copies:
-        copy.wait()
+    refs[-1][...] = half[...].reshape(refs[-1].shape)
 
 
 def set_half(place, half, pair=None):
-    anywhere = pl.BlockSpec(memory_space=pl.ANY)
     lanes, rows, width = half.shape
+    step = rows // 2
     args = (place, half) + (() if pair is None else (pair,))
     return pl.pallas_call(
         half_kernel,
         out_shape=jax.ShapeDtypeStruct((lanes, 2, rows, width), half.dtype),
-        in_specs=[pl.BlockSpec(memory_space=pltpu.SMEM)] + [anywhere] * (len(args) - 1),
-        out_specs=anywhere,
-        scratch_shapes=[pltpu.SemaphoreType.DMA((lanes,))],
+        grid_spec=pltpu.PrefetchScalarGridSpec(
+            num_scalar_prefetch=1,
+            grid=(lanes, rows // step),
+            in_specs=[pl.BlockSpec((1, step, width), lambda i, j, place: (i, j, 0))]
+            + [pl.BlockSpec(memory_space=pl.ANY)] * (len(args) - 2),
+            out_specs=pl.BlockSpec((1, 1, step, width), lambda i, j, place: (i, place[0], j, 0)),
+        ),
         input_output_aliases={} if pair is None else {2: 0},
-        cost_estimate=pl.CostEstimate(flops=0, bytes_accessed=2 * half.size * 2, transcendentals=0),
+        compiler_params=pltpu.CompilerParams(vmem_limit_bytes=16 * 2**20),
+        cost_estimate=pl.CostEstimate(flops=0, bytes_accessed=4 * half.size, transcendentals=0),
     )(*args)
 
 

time: 186 us -> 69.8 us (0.38)
  Pallas kernels: 138 us -> 14.3 us
  waiting for transfers between devices: 4.82 us -> 11.6 us
    pallas_call x2, Pallas kernels: 129 us -> 5.64 us  [set_half(): pl.pallas_call(half_kernel, out_shape=jax.ShapeDtypeStruct((lanes, 2, row...]
    all_to_all x1, waiting for transfers between devices: 0.01 us -> 7.19 us  [local(): lax.all_to_all(placed, PLANE, split_axis=0, concat_axis=0, tiled=True)]
  transfers between devices with their start and end apart: 11 -> 11, of which waited for: 2 -> 2; matrix products, arithmetic and copies ran while one was open for 0% -> 0% of each run, Pallas kernels for 40% -> 15%
where the time goes in v4:
time: 69.8 us; the launch traced here: 69.4 us
  starting transfers between devices  33.7 us (48%)
  Pallas kernels  14.3 us (20%)
  waiting for transfers between devices  11.6 us (17%)
  local copies, waits for them, and re-layouts  6.08 us (9%)
  other arithmetic  2.19 us (3%)
  between operations  1.51 us (2%)
    ppermute x8, starting transfers between devices, along_tp(): lax.ppermute(value, 'tp', [(i, (i + step) % size) for i in range(size)])  15.2 us
    all_to_all x1, starting transfers between devices, local(): lax.all_to_all(spread, CHIPS, split_axis=0, concat_axis=0, tiled=True)  7.72 us
    all_to_all x1, starting transfers between devices, local(): lax.all_to_all(placed, PLANE, split_axis=0, concat_axis=0, tiled=True)  7.38 us
    all_to_all x1, waiting for transfers between devices, local(): lax.all_to_all(placed, PLANE, split_axis=0, concat_axis=0, tiled=True)  7.19 us
    pallas_call x2, Pallas kernels, products(): pl.pallas_call(kernel, out_shape=outs, grid_spec=pltpu.PrefetchScalarGrid...  6.47 us
    pallas_call x2, Pallas kernels, set_half(): pl.pallas_call(half_kernel, out_shape=jax.ShapeDtypeStruct((lanes, 2, row...  5.64 us
    unnamed x15, local copies, waits for them, and re-layouts  4.5 us
    ppermute x8, waiting for transfers between devices, along_tp(): lax.ppermute(value, 'tp', [(i, (i + step) % size) for i in range(size)])  4.42 us
  transfers between devices with their start and end apart: 11, of which 2 were waited for; matrix products, arithmetic and copies ran while one was open for 0% of the time, Pallas kernels for 15%

profile of v4, /device:TPU:1, one launch (start us, length us, event | category | flops | bytes accessed | tf_op | source)
XLA Modules:
  0.0 69.4 jit_solution(3339468337068387166)
XLA Ops:
  1.4 2.2 %fusion.3 = (bf16[64,1024]{1,0:T(8,128)(2,1)S(1)}, f32[64,1024]{1,0:T(8,128)}, f32[64,1024]{1,0:T(8,128)}, f32[64,1024]{1,0:T(8,128)}) fusion(f32[64,1024]{1,0:T(8,128)} %param.10, f32[]{:T(128)} %bitcast.1, f32[]{:T(128)} %bitcast, f32[64,1024]{1,0:T(8,128)} %param.13, f32[64,1024]{1,0:T(8,128)} %param.12, f32[64,1024]{1,0:T(8,128)} %param.11), kind=kLoop, calls=%fused_computation.10 | loop fusion | flops 1048576 | bytes 1966088 | tf_op jit(solution)/shard_map/convert_element_type | solution.py:172
  3.5 1.6 %broadcast_in_dim.2 = bf16[16,64,1024]{2,1,0:T(8,128)(2,1)} broadcast(bf16[64,1024]{1,0:T(8,128)(2,1)S(1)} %get-tuple-element.31), dimensions={1,2} | broadcast | bytes 2228224 | tf_op jit(solution)/shard_map/broadcast_in_dim | solution.py:173
  5.1 0.0 copy-start.6
  5.1 7.7 %all-to-all-start = ((bf16[16,64,1024]{2,1,0:T(8,128)(2,1)}), bf16[16,64,1024]{2,1,0:T(8,128)(2,1)S(1)}, u32[]{:S(2)}, u32[]{:S(2)}) async-start(bf16[16,64,1024]{2,1,0:T(8,128)(2,1)} %broadcast_in_dim.2), calls=%async_computation | async-start | bytes 4194304 | tf_op jit(solution)/shard_map/all_to_all | solution.py:174
  12.8 0.0 copy-done.6
  12.9 0.0 copy-start
  12.9 2.2 %copy-done = bf16[2048,1024]{1,0:T(8,128)(2,1)S(1)} copy-done((bf16[2048,1024]{1,0:T(8,128)(2,1)S(1)}, bf16[2048,1024]{1,0:T(8,128)(2,1)}, u32[]{:S(2)}) %copy-start) | copy-done | bytes 4194328
  15.1 0.0 copy-start.2
  15.1 1.6 %copy-done.2 = bf16[512,2048]{1,0:T(8,128)(2,1)S(1)} copy-done((bf16[512,2048]{1,0:T(8,128)(2,1)S(1)}, bf16[512,2048]{1,0:T(8,128)(2,1)}, u32[]{:S(2)}) %copy-start.2) | copy-done | bytes 2097176
  16.7 0.0 copy-start.5
  16.7 0.0 copy-start.1
  16.7 0.0 copy-start.3
  16.7 2.7 %shard_map.138 = (s16[528,128]{1,0:T(8,128)(2,1)S(1)}, s16[528,128]{1,0:T(8,128)(2,1)S(1)}, s16[272,128]{1,0:T(8,128)(2,1)S(1)}, s16[272,128]{1,0:T(8,128)(2,1)S(1)}) custom-call(s32[3]{0:T(128)S(1)} %compare_select_fusion.ids, bf16[512,2048]{1,0:T(8,128)(2,1)S(1)} %copy-done.2, bf16[2048,1024]{1,0:T(8,128)(2,1)S(1)} %copy-done, ...), custom_call_target="tpu_custom_call" | custom-call | flops 805306368 | bytes 3670016 | tf_op jit(solution)/shard_map/pallas_call | solution.py:72
  19.4 3.1 %collective-permute-start.3 = (s16[272,128]{1,0:T(8,128)(2,1)S(1)}, s16[272,128]{1,0:T(8,128)(2,1)S(1)}, u32[]{:S(2)}, u32[]{:S(2)}) collective-permute-start(s16[272,128]{1,0:T(8,128)(2,1)S(1)} %get-tuple-element.23), channel_id=1, source_target_pairs={{0,2},{1,3},{2,4},{3,5},{4,6},{5,7},{6,0},{7,1},{8,10},{9,11},{10,... | collective-permute-start | bytes 208904 | tf_op jit(solution)/shard_map/ppermute | solution.py:158
  22.4 3.1 %collective-permute-start.5 = (s16[272,128]{1,0:T(8,128)(2,1)S(1)}, s16[272,128]{1,0:T(8,128)(2,1)S(1)}, u32[]{:S(2)}, u32[]{:S(2)}) collective-permute-start(s16[272,128]{1,0:T(8,128)(2,1)S(1)} %get-tuple-element.26), channel_id=1, source_target_pairs={{0,6},{1,7},{2,0},{3,1},{4,2},{5,3},{6,4},{7,5},{8,14},{9,15},{10,... | collective-permute-start | bytes 208904 | tf_op jit(solution)/shard_map/ppermute | solution.py:158
  25.5 0.8 %collective-permute-start.2 = (s16[528,128]{1,0:T(8,128)(2,1)S(1)}, s16[528,128]{1,0:T(8,128)(2,1)S(1)}, u32[]{:S(2)}, u32[]{:S(2)}) collective-permute-start(s16[528,128]{1,0:T(8,128)(2,1)S(1)} %get-tuple-element.22), channel_id=1, source_target_pairs={{0,1},{1,2},{2,3},{3,4},{4,5},{5,6},{6,7},{7,0},{8,9},{9,10},{10,1... | collective-permute-start | bytes 405512 | tf_op jit(solution)/shard_map/ppermute | solution.py:158
  26.3 1.9 %collective-permute-start.4 = (s16[528,128]{1,0:T(8,128)(2,1)S(1)}, s16[528,128]{1,0:T(8,128)(2,1)S(1)}, u32[]{:S(2)}, u32[]{:S(2)}) collective-permute-start(s16[528,128]{1,0:T(8,128)(2,1)S(1)} %get-tuple-element.25), channel_id=1, source_target_pairs={{0,7},{1,0},{2,1},{3,2},{4,3},{5,4},{6,5},{7,6},{8,15},{9,8},{10,9... | collective-permute-start | bytes 405512 | tf_op jit(solution)/shard_map/ppermute | solution.py:158
  28.2 0.0 copy-done.5
  28.2 0.0 copy-done.1
  28.2 0.0 copy-done.3
  28.2 0.0 copy-start.4
  28.2 3.8 %shard_map.137 = (s16[528,128]{1,0:T(8,128)(2,1)S(1)}, s16[528,128]{1,0:T(8,128)(2,1)S(1)}, f32[512,128]{1,0:T(8,128)S(1)}, f32[512,128]{1,0:T(8,128)S(1)}, f32[512,128]{1,0:T(8,128)S(1)}) custom-call(s32[5]{0:T(128)S(1)} %compare_select_fusion.2.ids, bf16[512,2048]{1,0:T(8,128)(2,1)S(1)} %copy-done.3, bf16[2048,1024]{1,0:T(8,128)(2,1)S(1)} %copy-done.1, ...), custom_call_target="tpu_custom_call" | custom-call | flops 1342177280 | bytes 4718592 | tf_op jit(solution)/shard_map/pallas_call | solution.py:72
  32.0 0.1 collective-permute-start
  32.1 0.0 collective-permute-done.3.far_a
  32.1 2.7 %collective-permute-start.1 = (s16[528,128]{1,0:T(8,128)(2,1)S(1)}, s16[528,128]{1,0:T(8,128)(2,1)S(1)}, u32[]{:S(2)}, u32[]{:S(2)}) collective-permute-start(s16[528,128]{1,0:T(8,128)(2,1)S(1)} %get-tuple-element.20), channel_id=1, source_target_pairs={{0,7},{1,0},{2,1},{3,2},{4,3},{5,4},{6,5},{7,6},{8,15},{9,8},{10,9... | collective-permute-start | bytes 405512 | tf_op jit(solution)/shard_map/ppermute | solution.py:158
  34.8 0.0 collective-permute-done.5.far_b
  34.8 0.0 collective-permute-done.2.next_a
  34.8 0.0 collective-permute-done.4.next_b
  34.8 0.3 shard_map.139
  35.1 0.1 collective-permute-start.6
  35.2 3.6 %collective-permute-start.7 = (s16[528,128]{1,0:T(8,128)(2,1)S(1)}, s16[528,128]{1,0:T(8,128)(2,1)S(1)}, u32[]{:S(2)}, u32[]{:S(2)}) collective-permute-start(s16[528,128]{1,0:T(8,128)(2,1)S(1)} %get-tuple-element.28), channel_id=1, source_target_pairs={{0,6},{1,7},{2,0},{3,1},{4,2},{5,3},{6,4},{7,5},{8,14},{9,15},{10,... | collective-permute-start | bytes 405512 | tf_op jit(solution)/shard_map/ppermute | solution.py:158
  38.7 0.0 copy-done.4
  38.7 0.6 shard_map.140.selector
  39.4 0.0 collective-permute-done.ra
  39.4 0.0 collective-permute-done.1.rb
  39.4 4.4 %collective-permute-done.6.rc = s16[528,128]{1,0:T(8,128)(2,1)S(1)} collective-permute-done((s16[528,128]{1,0:T(8,128)(2,1)S(1)}, s16[528,128]{1,0:T(8,128)(2,1)S(1)}, u32[]{:S(2)}, u32[]{:S(2)}) %collective-permute-start.6) | collective-permute-done | bytes 135200 | tf_op jit(solution)/shard_map/ppermute | solution.py:158
  43.8 0.0 collective-permute-done.7.rd
  43.8 1.3 %shard_map.141 = bf16[1024,128]{1,0:T(8,128)(2,1)} custom-call(f32[512,128]{1,0:T(8,128)S(1)} %get-tuple-element.18.own, s16[528,128]{1,0:T(8,128)(2,1)S(1)} %collective-permute-done.ra, s16[528,128]{1,0:T(8,128)(2,1)S(1)} %collective-permute-done.1.rb, s16[528,128]{1,0:T(8,128)(2,1)S(1)} %collective-permute-done.6.rc, ...), custom_call_target="tpu_custom_call" | custom-call | bytes 1048576 | tf_op jit(solution)/shard_map/pallas_call | solution.py:91
  45.1 0.0 all-to-all-done
  45.1 3.3 %collective-permute-start.8 = (bf16[16,64,1024]{2,1,0:T(8,128)(2,1)S(1)}, bf16[16,64,1024]{2,1,0:T(8,128)(2,1)}, u32[]{:S(2)}, u32[]{:S(2)}) collective-permute-start(bf16[16,64,1024]{2,1,0:T(8,128)(2,1)S(1)} %all-to-all-done), channel_id=1, source_target_pairs={{0,64},{64,0},{1,65},{65,1},{2,66},{66,2},{3,67},{67,3},{4,68},{68... | collective-permute-start | bytes 6291464 | tf_op jit(solution)/shard_map/ppermute | solution.py:209
  48.5 7.4 %all-to-all-start.1 = ((bf16[32,32,128]{2,1,0:T(8,128)(2,1)}), bf16[32,32,128]{2,1,0:T(8,128)(2,1)S(1)}, u32[]{:S(2)}, u32[]{:S(2)}) async-start(bf16[32,32,128]{2,1,0:T(8,128)(2,1)} %bitcast.7), calls=%async_computation.1 | async-start | bytes 524288 | tf_op jit(solution)/shard_map/all_to_all | solution.py:207
  55.9 1.9 %shard_map.142.refs_0_ = bf16[2,2,512,1024]{3,2,1,0:T(8,128)(2,1)} custom-call(s32[1]{0:T(128)} %bitcast.2.place, bf16[2,512,1024]{2,1,0:T(8,128)(2,1)S(1)} %bitcast.9), custom_call_target="tpu_custom_call" | custom-call | bytes 4194304 | tf_op jit(solution)/shard_map/pallas_call | solution.py:140
  57.7 7.2 %all-to-all-done.1 = bf16[32,32,128]{2,1,0:T(8,128)(2,1)S(1)} async-done(((bf16[32,32,128]{2,1,0:T(8,128)(2,1)}), bf16[32,32,128]{2,1,0:T(8,128)(2,1)S(1)}, u32[]{:S(2)}, u32[]{:S(2)}) %all-to-all-start.1) | async-done | bytes 262176 | tf_op jit(solution)/shard_map/all_to_all | solution.py:207
  64.9 0.0 collective-permute-done.8
  64.9 3.8 %shard_map.143 = bf16[2,2,512,1024]{3,2,1,0:T(8,128)(2,1)} custom-call(s32[1]{0:T(128)S(6)} %sub.23.place, bf16[2,512,1024]{2,1,0:T(8,128)(2,1)} %bitcast.4.half, bf16[2,2,512,1024]{3,2,1,0:T(8,128)(2,1)} %shard_map.142.refs_0_), custom_call_target="tpu_custom_call", output_to_operand_aliasing={{}: (2, {})} | custom-call | bytes 4194304 | tf_op jit(solution)/shard_map/pallas_call | solution.py:140
  68.7 0.7 %copy.19 = bf16[1,32,32,128]{3,2,1,0:T(8,128)(2,1)} copy(bf16[1,32,32,128]{3,2,1,0:T(8,128)(2,1)S(1)} %bitcast.12) | data formatting | bytes 524288
  (2 shorter events, 0.0 us)
Async XLA Ops:
  5.1 7.7 %copy-start.6 = (s32[3]{0:T(128)S(1)}, s32[3]{0:T(128)}, u32[]{:S(2)}) copy-start(s32[3]{0:T(128)} %constant.44.clone) | copy-start | bytes 40
  5.1 40.0 %all-to-all-start = ((bf16[16,64,1024]{2,1,0:T(8,128)(2,1)}), bf16[16,64,1024]{2,1,0:T(8,128)(2,1)S(1)}, u32[]{:S(2)}, u32[]{:S(2)}) async-start(bf16[16,64,1024]{2,1,0:T(8,128)(2,1)} %broadcast_in_dim.2), calls=%async_computation | async-start | bytes 4194304 | tf_op jit(solution)/shard_map/all_to_all | solution.py:174
  12.9 2.2 %copy-start = (bf16[2048,1024]{1,0:T(8,128)(2,1)S(1)}, bf16[2048,1024]{1,0:T(8,128)(2,1)}, u32[]{:S(2)}) copy-start(bf16[2048,1024]{1,0:T(8,128)(2,1)} %wc.3) | copy-start | bytes 12582916
  15.1 1.6 %copy-start.2 = (bf16[512,2048]{1,0:T(8,128)(2,1)S(1)}, bf16[512,2048]{1,0:T(8,128)(2,1)}, u32[]{:S(2)}) copy-start(bf16[512,2048]{1,0:T(8,128)(2,1)} %x.3) | copy-start | bytes 6291460
  16.7 11.6 %copy-start.5 = (s32[5]{0:T(128)S(1)}, s32[5]{0:T(128)}, u32[]{:S(2)}) copy-start(s32[5]{0:T(128)} %constant.45.clone) | copy-start | bytes 64
  16.7 11.6 %copy-start.1 = (bf16[2048,1024]{1,0:T(8,128)(2,1)S(1)}, bf16[2048,1024]{1,0:T(8,128)(2,1)}, u32[]{:S(2)}) copy-start(bf16[2048,1024]{1,0:T(8,128)(2,1)} %wc.3) | copy-start | bytes 12582916
  16.7 11.6 %copy-start.3 = (bf16[512,2048]{1,0:T(8,128)(2,1)S(1)}, bf16[512,2048]{1,0:T(8,128)(2,1)}, u32[]{:S(2)}) copy-start(bf16[512,2048]{1,0:T(8,128)(2,1)} %x.3) | copy-start | bytes 6291460
  19.4 12.8 %collective-permute-start.3 = (s16[272,128]{1,0:T(8,128)(2,1)S(1)}, s16[272,128]{1,0:T(8,128)(2,1)S(1)}, u32[]{:S(2)}, u32[]{:S(2)}) collective-permute-start(s16[272,128]{1,0:T(8,128)(2,1)S(1)} %get-tuple-element.23), channel_id=1, source_target_pairs={{0,2},{1,3},{2,4},{3,5},{4,6},{5,7},{6,0},{7,1},{8,10},{9,11},{10,... | collective-permute-start | bytes 208904 | tf_op jit(solution)/shard_map/ppermute | solution.py:158
  22.4 12.4 %collective-permute-start.5 = (s16[272,128]{1,0:T(8,128)(2,1)S(1)}, s16[272,128]{1,0:T(8,128)(2,1)S(1)}, u32[]{:S(2)}, u32[]{:S(2)}) collective-permute-start(s16[272,128]{1,0:T(8,128)(2,1)S(1)} %get-tuple-element.26), channel_id=1, source_target_pairs={{0,6},{1,7},{2,0},{3,1},{4,2},{5,3},{6,4},{7,5},{8,14},{9,15},{10,... | collective-permute-start | bytes 208904 | tf_op jit(solution)/shard_map/ppermute | solution.py:158
  25.5 9.3 %collective-permute-start.2 = (s16[528,128]{1,0:T(8,128)(2,1)S(1)}, s16[528,128]{1,0:T(8,128)(2,1)S(1)}, u32[]{:S(2)}, u32[]{:S(2)}) collective-permute-start(s16[528,128]{1,0:T(8,128)(2,1)S(1)} %get-tuple-element.22), channel_id=1, source_target_pairs={{0,1},{1,2},{2,3},{3,4},{4,5},{5,6},{6,7},{7,0},{8,9},{9,10},{10,1... | collective-permute-start | bytes 405512 | tf_op jit(solution)/shard_map/ppermute | solution.py:158
  26.3 8.5 %collective-permute-start.4 = (s16[528,128]{1,0:T(8,128)(2,1)S(1)}, s16[528,128]{1,0:T(8,128)(2,1)S(1)}, u32[]{:S(2)}, u32[]{:S(2)}) collective-permute-start(s16[528,128]{1,0:T(8,128)(2,1)S(1)} %get-tuple-element.25), channel_id=1, source_target_pairs={{0,7},{1,0},{2,1},{3,2},{4,3},{5,4},{6,5},{7,6},{8,15},{9,8},{10,9... | collective-permute-start | bytes 405512 | tf_op jit(solution)/shard_map/ppermute | solution.py:158
  28.2 10.5 %copy-start.4 = (s32[512,1]{0,1:T(1,128)S(1)}, s32[512,1]{0,1:T(1,128)}, u32[]{:S(2)}) copy-start(s32[512,1]{0,1:T(1,128)} %param.17) | copy-start | bytes 6148
  32.0 7.4 %collective-permute-start = (s16[528,128]{1,0:T(8,128)(2,1)S(1)}, s16[528,128]{1,0:T(8,128)(2,1)S(1)}, u32[]{:S(2)}, u32[]{:S(2)}) collective-permute-start(s16[528,128]{1,0:T(8,128)(2,1)S(1)} %get-tuple-element.19), channel_id=1, source_target_pairs={{0,1},{1,2},{2,3},{3,4},{4,5},{5,6},{6,7},{7,0},{8,9},{9,10},{10,1... | collective-permute-start | bytes 405512 | tf_op jit(solution)/shard_map/ppermute | solution.py:158
  32.1 7.3 %collective-permute-start.1 = (s16[528,128]{1,0:T(8,128)(2,1)S(1)}, s16[528,128]{1,0:T(8,128)(2,1)S(1)}, u32[]{:S(2)}, u32[]{:S(2)}) collective-permute-start(s16[528,128]{1,0:T(8,128)(2,1)S(1)} %get-tuple-element.20), channel_id=1, source_target_pairs={{0,7},{1,0},{2,1},{3,2},{4,3},{5,4},{6,5},{7,6},{8,15},{9,8},{10,9... | collective-permute-start | bytes 405512 | tf_op jit(solution)/shard_map/ppermute | solution.py:158
  35.1 8.7 %collective-permute-start.6 = (s16[528,128]{1,0:T(8,128)(2,1)S(1)}, s16[528,128]{1,0:T(8,128)(2,1)S(1)}, u32[]{:S(2)}, u32[]{:S(2)}) collective-permute-start(s16[528,128]{1,0:T(8,128)(2,1)S(1)} %get-tuple-element.27), channel_id=1, source_target_pairs={{0,2},{1,3},{2,4},{3,5},{4,6},{5,7},{6,0},{7,1},{8,10},{9,11},{10,... | collective-permute-start | bytes 405512 | tf_op jit(solution)/shard_map/ppermute | solution.py:158
  35.2 8.7 %collective-permute-start.7 = (s16[528,128]{1,0:T(8,128)(2,1)S(1)}, s16[528,128]{1,0:T(8,128)(2,1)S(1)}, u32[]{:S(2)}, u32[]{:S(2)}) collective-permute-start(s16[528,128]{1,0:T(8,128)(2,1)S(1)} %get-tuple-element.28), channel_id=1, source_target_pairs={{0,6},{1,7},{2,0},{3,1},{4,2},{5,3},{6,4},{7,5},{8,14},{9,15},{10,... | collective-permute-start | bytes 405512 | tf_op jit(solution)/shard_map/ppermute | solution.py:158
  45.1 19.8 %collective-permute-start.8 = (bf16[16,64,1024]{2,1,0:T(8,128)(2,1)S(1)}, bf16[16,64,1024]{2,1,0:T(8,128)(2,1)}, u32[]{:S(2)}, u32[]{:S(2)}) collective-permute-start(bf16[16,64,1024]{2,1,0:T(8,128)(2,1)S(1)} %all-to-all-done), channel_id=1, source_target_pairs={{0,64},{64,0},{1,65},{65,1},{2,66},{66,2},{3,67},{67,3},{4,68},{68... | collective-permute-start | bytes 6291464 | tf_op jit(solution)/shard_map/ppermute | solution.py:209
  48.5 16.4 %all-to-all-start.1 = ((bf16[32,32,128]{2,1,0:T(8,128)(2,1)}), bf16[32,32,128]{2,1,0:T(8,128)(2,1)S(1)}, u32[]{:S(2)}, u32[]{:S(2)}) async-start(bf16[32,32,128]{2,1,0:T(8,128)(2,1)} %bitcast.7), calls=%async_computation.1 | async-start | bytes 524288 | tf_op jit(solution)/shard_map/all_to_all | solution.py:207

commit v5 on v4

--- a/solution.py
+++ b/solution.py
@@ -1,5 +1,3 @@
-import functools
-
 import jax
 import jax.numpy as jnp
 from jax import lax
@@ -41,50 +39,94 @@
     return codes * (1.0 / LEVELS) * jnp.exp2(power * (1.0 / 256.0))
 
 
-def product(rows_ref, columns_ref):
-    return jnp.dot(rows_ref[...], columns_ref[...], preferred_element_type=jnp.float32)
-
-
-def far_kernel(ids, x, wa, wb, wc, qa, qb, qc, qd):
+def products_kernel(ids, x_hbm, w_hbm, up, down, far_up, far_down, next_up, next_down, own, x, w, x_sem, w_sems):
+    depth, part = w.shape[1], w.shape[2] // 2
     half = x.shape[0] // 2
-    put_coded(qa, product(x, wa))
-    put_coded(qb, product(x, wb))
-    far = product(x, wc)
-    put_coded(qc, far[:half])
-    put_coded(qd, far[half:])
-
-
-def near_kernel(ids, x, wa, wb, wc, wd, we, qa, qb, pc, pd, pe):
-    put_coded(qa, product(x, wa))
-    put_coded(qb, product(x, wb))
-    pc[...] = product(x, wc)
-    pd[...] = product(x, wd)
-    pe[...] = product(x, we)
-
-
-def products(kernel, x, w, ids, count, width, outs):
+    load = pltpu.make_async_copy(x_hbm, x, x_sem)
+    load.start()
+    loads = []
+    for k in range(8):
+        column = pl.multiple_of(ids[k] * part, part)
+        loads.append(
+            pltpu.make_async_copy(
+                w_hbm.at[:, pl.ds(column, part)],
+                w.at[k // 2, :, pl.ds(k % 2 * part, part)],
+                w_sems.at[k],
+            )
+        )
+        loads[-1].start()
+    load.wait()
+
+    def pair(k):
+        loads[2 * k].wait()
+        loads[2 * k + 1].wait()
+        both = jnp.dot(x[...], w[k], preferred_element_type=jnp.float32)
+        return both[:, :part], both[:, part:]
+
+    for k, out in enumerate((up, down)):
+        for i, value in enumerate(pair(k)):
+            put_coded(out.at[i], value)
+    far, mine = pair(2)
+    put_coded(far_up, far[:half])
+    put_coded(far_down, far[half:])
+    own[...] = mine
+    next_up[...], next_down[...] = pair(3)
+
+
+def products(x, w, ids, outs):
     rows, depth = x.shape
-    whole = lambda g, ids: (0, 0)
-    columns = [
-        pl.BlockSpec((depth, width), functools.partial(lambda k, g, ids: (0, ids[k]), k))
-        for k in range(count)
-    ]
-    return pl.pallas_call(
-        kernel,
+    width = w.shape[1] // 4
+    return pl.pallas_call(
+        products_kernel,
         out_shape=outs,
-        grid_spec=pltpu.PrefetchScalarGridSpec(
-            num_scalar_prefetch=1,
-            grid=(1,),
-            in_specs=[pl.BlockSpec((rows, depth), whole)] + columns,
-            out_specs=[pl.BlockSpec(o.shape, whole) for o in outs],
+        in_specs=[pl.BlockSpec(memory_space=pltpu.SMEM)] + [pl.BlockSpec(memory_space=pl.ANY)] * 2,
+        out_specs=[pl.BlockSpec(memory_space=pltpu.VMEM)] * len(outs),
+        scratch_shapes=[
+            pltpu.VMEM((rows, depth), x.dtype),
+            pltpu.VMEM((4, depth, width), w.dtype),
+            pltpu.SemaphoreType.DMA,
+            pltpu.SemaphoreType.DMA((8,)),
+        ],
+        compiler_params=pltpu.CompilerParams(vmem_limit_bytes=60 * 2**20),
+        cost_estimate=pl.CostEstimate(
+            flops=2 * rows * depth * w.shape[1], bytes_accessed=2 * (x.size + w.size), transcendentals=0
         ),
-        compiler_params=pltpu.CompilerParams(vmem_limit_bytes=40 * 2**20),
+    )(ids, x, w)
+
+
+def update_kernel(step_ref, master, moment, second, gradient, new_master, new_moment, new_second, spread):
+    def times(k, fixes):
+        return fixes[0] * 0.9, fixes[1] * 0.95
+
+    one = jnp.float32(1.0)
+    first, other = lax.fori_loop(0, step_ref[0], times, (one, one))
+    first_fix, second_fix = 1.0 - first, 1.0 - other
+    g, old = gradient[...], master[...]
+    m = 0.9 * moment[...] + 0.1 * g
+    v = 0.95 * second[...] + 0.05 * g * g
+    ones = jnp.ones((1, g.shape[1]), jnp.float32)
+    update = m / (ones * first_fix) / (jnp.sqrt(v / (ones * second_fix)) + 1e-08)
+    new = old - learn_rate * (update + decay_rate * old)
+    new_moment[...] = m
+    new_second[...] = v
+    new_master[...] = new
+    fresh = new.astype(jnp.bfloat16)
+    for k in range(spread.shape[0]):
+        spread[k] = fresh
+
+
+def updated(step_count, master, moment, second, gradient, chips):
+    same = jax.ShapeDtypeStruct(master.shape, jnp.float32)
+    return pl.pallas_call(
+        update_kernel,
+        out_shape=[same, same, same, jax.ShapeDtypeStruct((chips,) + master.shape, jnp.bfloat16)],
+        in_specs=[pl.BlockSpec(memory_space=pltpu.SMEM)] + [pl.BlockSpec(master.shape, lambda: (0, 0))] * 4,
+        out_specs=[pl.BlockSpec(master.shape, lambda: (0, 0))] * 3 + [pl.BlockSpec((chips,) + master.shape, lambda: (0, 0, 0))],
+        compiler_params=pltpu.CompilerParams(vmem_limit_bytes=60 * 2**20),
         cost_estimate=pl.CostEstimate(
-            flops=2 * rows * depth * width * count,
-            bytes_accessed=2 * depth * (rows + width * count),
-            transcendentals=0,
+            flops=30 * master.size, bytes_accessed=28 * master.size, transcendentals=3 * master.size
         ),
-    )(ids, x, *([w] * count))
+    )(step_count, master, moment, second, gradient)
 
 
 def local_call(kernel, outs, *args, flops=0):
@@ -98,10 +140,10 @@
 
 def merge_kernel(own_a, next_a, far_a, own_b, next_b, far_b, qa, qb):
     half = own_a.shape[0] // 2
-    total = own_a[...] + take_coded(next_a)
+    total = own_a[...] + take_coded(next_a.at[0])
     total = jnp.concatenate([total[:half] + take_coded(far_a), total[half:]], axis=0)
     put_coded(qa, total)
-    total = own_b[...] + take_coded(next_b)
+    total = own_b[...] + take_coded(next_b.at[0])
     total = jnp.concatenate([total[:half], total[half:] + take_coded(far_b)], axis=0)
     put_coded(qb, total)
 
@@ -123,7 +165,7 @@
 
 
 def final_kernel(own, ra, rb, rc, rd, selector, out):
-    keys = own[...] + take_coded(ra) + take_coded(rb) + take_coded(rc) + take_coded(rd)
+    keys = own[...] + take_coded(ra.at[1]) + take_coded(rb.at[1]) + take_coded(rc) + take_coded(rd)
     out[...] = jnp.dot(
         selector[...], keys.astype(jnp.bfloat16), preferred_element_type=jnp.float32
     ).astype(jnp.bfloat16)
@@ -159,40 +201,31 @@
 
 
 def local(master, moment, second, gradient, step_count, old_weights, branch_rows, assignment):
-    steps_f = step_count[0].astype(jnp.float32)
-    first_fix = 1.0 - jnp.power(jnp.float32(0.9), steps_f)
-    second_fix = 1.0 - jnp.power(jnp.float32(0.95), steps_f)
-    new_moment = 0.9 * moment + 0.1 * gradient
-    new_second = 0.95 * second + 0.05 * gradient * gradient
-    update = new_moment / first_fix / (jnp.sqrt(new_second / second_fix) + 1e-08)
-    new_master = master - learn_rate * (update + decay_rate * master)
-
-    rows, width = new_master.shape
+    rows, width = master.shape
     chips = lax.axis_size(CHIPS)
-    fresh = new_master.astype(jnp.bfloat16)
-    spread = jnp.broadcast_to(fresh[None], (chips, rows, width))
+    new_master, new_moment, new_second, spread = updated(
+        step_count, master, moment, second, gradient, chips
+    )
     mine = lax.all_to_all(spread, CHIPS, split_axis=0, concat_axis=0, tiled=True)
+
     size = lax.axis_size("tp")
     me = lax.axis_index("tp")
     count = branch_rows.shape[0]
     part = old_weights.shape[1] // size
-    code = lambda n: jax.ShapeDtypeStruct((n + TAIL, part), jnp.int16)
+    code = lambda *n: jax.ShapeDtypeStruct(n[:-1] + (n[-1] + TAIL, part), jnp.int16)
     full = jax.ShapeDtypeStruct((count, part), jnp.float32)
-    ids = lax.rem(me + jnp.array([3, 5, 4], jnp.int32), size)
-    q3, q5, q4a, q4b = products(
-        far_kernel, branch_rows, old_weights, ids, 3, part,
-        [code(count), code(count), code(count // 2), code(count // 2)],
-    )
-    r3, r5 = along_tp(q3, 1), along_tp(q5, -1)
-    r4a, r4b = along_tp(q4a, 2), along_tp(q4b, -2)
-    ids = lax.rem(me + jnp.array([1, 7, 2, 6, 0], jnp.int32), size)
-    q1, q7, p2, p6, p0 = products(
-        near_kernel, branch_rows, old_weights, ids, 5, part,
-        [code(count), code(count), full, full, full],
-    )
-    r1, r7 = along_tp(q1, 1), along_tp(q7, -1)
-    q2, q6 = local_call(merge_kernel, [code(count), code(count)], p2, r3, r4a, p6, r5, r4b)
+    ids = lax.rem(me + jnp.array([3, 1, 5, 7, 4, 0, 2, 6], jnp.int32), size)
+    up, down, far_up, far_down, p2, p6, p0 = products(
+        branch_rows, old_weights, ids,
+        [code(2, count), code(2, count), code(count // 2), code(count // 2), full, full, full],
+    )
+    up, down = along_tp(up, 1), along_tp(down, -1)
+    far_up, far_down = along_tp(far_up, 2), along_tp(far_down, -2)
+    q2, q6 = local_call(
+        merge_kernel, [code(count), code(count)], p2, up, far_up, p6, down, far_down
+    )
     r2, r6 = along_tp(q2, 2), along_tp(q6, -2)
+    r2, mine = lax.optimization_barrier((r2, mine))
     replicas = lax.axis_size(PLANE)
     slots_each = 2 * count // replicas
     places = replicas * slots_each
@@ -200,9 +233,8 @@
         selector_kernel, jax.ShapeDtypeStruct((places, count), jnp.bfloat16), assignment.reshape(1, count)
     )
     placed = local_call(
-        final_kernel, jax.ShapeDtypeStruct((places, part), jnp.bfloat16), p0, r1, r7, r2, r6, selector
-    )
-    placed, mine = lax.optimization_barrier((placed, mine))
+        final_kernel, jax.ShapeDtypeStruct((places, part), jnp.bfloat16), p0, up, down, r2, r6, selector
+    )
     placed = placed.reshape(replicas, slots_each, part)
     arrived = lax.all_to_all(placed, PLANE, split_axis=0, concat_axis=0, tiled=True)
     branch_keys = arrived.reshape(1, replicas, slots_each, part)

time: 69.8 us -> 80.9 us (1.16)
  waiting for transfers between devices: 11.6 us -> 24.1 us
  Pallas kernels: 14.3 us -> 20.5 us
  local copies, waits for them, and re-layouts: 6.08 us -> 2.61 us
  starting transfers between devices: 33.7 us -> 31.4 us
  other arithmetic: 2.19 us -> 0.6 us
    ppermute x8 -> x6, waiting for transfers between devices: 4.42 us -> 16.9 us  [along_tp(): lax.ppermute(value, 'tp', [(i, (i + step) % size) for i in range(size)])]
    pallas_call x2, Pallas kernels: 6.47 us -> 12.6 us  [the longest x1 9.66 us: products(): pl.pallas_call(products_kernel, out_shape=outs, in_specs=[pl.BlockSpec(me...]
    convert_element_type x1 -> x0, other arithmetic: 2.18 us -> none  [local(): fresh = new_master.astype(jnp.bfloat16)]
    unnamed x15 -> x11, local copies, waits for them, and re-layouts: 4.5 us -> 2.61 us
    broadcast_in_dim x1 -> x0, local copies, waits for them, and re-layouts: 1.58 us -> none  [local(): spread = jnp.broadcast_to(fresh[None], (chips, rows, width))]
    ppermute x8 -> x6, starting transfers between devices: 15.2 us -> 14 us  [along_tp(): lax.ppermute(value, 'tp', [(i, (i + step) % size) for i in range(size)])]
  transfers between devices with their start and end apart: 11 -> 9, of which waited for: 2 -> 4; matrix products, arithmetic and copies ran while one was open for 0% -> 1% of each run, Pallas kernels for 15% -> 17%
where the time goes in v5:
time: 80.9 us; the launch traced here: 80.5 us
  starting transfers between devices  31.4 us (39%)
  waiting for transfers between devices  24.1 us (30%)
  Pallas kernels  20.5 us (25%)
  local copies, waits for them, and re-layouts  2.61 us (3%)
  between operations  1.37 us (2%)
    ppermute x6, waiting for transfers between devices, along_tp(): lax.ppermute(value, 'tp', [(i, (i + step) % size) for i in range(size)])  16.9 us
    ppermute x6, starting transfers between devices, along_tp(): lax.ppermute(value, 'tp', [(i, (i + step) % size) for i in range(size)])  14 us
    pallas_call x1, Pallas kernels, products(): pl.pallas_call(products_kernel, out_shape=outs, in_specs=[pl.BlockSpec(me...  9.66 us
    all_to_all x1, starting transfers between devices, local(): lax.all_to_all(spread, CHIPS, split_axis=0, concat_axis=0, tiled=True)  7.72 us
    all_to_all x1, waiting for transfers between devices, local(): lax.all_to_all(placed, PLANE, split_axis=0, concat_axis=0, tiled=True)  7.19 us
    all_to_all x1, starting transfers between devices, local(): lax.all_to_all(placed, PLANE, split_axis=0, concat_axis=0, tiled=True)  7.12 us
    pallas_call x2, Pallas kernels, set_half(): pl.pallas_call(half_kernel, out_shape=jax.ShapeDtypeStruct((lanes, 2, row...  5.64 us
    pallas_call x1, Pallas kernels, updated(): pl.pallas_call(update_kernel, out_shape=[same, same, same, jax.ShapeDtype...  2.95 us
  transfers between devices with their start and end apart: 9, of which 4 were waited for; matrix products, arithmetic and copies ran while one was open for 1% of the time, Pallas kernels for 17%

profile of v5, /device:TPU:1, one launch (start us, length us, event | category | flops | bytes accessed | tf_op | source)
XLA Modules:
  0.0 80.5 jit_solution(13872905442712862221)
XLA Ops:
  1.3 2.9 %shard_map.128 = (f32[64,1024]{1,0:T(8,128)}, f32[64,1024]{1,0:T(8,128)}, f32[64,1024]{1,0:T(8,128)}, bf16[16,64,1024]{2,1,0:T(8,128)(2,1)}) custom-call(s32[1]{0:T(128)S(6)} %copy.17.step_ref, f32[64,1024]{1,0:T(8,128)} %master.1, f32[64,1024]{1,0:T(8,128)} %moment.1, f32[64,1024]{1,0:T(8,128)} %second.1, f32[64,1024]{1,0:T(8,128)} %gradient.1), custom_call_target="tpu_custom_call" | custom-call | flops 1966080 | bytes 1835008 | tf_op jit(solution)/shard_map/pallas_call | solution.py:120
  4.2 0.0 copy-start.4
  4.2 7.7 %all-to-all-start = ((bf16[16,64,1024]{2,1,0:T(8,128)(2,1)}), bf16[16,64,1024]{2,1,0:T(8,128)(2,1)S(1)}, u32[]{:S(2)}, u32[]{:S(2)}) async-start(bf16[16,64,1024]{2,1,0:T(8,128)(2,1)} %get-tuple-element.30), calls=%async_computation | async-start | bytes 4194304 | tf_op jit(solution)/shard_map/all_to_all | solution.py:209
  12.0 0.0 copy-done.4
  12.0 0.6 compare_select_fusion.ids
  12.6 0.0 copy-start.3
  12.6 9.7 %shard_map.129 = (s16[2,528,128]{2,1,0:T(8,128)(2,1)}, s16[2,528,128]{2,1,0:T(8,128)(2,1)}, s16[272,128]{1,0:T(8,128)(2,1)}, s16[272,128]{1,0:T(8,128)(2,1)}, f3...) custom-call(s32[8]{0:T(128)} %compare_select_fusion.ids, bf16[512,2048]{1,0:T(8,128)(2,1)} %x_hbm.1, ...), custom_call_target="tpu_custom_call" | custom-call | flops 2147483648 | bytes 6291456 | tf_op jit(solution)/shard_map/pallas_call | solution.py:79
  22.2 0.0 copy-start
  22.2 1.7 %collective-permute-start = (s16[2,528,128]{2,1,0:T(8,128)(2,1)}, s16[2,528,128]{2,1,0:T(8,128)(2,1)S(1)}, u32[]{:S(2)}, u32[]{:S(2)}) collective-permute-start(s16[2,528,128]{2,1,0:T(8,128)(2,1)} %get-tuple-element.24), channel_id=1, source_target_pairs={{0,1},{1,2},{2,3},{3,4},{4,5},{5,6},{6,7},{7,0},{8,9},{9,10},{10,1... | collective-permute-start | bytes 811016 | tf_op jit(solution)/shard_map/ppermute | solution.py:200
  24.0 4.0 %collective-permute-start.2 = (s16[2,528,128]{2,1,0:T(8,128)(2,1)}, s16[2,528,128]{2,1,0:T(8,128)(2,1)S(1)}, u32[]{:S(2)}, u32[]{:S(2)}) collective-permute-start(s16[2,528,128]{2,1,0:T(8,128)(2,1)} %get-tuple-element.27), channel_id=1, source_target_pairs={{0,7},{1,0},{2,1},{3,2},{4,3},{5,4},{6,5},{7,6},{8,15},{9,8},{10,9... | collective-permute-start | bytes 811016 | tf_op jit(solution)/shard_map/ppermute | solution.py:200
  28.0 0.0 collective-permute-start.1
  28.0 3.6 %collective-permute-start.3 = (s16[272,128]{1,0:T(8,128)(2,1)}, s16[272,128]{1,0:T(8,128)(2,1)S(1)}, u32[]{:S(2)}, u32[]{:S(2)}) collective-permute-start(s16[272,128]{1,0:T(8,128)(2,1)} %get-tuple-element.28), channel_id=1, source_target_pairs={{0,6},{1,7},{2,0},{3,1},{4,2},{5,3},{6,4},{7,5},{8,14},{9,15},{10,... | collective-permute-start | bytes 208904 | tf_op jit(solution)/shard_map/ppermute | solution.py:200
  31.6 5.0 %collective-permute-done.1.far_a = s16[272,128]{1,0:T(8,128)(2,1)S(1)} collective-permute-done((s16[272,128]{1,0:T(8,128)(2,1)}, s16[272,128]{1,0:T(8,128)(2,1)S(1)}, u32[]{:S(2)}, u32[]{:S(2)}) %collective-permute-start.1) | collective-permute-done | bytes 69664 | tf_op jit(solution)/shard_map/ppermute | solution.py:200
  36.5 0.0 collective-permute-done.3.far_b
  36.6 0.0 collective-permute-done.next_a.ra
  36.6 0.0 collective-permute-done.2.next_b.rb
  36.6 0.0 copy-start.1
  36.6 0.9 %copy-done.1 = f32[512,128]{1,0:T(8,128)S(1)} copy-done((f32[512,128]{1,0:T(8,128)S(1)}, f32[512,128]{1,0:T(8,128)}, u32[]{:S(2)}) %copy-start.1) | copy-done | bytes 262168
  37.5 0.0 copy-start.2
  37.5 0.9 %copy-done.2 = f32[512,128]{1,0:T(8,128)S(1)} copy-done((f32[512,128]{1,0:T(8,128)S(1)}, f32[512,128]{1,0:T(8,128)}, u32[]{:S(2)}) %copy-start.2) | copy-done | bytes 262168
  38.5 0.3 shard_map.130
  38.8 3.1 %collective-permute-start.4 = (s16[528,128]{1,0:T(8,128)(2,1)S(1)}, s16[528,128]{1,0:T(8,128)(2,1)S(1)}, u32[]{:S(2)}, u32[]{:S(2)}) collective-permute-start(s16[528,128]{1,0:T(8,128)(2,1)S(1)} %get-tuple-element.29), channel_id=1, source_target_pairs={{0,2},{1,3},{2,4},{3,5},{4,6},{5,7},{6,0},{7,1},{8,10},{9,11},{10,... | collective-permute-start | bytes 405512 | tf_op jit(solution)/shard_map/ppermute | solution.py:200
  41.9 5.1 %collective-permute-done.4.rc = s16[528,128]{1,0:T(8,128)(2,1)S(1)} collective-permute-done((s16[528,128]{1,0:T(8,128)(2,1)S(1)}, s16[528,128]{1,0:T(8,128)(2,1)S(1)}, u32[]{:S(2)}, u32[]{:S(2)}) %collective-permute-start.4) | collective-permute-done | bytes 135200 | tf_op jit(solution)/shard_map/ppermute | solution.py:200
  47.0 0.0 all-to-all-done
  47.0 2.7 %collective-permute-start.5 = (bf16[16,64,1024]{2,1,0:T(8,128)(2,1)S(1)}, bf16[16,64,1024]{2,1,0:T(8,128)(2,1)}, u32[]{:S(2)}, u32[]{:S(2)}) collective-permute-start(bf16[16,64,1024]{2,1,0:T(8,128)(2,1)S(1)} %all-to-all-done), channel_id=1, source_target_pairs={{0,64},{64,0},{1,65},{65,1},{2,66},{66,2},{3,67},{67,3},{4,68},{68... | collective-permute-start | bytes 6291464 | tf_op jit(solution)/shard_map/ppermute | solution.py:241
  49.6 1.5 %collective-permute-start.6 = (s16[528,128]{1,0:T(8,128)(2,1)S(1)}, s16[528,128]{1,0:T(8,128)(2,1)S(1)}, u32[]{:S(2)}, u32[]{:S(2)}) collective-permute-start(s16[528,128]{1,0:T(8,128)(2,1)S(1)} %get-tuple-element.34), channel_id=1, source_target_pairs={{0,6},{1,7},{2,0},{3,1},{4,2},{5,3},{6,4},{7,5},{8,14},{9,15},{10,... | collective-permute-start | bytes 405512 | tf_op jit(solution)/shard_map/ppermute | solution.py:200
  51.1 0.0 copy-done.3
  51.1 0.6 shard_map.133.selector
  51.8 6.8 %collective-permute-done.6.rd = s16[528,128]{1,0:T(8,128)(2,1)S(1)} collective-permute-done((s16[528,128]{1,0:T(8,128)(2,1)S(1)}, s16[528,128]{1,0:T(8,128)(2,1)S(1)}, u32[]{:S(2)}, u32[]{:S(2)}) %collective-permute-start.6) | collective-permute-done | bytes 135200 | tf_op jit(solution)/shard_map/ppermute | solution.py:200
  58.6 0.0 copy-done
  58.6 1.3 %shard_map.134 = bf16[1024,128]{1,0:T(8,128)(2,1)} custom-call(f32[512,128]{1,0:T(8,128)S(1)} %copy-done, s16[2,528,128]{2,1,0:T(8,128)(2,1)S(1)} %collective-permute-done.next_a.ra, s16[2,528,128]{2,1,0:T(8,128)(2,1)S(1)} %collective-permute-done.2.next_b.rb, s16[528,128]{1,0:T(8,128)(2,1)S(1)} %collective-permute-done.4.rc, ...), custom_call_target="tpu_custom_call" | custom-call | bytes 1048576 | tf_op jit(solution)/shard_map/pallas_call | solution.py:133
  59.9 7.1 %all-to-all-start.1 = ((bf16[32,32,128]{2,1,0:T(8,128)(2,1)}), bf16[32,32,128]{2,1,0:T(8,128)(2,1)S(1)}, u32[]{:S(2)}, u32[]{:S(2)}) async-start(bf16[32,32,128]{2,1,0:T(8,128)(2,1)} %bitcast.5), calls=%async_computation.1 | async-start | bytes 524288 | tf_op jit(solution)/shard_map/all_to_all | solution.py:239
  67.0 1.9 %shard_map.131.refs_0_ = bf16[2,2,512,1024]{3,2,1,0:T(8,128)(2,1)} custom-call(s32[1]{0:T(128)} %bitcast.place, bf16[2,512,1024]{2,1,0:T(8,128)(2,1)S(1)} %bitcast.7), custom_call_target="tpu_custom_call" | custom-call | bytes 4194304 | tf_op jit(solution)/shard_map/pallas_call | solution.py:182
  68.9 7.2 %all-to-all-done.1 = bf16[32,32,128]{2,1,0:T(8,128)(2,1)S(1)} async-done(((bf16[32,32,128]{2,1,0:T(8,128)(2,1)}), bf16[32,32,128]{2,1,0:T(8,128)(2,1)S(1)}, u32[]{:S(2)}, u32[]{:S(2)}) %all-to-all-start.1) | async-done | bytes 262176 | tf_op jit(solution)/shard_map/all_to_all | solution.py:239
  76.1 0.0 collective-permute-done.5
  76.1 3.8 %shard_map.132 = bf16[2,2,512,1024]{3,2,1,0:T(8,128)(2,1)} custom-call(s32[1]{0:T(128)S(6)} %sub.3.place, bf16[2,512,1024]{2,1,0:T(8,128)(2,1)} %bitcast.1.half, bf16[2,2,512,1024]{3,2,1,0:T(8,128)(2,1)} %shard_map.131.refs_0_), custom_call_target="tpu_custom_call", output_to_operand_aliasing={{}: (2, {})} | custom-call | bytes 4194304 | tf_op jit(solution)/shard_map/pallas_call | solution.py:182
  79.8 0.7 copy.18
Async XLA Ops:
  4.2 7.7 %copy-start.4 = (s32[8]{0:T(128)S(1)}, s32[8]{0:T(128)}, u32[]{:S(2)}) copy-start(s32[8]{0:T(128)} %constant.19.clone) | copy-start | bytes 100
  4.2 42.7 %all-to-all-start = ((bf16[16,64,1024]{2,1,0:T(8,128)(2,1)}), bf16[16,64,1024]{2,1,0:T(8,128)(2,1)S(1)}, u32[]{:S(2)}, u32[]{:S(2)}) async-start(bf16[16,64,1024]{2,1,0:T(8,128)(2,1)} %get-tuple-element.30), calls=%async_computation | async-start | bytes 4194304 | tf_op jit(solution)/shard_map/all_to_all | solution.py:209
  12.6 38.6 %copy-start.3 = (s32[512,1]{0,1:T(1,128)S(1)}, s32[512,1]{0,1:T(1,128)}, u32[]{:S(2)}) copy-start(s32[512,1]{0,1:T(1,128)} %param.16) | copy-start | bytes 6148
  22.2 36.3 %copy-start = (f32[512,128]{1,0:T(8,128)S(1)}, f32[512,128]{1,0:T(8,128)}, u32[]{:S(2)}) copy-start(f32[512,128]{1,0:T(8,128)} %get-tuple-element.32.own) | copy-start | bytes 786436
  22.2 14.3 %collective-permute-start = (s16[2,528,128]{2,1,0:T(8,128)(2,1)}, s16[2,528,128]{2,1,0:T(8,128)(2,1)S(1)}, u32[]{:S(2)}, u32[]{:S(2)}) collective-permute-start(s16[2,528,128]{2,1,0:T(8,128)(2,1)} %get-tuple-element.24), channel_id=1, source_target_pairs={{0,1},{1,2},{2,3},{3,4},{4,5},{5,6},{6,7},{7,0},{8,9},{9,10},{10,1... | collective-permute-start | bytes 811016 | tf_op jit(solution)/shard_map/ppermute | solution.py:200
  24.0 12.6 %collective-permute-start.2 = (s16[2,528,128]{2,1,0:T(8,128)(2,1)}, s16[2,528,128]{2,1,0:T(8,128)(2,1)S(1)}, u32[]{:S(2)}, u32[]{:S(2)}) collective-permute-start(s16[2,528,128]{2,1,0:T(8,128)(2,1)} %get-tuple-element.27), channel_id=1, source_target_pairs={{0,7},{1,0},{2,1},{3,2},{4,3},{5,4},{6,5},{7,6},{8,15},{9,8},{10,9... | collective-permute-start | bytes 811016 | tf_op jit(solution)/shard_map/ppermute | solution.py:200
  28.0 8.6 %collective-permute-start.1 = (s16[272,128]{1,0:T(8,128)(2,1)}, s16[272,128]{1,0:T(8,128)(2,1)S(1)}, u32[]{:S(2)}, u32[]{:S(2)}) collective-permute-start(s16[272,128]{1,0:T(8,128)(2,1)} %get-tuple-element.25), channel_id=1, source_target_pairs={{0,2},{1,3},{2,4},{3,5},{4,6},{5,7},{6,0},{7,1},{8,10},{9,11},{10,... | collective-permute-start | bytes 208904 | tf_op jit(solution)/shard_map/ppermute | solution.py:200
  28.0 8.6 %collective-permute-start.3 = (s16[272,128]{1,0:T(8,128)(2,1)}, s16[272,128]{1,0:T(8,128)(2,1)S(1)}, u32[]{:S(2)}, u32[]{:S(2)}) collective-permute-start(s16[272,128]{1,0:T(8,128)(2,1)} %get-tuple-element.28), channel_id=1, source_target_pairs={{0,6},{1,7},{2,0},{3,1},{4,2},{5,3},{6,4},{7,5},{8,14},{9,15},{10,... | collective-permute-start | bytes 208904 | tf_op jit(solution)/shard_map/ppermute | solution.py:200
  36.6 1.0 %copy-start.1 = (f32[512,128]{1,0:T(8,128)S(1)}, f32[512,128]{1,0:T(8,128)}, u32[]{:S(2)}) copy-start(f32[512,128]{1,0:T(8,128)} %get-tuple-element.23.own_a) | copy-start | bytes 786436
  37.5 0.9 %copy-start.2 = (f32[512,128]{1,0:T(8,128)S(1)}, f32[512,128]{1,0:T(8,128)}, u32[]{:S(2)}) copy-start(f32[512,128]{1,0:T(8,128)} %get-tuple-element.26.own_b) | copy-start | bytes 786436
  38.8 8.2 %collective-permute-start.4 = (s16[528,128]{1,0:T(8,128)(2,1)S(1)}, s16[528,128]{1,0:T(8,128)(2,1)S(1)}, u32[]{:S(2)}, u32[]{:S(2)}) collective-permute-start(s16[528,128]{1,0:T(8,128)(2,1)S(1)} %get-tuple-element.29), channel_id=1, source_target_pairs={{0,2},{1,3},{2,4},{3,5},{4,6},{5,7},{6,0},{7,1},{8,10},{9,11},{10,... | collective-permute-start | bytes 405512 | tf_op jit(solution)/shard_map/ppermute | solution.py:200
  47.0 29.1 %collective-permute-start.5 = (bf16[16,64,1024]{2,1,0:T(8,128)(2,1)S(1)}, bf16[16,64,1024]{2,1,0:T(8,128)(2,1)}, u32[]{:S(2)}, u32[]{:S(2)}) collective-permute-start(bf16[16,64,1024]{2,1,0:T(8,128)(2,1)S(1)} %all-to-all-done), channel_id=1, source_target_pairs={{0,64},{64,0},{1,65},{65,1},{2,66},{66,2},{3,67},{67,3},{4,68},{68... | collective-permute-start | bytes 6291464 | tf_op jit(solution)/shard_map/ppermute | solution.py:241
  49.6 9.0 %collective-permute-start.6 = (s16[528,128]{1,0:T(8,128)(2,1)S(1)}, s16[528,128]{1,0:T(8,128)(2,1)S(1)}, u32[]{:S(2)}, u32[]{:S(2)}) collective-permute-start(s16[528,128]{1,0:T(8,128)(2,1)S(1)} %get-tuple-element.34), channel_id=1, source_target_pairs={{0,6},{1,7},{2,0},{3,1},{4,2},{5,3},{6,4},{7,5},{8,14},{9,15},{10,... | collective-permute-start | bytes 405512 | tf_op jit(solution)/shard_map/ppermute | solution.py:200
  59.9 16.2 %all-to-all-start.1 = ((bf16[32,32,128]{2,1,0:T(8,128)(2,1)}), bf16[32,32,128]{2,1,0:T(8,128)(2,1)S(1)}, u32[]{:S(2)}, u32[]{:S(2)}) async-start(bf16[32,32,128]{2,1,0:T(8,128)(2,1)} %bitcast.5), calls=%async_computation.1 | async-start | bytes 524288 | tf_op jit(solution)/shard_map/all_to_all | solution.py:239

commit v6 on v4

--- a/solution.py
+++ b/solution.py
@@ -45,20 +45,121 @@
     return jnp.dot(rows_ref[...], columns_ref[...], preferred_element_type=jnp.float32)
 
 
-def far_kernel(ids, x, wa, wb, wc, qa, qb, qc, qd):
+def pair_product(rows_ref, first_ref, second_ref):
+    part = first_ref.shape[1]
+    columns = jnp.concatenate([first_ref[...], second_ref[...]], axis=1)
+    both = jnp.dot(rows_ref[...], columns, preferred_element_type=jnp.float32)
+    return both[:, :part], both[:, part:]
+
+
+def head_kernel(
+    step_ref, ids, master_h, moment_h, second_h, gradient_h, x_h, w_h,
+    new_master_h, new_moment_h, new_second_h, spread_h, up_h, down_h, far_up_h, far_down_h,
+    master, moment, second, gradient, new_master, new_moment, new_second, fresh,
+    x, wa, wb, wc, up, down, far_up, far_down, sems, out_sems, spread_sems,
+):
+    part = wa.shape[1]
     half = x.shape[0] // 2
-    put_coded(qa, product(x, wa))
-    put_coded(qb, product(x, wb))
+    columns = [w_h.at[:, pl.ds(pl.multiple_of(ids[k] * part, part), part)] for k in range(3)]
+    sources = [master_h, moment_h, second_h, gradient_h, x_h] + columns
+    places = [master, moment, second, gradient, x, wa, wb, wc]
+    loads = [
+        pltpu.make_async_copy(source, place, sems.at[k])
+        for k, (source, place) in enumerate(zip(sources, places))
+    ]
+    for load in loads:
+        load.start()
+
+    def times(k, fixes):
+        return fixes[0] * 0.9, fixes[1] * 0.95
+
+    one = jnp.float32(1.0)
+    first, other = lax.fori_loop(0, step_ref[0], times, (one, one))
+    for load in loads[:4]:
+        load.wait()
+    ones = jnp.ones((1, master.shape[1]), jnp.float32)
+    first_fix, second_fix = ones * (1.0 - first), ones * (1.0 - other)
+    g, old = gradient[...], master[...]
+    m = 0.9 * moment[...] + 0.1 * g
+    v = 0.95 * second[...] + 0.05 * g * g
+    update = m / first_fix / (jnp.sqrt(v / second_fix) + 1e-08)
+    new = old - learn_rate * (update + decay_rate * old)
+    new_moment[...] = m
+    new_second[...] = v
+    new_master[...] = new
+    fresh[...] = new.astype(jnp.bfloat16)
+    stores = [
+        pltpu.make_async_copy(fresh, spread_h.at[k], spread_sems.at[k])
+        for k in range(spread_h.shape[0])
+    ]
+    finished = [(new_master, new_master_h), (new_moment, new_moment_h), (new_second, new_second_h)]
+    stores += [
+        pltpu.make_async_copy(source, place, out_sems.at[k])
+        for k, (source, place) in enumerate(finished)
+    ]
+    for store in stores:
+        store.start()
+
+    def send(k, source, place):
+        store = pltpu.make_async_copy(source, place, out_sems.at[3 + k])
+        store.start()
+        stores.append(store)
+
+    for load in loads[4:7]:
+        load.wait()
+    above, below = pair_product(x, wa, wb)
+    put_coded(up, above)
+    send(0, up, up_h)
+    put_coded(down, below)
+    send(1, down, down_h)
+    loads[7].wait()
     far = product(x, wc)
-    put_coded(qc, far[:half])
-    put_coded(qd, far[half:])
+    put_coded(far_up, far[:half])
+    send(2, far_up, far_up_h)
+    put_coded(far_down, far[half:])
+    send(3, far_down, far_down_h)
+    for store in stores:
+        store.wait()
+
+
+def head(step_count, ids, master, moment, second, gradient, x, w, chips):
+    rows, depth = x.shape
+    part = w.shape[1] // 8
+    anywhere = pl.BlockSpec(memory_space=pl.ANY)
+    scalar = pl.BlockSpec(memory_space=pltpu.SMEM)
+    shard = master.shape
+    codes = [(rows + TAIL, part)] * 2 + [(rows // 2 + TAIL, part)] * 2
+    outs = [jax.ShapeDtypeStruct(shard, jnp.float32)] * 3
+    outs += [jax.ShapeDtypeStruct((chips,) + shard, jnp.bfloat16)]
+    outs += [jax.ShapeDtypeStruct(c, jnp.int16) for c in codes]
+    return pl.pallas_call(
+        head_kernel,
+        out_shape=outs,
+        in_specs=[scalar] * 2 + [anywhere] * 6,
+        out_specs=[anywhere] * len(outs),
+        scratch_shapes=[pltpu.VMEM(shard, jnp.float32)] * 7
+        + [pltpu.VMEM(shard, jnp.bfloat16), pltpu.VMEM((rows, depth), x.dtype)]
+        + [pltpu.VMEM((depth, part), w.dtype)] * 3
+        + [pltpu.VMEM(c, jnp.int16) for c in codes]
+        + [
+            pltpu.SemaphoreType.DMA((8,)),
+            pltpu.SemaphoreType.DMA((7,)),
+            pltpu.SemaphoreType.DMA((chips,)),
+        ],
+        compiler_params=pltpu.CompilerParams(vmem_limit_bytes=60 * 2**20),
+        cost_estimate=pl.CostEstimate(
+            flops=6 * rows * depth * part + 30 * master.size,
+            bytes_accessed=2 * x.size + 6 * depth * part + 60 * master.size,
+            transcendentals=3 * master.size,
+        ),
+    )(step_count, ids, master, moment, second, gradient, x, w)
 
 
 def near_kernel(ids, x, wa, wb, wc, wd, we, qa, qb, pc, pd, pe):
-    put_coded(qa, product(x, wa))
-    put_coded(qb, product(x, wb))
-    pc[...] = product(x, wc)
-    pd[...] = product(x, wd)
+    above, below = pair_product(x, wa, wb)
+    put_coded(qa, above)
+    put_coded(qb, below)
+    pc[...], pd[...] = pair_product(x, wc, wd)
     pe[...] = product(x, we)
 
 
@@ -159,35 +260,23 @@
 
 
 def local(master, moment, second, gradient, step_count, old_weights, branch_rows, assignment):
-    steps_f = step_count[0].astype(jnp.float32)
-    first_fix = 1.0 - jnp.power(jnp.float32(0.9), steps_f)
-    second_fix = 1.0 - jnp.power(jnp.float32(0.95), steps_f)
-    new_moment = 0.9 * moment + 0.1 * gradient
-    new_second = 0.95 * second + 0.05 * gradient * gradient
-    update = new_moment / first_fix / (jnp.sqrt(new_second / second_fix) + 1e-08)
-    new_master = master - learn_rate * (update + decay_rate * master)
-
-    rows, width = new_master.shape
+    rows, width = master.shape
     chips = lax.axis_size(CHIPS)
-    fresh = new_master.astype(jnp.bfloat16)
-    spread = jnp.broadcast_to(fresh[None], (chips, rows, width))
-    mine = lax.all_to_all(spread, CHIPS, split_axis=0, concat_axis=0, tiled=True)
     size = lax.axis_size("tp")
     me = lax.axis_index("tp")
     count = branch_rows.shape[0]
     part = old_weights.shape[1] // size
     code = lambda n: jax.ShapeDtypeStruct((n + TAIL, part), jnp.int16)
     full = jax.ShapeDtypeStruct((count, part), jnp.float32)
-    ids = lax.rem(me + jnp.array([3, 5, 4], jnp.int32), size)
-    q3, q5, q4a, q4b = products(
-        far_kernel, branch_rows, old_weights, ids, 3, part,
-        [code(count), code(count), code(count // 2), code(count // 2)],
-    )
+    at = lambda *steps: jnp.stack([lax.rem(me + k, size) for k in steps]).astype(jnp.int32)
+    new_master, new_moment, new_second, spread, q3, q5, q4a, q4b = head(
+        step_count, at(3, 5, 4), master, moment, second, gradient, branch_rows, old_weights, chips
+    )
+    mine = lax.all_to_all(spread, CHIPS, split_axis=0, concat_axis=0, tiled=True)
     r3, r5 = along_tp(q3, 1), along_tp(q5, -1)
     r4a, r4b = along_tp(q4a, 2), along_tp(q4b, -2)
-    ids = lax.rem(me + jnp.array([1, 7, 2, 6, 0], jnp.int32), size)
     q1, q7, p2, p6, p0 = products(
-        near_kernel, branch_rows, old_weights, ids, 5, part,
+        near_kernel, branch_rows, old_weights, at(1, 7, 2, 6, 0), 5, part,
         [code(count), code(count), full, full, full],
     )
     r1, r7 = along_tp(q1, 1), along_tp(q7, -1)
@@ -202,10 +291,9 @@
     placed = local_call(
         final_kernel, jax.ShapeDtypeStruct((places, part), jnp.bfloat16), p0, r1, r7, r2, r6, selector
     )
-    placed, mine = lax.optimization_barrier((placed, mine))
+    mine, _ = lax.optimization_barrier((mine, placed))
     placed = placed.reshape(replicas, slots_each, part)
     arrived = lax.all_to_all(placed, PLANE, split_axis=0, concat_axis=0, tiled=True)
-    branch_keys = arrived.reshape(1, replicas, slots_each, part)
     other = lax.ppermute(mine, "core", [(0, 1), (1, 0)])
     core = jnp.reshape(lax.axis_index("core"), (1,)).astype(jnp.int32)
     lanes = lax.axis_size("xlo")
@@ -213,6 +301,8 @@
     other = other.reshape(lanes, -1, width)
     pair = set_half(core, mine)
     pair = set_half(1 - core, other, pair)
+    pair, arrived = lax.optimization_barrier((pair, arrived))
+    branch_keys = arrived.reshape(1, replicas, slots_each, part)
     rollout_weights = pair.reshape(2 * chips * rows, width)
     return (new_master, new_moment, new_second, rollout_weights, branch_keys)
 

time: 69.8 us -> 65.6 us (0.940)
  Pallas kernels: 14.3 us -> 17 us
  waiting for transfers between devices: 11.6 us -> 9.72 us
  starting transfers between devices: 33.7 us -> 31.9 us
  other arithmetic: 2.19 us -> 0.61 us
  local copies, waits for them, and re-layouts: 6.08 us -> 4.59 us
    pallas_call x0 -> x1, Pallas kernels: none -> 6.39 us  [head(): pl.pallas_call(head_kernel, out_shape=outs, in_specs=[scalar] * 2 + [anyw...]
    all_to_all x1, waiting for transfers between devices: 7.19 us -> 3.41 us  [local(): lax.all_to_all(placed, PLANE, split_axis=0, concat_axis=0, tiled=True)]
    pallas_call x2 -> x1, Pallas kernels: 6.47 us -> 2.79 us  [products(): pl.pallas_call(kernel, out_shape=outs, grid_spec=pltpu.PrefetchScalarGrid...]
    convert_element_type x1 -> x0, other arithmetic: 2.18 us -> none  [local(): fresh = new_master.astype(jnp.bfloat16)]
    broadcast_in_dim x1 -> x0, local copies, waits for them, and re-layouts: 1.58 us -> none  [local(): spread = jnp.broadcast_to(fresh[None], (chips, rows, width))]
    all_to_all x1, waiting for transfers between devices: 0.01 us -> 1.55 us  [local(): lax.all_to_all(spread, CHIPS, split_axis=0, concat_axis=0, tiled=True)]
    ppermute x1, starting transfers between devices: 3.34 us -> 2.17 us  [local(): other = lax.ppermute(mine, 'core', [(0, 1), (1, 0)])]
    all_to_all x1, starting transfers between devices: 7.38 us -> 6.25 us  [local(): lax.all_to_all(placed, PLANE, split_axis=0, concat_axis=0, tiled=True)]
  transfers between devices with their start and end apart: 11 -> 11, of which waited for: 2 -> 3; matrix products, arithmetic and copies ran while one was open for 0% -> 0% of each run, Pallas kernels for 15% -> 16%
where the time goes in v6:
time: 65.6 us; the launch traced here: 65.2 us
  starting transfers between devices  31.9 us (49%)
  Pallas kernels  17 us (26%)
  waiting for transfers between devices  9.72 us (15%)
  local copies, waits for them, and re-layouts  4.59 us (7%)
  between operations  1.43 us (2%)
    ppermute x8, starting transfers between devices, along_tp(): lax.ppermute(value, 'tp', [(i, (i + step) % size) for i in range(size)])  15.7 us
    all_to_all x1, starting transfers between devices, local(): lax.all_to_all(spread, CHIPS, split_axis=0, concat_axis=0, tiled=True)  7.73 us
    pallas_call x1, Pallas kernels, head(): pl.pallas_call(head_kernel, out_shape=outs, in_specs=[scalar] * 2 + [anyw...  6.39 us
    all_to_all x1, starting transfers between devices, local(): lax.all_to_all(placed, PLANE, split_axis=0, concat_axis=0, tiled=True)  6.25 us
    pallas_call x2, Pallas kernels, set_half(): pl.pallas_call(half_kernel, out_shape=jax.ShapeDtypeStruct((lanes, 2, row...  5.64 us
    ppermute x8, waiting for transfers between devices, along_tp(): lax.ppermute(value, 'tp', [(i, (i + step) % size) for i in range(size)])  4.76 us
    unnamed x15, local copies, waits for them, and re-layouts  4.5 us
    all_to_all x1, waiting for transfers between devices, local(): lax.all_to_all(placed, PLANE, split_axis=0, concat_axis=0, tiled=True)  3.41 us
  transfers between devices with their start and end apart: 11, of which 3 were waited for; matrix products, arithmetic and copies ran while one was open for 0% of the time, Pallas kernels for 16%

profile of v6, /device:TPU:1, one launch (start us, length us, event | category | flops | bytes accessed | tf_op | source)
XLA Modules:
  0.0 65.2 jit_solution(10997987183632400741)
XLA Ops:
  1.3 0.6 pad_add_fusion.ids
  1.9 6.4 %shard_map.119 = (f32[64,1024]{1,0:T(8,128)}, f32[64,1024]{1,0:T(8,128)}, f32[64,1024]{1,0:T(8,128)}, bf16[16,64,1024]{2,1,0:T(8,128)(2,1)}, s16[528,128]{1,0:T(...) custom-call(s32[1]{0:T(128)S(6)} %copy.16.step_ref, s32[3]{0:T(128)} %pad_add_fusion.ids, ...), custom_call_target="tpu_custom_call" | custom-call | flops 807272448 | bytes 7602176 | tf_op jit(solution)/shard_map/pallas_call | solution.py:135
  8.3 0.0 copy-start.4
  8.3 0.0 copy-start.3
  8.3 0.0 copy-start.6
  8.3 0.0 copy-start.5
  8.3 7.7 %all-to-all-start = ((bf16[16,64,1024]{2,1,0:T(8,128)(2,1)}), bf16[16,64,1024]{2,1,0:T(8,128)(2,1)S(1)}, u32[]{:S(2)}, u32[]{:S(2)}) async-start(bf16[16,64,1024]{2,1,0:T(8,128)(2,1)} %get-tuple-element.26), calls=%async_computation | async-start | bytes 4194304 | tf_op jit(solution)/shard_map/all_to_all | solution.py:275
  16.1 0.0 copy-done.4
  16.1 1.7 %collective-permute-start.2 = (s16[528,128]{1,0:T(8,128)(2,1)S(1)}, s16[528,128]{1,0:T(8,128)(2,1)S(1)}, u32[]{:S(2)}, u32[]{:S(2)}) collective-permute-start(s16[528,128]{1,0:T(8,128)(2,1)S(1)} %copy-done.4), channel_id=1, source_target_pairs={{0,1},{1,2},{2,3},{3,4},{4,5},{5,6},{6,7},{7,0},{8,9},{9,10},{10,1... | collective-permute-start | bytes 405512 | tf_op jit(solution)/shard_map/ppermute | solution.py:259
  17.8 0.0 copy-done.3
  17.8 4.0 %collective-permute-start.4 = (s16[528,128]{1,0:T(8,128)(2,1)S(1)}, s16[528,128]{1,0:T(8,128)(2,1)S(1)}, u32[]{:S(2)}, u32[]{:S(2)}) collective-permute-start(s16[528,128]{1,0:T(8,128)(2,1)S(1)} %copy-done.3), channel_id=1, source_target_pairs={{0,7},{1,0},{2,1},{3,2},{4,3},{5,4},{6,5},{7,6},{8,15},{9,8},{10,9... | collective-permute-start | bytes 405512 | tf_op jit(solution)/shard_map/ppermute | solution.py:259
  21.8 0.0 copy-done.6
  21.8 0.0 collective-permute-start.3
  21.8 0.0 copy-done.5
  21.9 3.6 %collective-permute-start.5 = (s16[272,128]{1,0:T(8,128)(2,1)S(1)}, s16[272,128]{1,0:T(8,128)(2,1)S(1)}, u32[]{:S(2)}, u32[]{:S(2)}) collective-permute-start(s16[272,128]{1,0:T(8,128)(2,1)S(1)} %copy-done.5), channel_id=1, source_target_pairs={{0,6},{1,7},{2,0},{3,1},{4,2},{5,3},{6,4},{7,5},{8,14},{9,15},{10,... | collective-permute-start | bytes 208904 | tf_op jit(solution)/shard_map/ppermute | solution.py:259
  25.4 0.1 stack.39.ids
  25.5 0.0 copy-start
  25.5 2.2 %copy-done = bf16[2048,1024]{1,0:T(8,128)(2,1)S(1)} copy-done((bf16[2048,1024]{1,0:T(8,128)(2,1)S(1)}, bf16[2048,1024]{1,0:T(8,128)(2,1)}, u32[]{:S(2)}) %copy-start) | copy-done | bytes 4194328
  27.7 0.0 copy-start.1
  27.7 1.6 %copy-done.1 = bf16[512,2048]{1,0:T(8,128)(2,1)S(1)} copy-done((bf16[512,2048]{1,0:T(8,128)(2,1)S(1)}, bf16[512,2048]{1,0:T(8,128)(2,1)}, u32[]{:S(2)}) %copy-start.1) | copy-done | bytes 2097176
  29.3 0.0 copy-start.2
  29.3 2.8 %shard_map.120 = (s16[528,128]{1,0:T(8,128)(2,1)S(1)}, s16[528,128]{1,0:T(8,128)(2,1)S(1)}, f32[512,128]{1,0:T(8,128)S(1)}, f32[512,128]{1,0:T(8,128)S(1)}, f32[512,128]{1,0:T(8,128)S(1)}) custom-call(s32[5]{0:T(128)S(1)} %stack.39.ids, bf16[512,2048]{1,0:T(8,128)(2,1)S(1)} %copy-done.1, bf16[2048,1024]{1,0:T(8,128)(2,1)S(1)} %copy-done, ...), custom_call_target="tpu_custom_call" | custom-call | flops 1342177280 | bytes 4718592 | tf_op jit(solution)/shard_map/pallas_call | solution.py:173
  32.1 0.1 collective-permute-start
  32.2 0.0 collective-permute-done.3.far_a
  32.2 2.7 %collective-permute-start.1 = (s16[528,128]{1,0:T(8,128)(2,1)S(1)}, s16[528,128]{1,0:T(8,128)(2,1)S(1)}, u32[]{:S(2)}, u32[]{:S(2)}) collective-permute-start(s16[528,128]{1,0:T(8,128)(2,1)S(1)} %get-tuple-element.29), channel_id=1, source_target_pairs={{0,7},{1,0},{2,1},{3,2},{4,3},{5,4},{6,5},{7,6},{8,15},{9,8},{10,9... | collective-permute-start | bytes 405512 | tf_op jit(solution)/shard_map/ppermute | solution.py:259
  34.8 0.0 collective-permute-done.5.far_b
  34.8 0.0 collective-permute-done.2.next_a
  34.9 0.0 collective-permute-done.4.next_b
  34.9 0.3 shard_map.121
  35.1 0.1 collective-permute-start.6
  35.2 3.6 %collective-permute-start.7 = (s16[528,128]{1,0:T(8,128)(2,1)S(1)}, s16[528,128]{1,0:T(8,128)(2,1)S(1)}, u32[]{:S(2)}, u32[]{:S(2)}) collective-permute-start(s16[528,128]{1,0:T(8,128)(2,1)S(1)} %get-tuple-element.37), channel_id=1, source_target_pairs={{0,6},{1,7},{2,0},{3,1},{4,2},{5,3},{6,4},{7,5},{8,14},{9,15},{10,... | collective-permute-start | bytes 405512 | tf_op jit(solution)/shard_map/ppermute | solution.py:259
  38.8 0.0 copy-done.2
  38.8 0.6 shard_map.122.selector
  39.5 0.0 collective-permute-done.ra
  39.5 0.0 collective-permute-done.1.rb
  39.5 4.7 %collective-permute-done.6.rc = s16[528,128]{1,0:T(8,128)(2,1)S(1)} collective-permute-done((s16[528,128]{1,0:T(8,128)(2,1)S(1)}, s16[528,128]{1,0:T(8,128)(2,1)S(1)}, u32[]{:S(2)}, u32[]{:S(2)}) %collective-permute-start.6) | collective-permute-done | bytes 135200 | tf_op jit(solution)/shard_map/ppermute | solution.py:259
  44.2 0.0 collective-permute-done.7.rd
  44.2 1.3 %shard_map.123 = bf16[1024,128]{1,0:T(8,128)(2,1)} custom-call(f32[512,128]{1,0:T(8,128)S(1)} %get-tuple-element.27.own, s16[528,128]{1,0:T(8,128)(2,1)S(1)} %collective-permute-done.ra, s16[528,128]{1,0:T(8,128)(2,1)S(1)} %collective-permute-done.1.rb, s16[528,128]{1,0:T(8,128)(2,1)S(1)} %collective-permute-done.6.rc, ...), custom_call_target="tpu_custom_call" | custom-call | bytes 1048576 | tf_op jit(solution)/shard_map/pallas_call | solution.py:192
  45.5 1.5 %all-to-all-done = bf16[16,64,1024]{2,1,0:T(8,128)(2,1)S(1)} async-done(((bf16[16,64,1024]{2,1,0:T(8,128)(2,1)}), bf16[16,64,1024]{2,1,0:T(8,128)(2,1)S(1)}, u32[]{:S(2)}, u32[]{:S(2)}) %all-to-all-start) | async-done | bytes 2097184 | tf_op jit(solution)/shard_map/all_to_all | solution.py:275
  47.1 2.2 %collective-permute-start.8 = (bf16[16,64,1024]{2,1,0:T(8,128)(2,1)S(1)}, bf16[16,64,1024]{2,1,0:T(8,128)(2,1)}, u32[]{:S(2)}, u32[]{:S(2)}) collective-permute-start(bf16[16,64,1024]{2,1,0:T(8,128)(2,1)S(1)} %all-to-all-done), channel_id=1, source_target_pairs={{0,64},{64,0},{1,65},{65,1},{2,66},{66,2},{3,67},{67,3},{4,68},{68... | collective-permute-start | bytes 6291464 | tf_op jit(solution)/shard_map/ppermute | solution.py:297
  49.2 6.3 %all-to-all-start.1 = ((bf16[32,32,128]{2,1,0:T(8,128)(2,1)}), bf16[32,32,128]{2,1,0:T(8,128)(2,1)S(1)}, u32[]{:S(2)}, u32[]{:S(2)}) async-start(bf16[32,32,128]{2,1,0:T(8,128)(2,1)} %bitcast.12), calls=%async_computation.1 | async-start | bytes 524288 | tf_op jit(solution)/shard_map/all_to_all | solution.py:296
  55.5 1.9 %shard_map.124.refs_0_ = bf16[2,2,512,1024]{3,2,1,0:T(8,128)(2,1)} custom-call(s32[1]{0:T(128)} %bitcast.3.place, bf16[2,512,1024]{2,1,0:T(8,128)(2,1)S(1)} %bitcast.15), custom_call_target="tpu_custom_call" | custom-call | bytes 4194304 | tf_op jit(solution)/shard_map/pallas_call | solution.py:241
  57.4 0.0 collective-permute-done.8
  57.4 3.8 %shard_map.125 = bf16[2,2,512,1024]{3,2,1,0:T(8,128)(2,1)} custom-call(s32[1]{0:T(128)S(6)} %sub.3.place, bf16[2,512,1024]{2,1,0:T(8,128)(2,1)} %bitcast.10.half, bf16[2,2,512,1024]{3,2,1,0:T(8,128)(2,1)} %shard_map.124.refs_0_), custom_call_target="tpu_custom_call", output_to_operand_aliasing={{}: (2, {})} | custom-call | bytes 4194304 | tf_op jit(solution)/shard_map/pallas_call | solution.py:241
  61.1 3.4 %all-to-all-done.1 = bf16[32,32,128]{2,1,0:T(8,128)(2,1)S(1)} async-done(((bf16[32,32,128]{2,1,0:T(8,128)(2,1)}), bf16[32,32,128]{2,1,0:T(8,128)(2,1)S(1)}, u32[]{:S(2)}, u32[]{:S(2)}) %all-to-all-start.1) | async-done | bytes 262176 | tf_op jit(solution)/shard_map/all_to_all | solution.py:296
  64.5 0.7 %copy.17 = bf16[1,32,32,128]{3,2,1,0:T(8,128)(2,1)} copy(bf16[1,32,32,128]{3,2,1,0:T(8,128)(2,1)S(1)} %bitcast.18) | data formatting | bytes 524288
Async XLA Ops:
  8.3 7.8 %copy-start.4 = (s16[528,128]{1,0:T(8,128)(2,1)S(1)}, s16[528,128]{1,0:T(8,128)(2,1)}, u32[]{:S(2)}) copy-start(s16[528,128]{1,0:T(8,128)(2,1)} %get-tuple-element.31) | copy-start | bytes 405508
  8.3 9.5 %copy-start.3 = (s16[528,128]{1,0:T(8,128)(2,1)S(1)}, s16[528,128]{1,0:T(8,128)(2,1)}, u32[]{:S(2)}) copy-start(s16[528,128]{1,0:T(8,128)(2,1)} %get-tuple-element.34) | copy-start | bytes 405508
  8.3 13.5 %copy-start.6 = (s16[272,128]{1,0:T(8,128)(2,1)S(1)}, s16[272,128]{1,0:T(8,128)(2,1)}, u32[]{:S(2)}) copy-start(s16[272,128]{1,0:T(8,128)(2,1)} %get-tuple-element.32) | copy-start | bytes 208900
  8.3 13.5 %copy-start.5 = (s16[272,128]{1,0:T(8,128)(2,1)S(1)}, s16[272,128]{1,0:T(8,128)(2,1)}, u32[]{:S(2)}) copy-start(s16[272,128]{1,0:T(8,128)(2,1)} %get-tuple-element.35) | copy-start | bytes 208900
  8.3 38.7 %all-to-all-start = ((bf16[16,64,1024]{2,1,0:T(8,128)(2,1)}), bf16[16,64,1024]{2,1,0:T(8,128)(2,1)S(1)}, u32[]{:S(2)}, u32[]{:S(2)}) async-start(bf16[16,64,1024]{2,1,0:T(8,128)(2,1)} %get-tuple-element.26), calls=%async_computation | async-start | bytes 4194304 | tf_op jit(solution)/shard_map/all_to_all | solution.py:275
  16.1 18.8 %collective-permute-start.2 = (s16[528,128]{1,0:T(8,128)(2,1)S(1)}, s16[528,128]{1,0:T(8,128)(2,1)S(1)}, u32[]{:S(2)}, u32[]{:S(2)}) collective-permute-start(s16[528,128]{1,0:T(8,128)(2,1)S(1)} %copy-done.4), channel_id=1, source_target_pairs={{0,1},{1,2},{2,3},{3,4},{4,5},{5,6},{6,7},{7,0},{8,9},{9,10},{10,1... | collective-permute-start | bytes 405512 | tf_op jit(solution)/shard_map/ppermute | solution.py:259
  17.8 17.0 %collective-permute-start.4 = (s16[528,128]{1,0:T(8,128)(2,1)S(1)}, s16[528,128]{1,0:T(8,128)(2,1)S(1)}, u32[]{:S(2)}, u32[]{:S(2)}) collective-permute-start(s16[528,128]{1,0:T(8,128)(2,1)S(1)} %copy-done.3), channel_id=1, source_target_pairs={{0,7},{1,0},{2,1},{3,2},{4,3},{5,4},{6,5},{7,6},{8,15},{9,8},{10,9... | collective-permute-start | bytes 405512 | tf_op jit(solution)/shard_map/ppermute | solution.py:259
  21.8 10.3 %collective-permute-start.3 = (s16[272,128]{1,0:T(8,128)(2,1)S(1)}, s16[272,128]{1,0:T(8,128)(2,1)S(1)}, u32[]{:S(2)}, u32[]{:S(2)}) collective-permute-start(s16[272,128]{1,0:T(8,128)(2,1)S(1)} %copy-done.6), channel_id=1, source_target_pairs={{0,2},{1,3},{2,4},{3,5},{4,6},{5,7},{6,0},{7,1},{8,10},{9,11},{10,... | collective-permute-start | bytes 208904 | tf_op jit(solution)/shard_map/ppermute | solution.py:259
  21.9 13.0 %collective-permute-start.5 = (s16[272,128]{1,0:T(8,128)(2,1)S(1)}, s16[272,128]{1,0:T(8,128)(2,1)S(1)}, u32[]{:S(2)}, u32[]{:S(2)}) collective-permute-start(s16[272,128]{1,0:T(8,128)(2,1)S(1)} %copy-done.5), channel_id=1, source_target_pairs={{0,6},{1,7},{2,0},{3,1},{4,2},{5,3},{6,4},{7,5},{8,14},{9,15},{10,... | collective-permute-start | bytes 208904 | tf_op jit(solution)/shard_map/ppermute | solution.py:259
  25.5 2.2 %copy-start = (bf16[2048,1024]{1,0:T(8,128)(2,1)S(1)}, bf16[2048,1024]{1,0:T(8,128)(2,1)}, u32[]{:S(2)}) copy-start(bf16[2048,1024]{1,0:T(8,128)(2,1)} %we.1) | copy-start | bytes 12582916
  27.7 1.6 %copy-start.1 = (bf16[512,2048]{1,0:T(8,128)(2,1)S(1)}, bf16[512,2048]{1,0:T(8,128)(2,1)}, u32[]{:S(2)}) copy-start(bf16[512,2048]{1,0:T(8,128)(2,1)} %x.1) | copy-start | bytes 6291460
  29.3 9.5 %copy-start.2 = (s32[512,1]{0,1:T(1,128)S(1)}, s32[512,1]{0,1:T(1,128)}, u32[]{:S(2)}) copy-start(s32[512,1]{0,1:T(1,128)} %param.15) | copy-start | bytes 6148
  32.1 7.4 %collective-permute-start = (s16[528,128]{1,0:T(8,128)(2,1)S(1)}, s16[528,128]{1,0:T(8,128)(2,1)S(1)}, u32[]{:S(2)}, u32[]{:S(2)}) collective-permute-start(s16[528,128]{1,0:T(8,128)(2,1)S(1)} %get-tuple-element.28), channel_id=1, source_target_pairs={{0,1},{1,2},{2,3},{3,4},{4,5},{5,6},{6,7},{7,0},{8,9},{9,10},{10,1... | collective-permute-start | bytes 405512 | tf_op jit(solution)/shard_map/ppermute | solution.py:259
  32.2 7.3 %collective-permute-start.1 = (s16[528,128]{1,0:T(8,128)(2,1)S(1)}, s16[528,128]{1,0:T(8,128)(2,1)S(1)}, u32[]{:S(2)}, u32[]{:S(2)}) collective-permute-start(s16[528,128]{1,0:T(8,128)(2,1)S(1)} %get-tuple-element.29), channel_id=1, source_target_pairs={{0,7},{1,0},{2,1},{3,2},{4,3},{5,4},{6,5},{7,6},{8,15},{9,8},{10,9... | collective-permute-start | bytes 405512 | tf_op jit(solution)/shard_map/ppermute | solution.py:259
  35.1 9.1 %collective-permute-start.6 = (s16[528,128]{1,0:T(8,128)(2,1)S(1)}, s16[528,128]{1,0:T(8,128)(2,1)S(1)}, u32[]{:S(2)}, u32[]{:S(2)}) collective-permute-start(s16[528,128]{1,0:T(8,128)(2,1)S(1)} %get-tuple-element.36), channel_id=1, source_target_pairs={{0,2},{1,3},{2,4},{3,5},{4,6},{5,7},{6,0},{7,1},{8,10},{9,11},{10,... | collective-permute-start | bytes 405512 | tf_op jit(solution)/shard_map/ppermute | solution.py:259
  35.2 9.0 %collective-permute-start.7 = (s16[528,128]{1,0:T(8,128)(2,1)S(1)}, s16[528,128]{1,0:T(8,128)(2,1)S(1)}, u32[]{:S(2)}, u32[]{:S(2)}) collective-permute-start(s16[528,128]{1,0:T(8,128)(2,1)S(1)} %get-tuple-element.37), channel_id=1, source_target_pairs={{0,6},{1,7},{2,0},{3,1},{4,2},{5,3},{6,4},{7,5},{8,14},{9,15},{10,... | collective-permute-start | bytes 405512 | tf_op jit(solution)/shard_map/ppermute | solution.py:259
  47.1 10.3 %collective-permute-start.8 = (bf16[16,64,1024]{2,1,0:T(8,128)(2,1)S(1)}, bf16[16,64,1024]{2,1,0:T(8,128)(2,1)}, u32[]{:S(2)}, u32[]{:S(2)}) collective-permute-start(bf16[16,64,1024]{2,1,0:T(8,128)(2,1)S(1)} %all-to-all-done), channel_id=1, source_target_pairs={{0,64},{64,0},{1,65},{65,1},{2,66},{66,2},{3,67},{67,3},{4,68},{68... | collective-permute-start | bytes 6291464 | tf_op jit(solution)/shard_map/ppermute | solution.py:297
  49.2 15.3 %all-to-all-start.1 = ((bf16[32,32,128]{2,1,0:T(8,128)(2,1)}), bf16[32,32,128]{2,1,0:T(8,128)(2,1)S(1)}, u32[]{:S(2)}, u32[]{:S(2)}) async-start(bf16[32,32,128]{2,1,0:T(8,128)(2,1)} %bitcast.12), calls=%async_computation.1 | async-start | bytes 524288 | tf_op jit(solution)/shard_map/all_to_all | solution.py:296

commit v7 on v6

--- a/solution.py
+++ b/solution.py
@@ -52,17 +52,13 @@
     return both[:, :part], both[:, part:]
 
 
-def head_kernel(
-    step_ref, ids, master_h, moment_h, second_h, gradient_h, x_h, w_h,
-    new_master_h, new_moment_h, new_second_h, spread_h, up_h, down_h, far_up_h, far_down_h,
-    master, moment, second, gradient, new_master, new_moment, new_second, fresh,
-    x, wa, wb, wc, up, down, far_up, far_down, sems, out_sems, spread_sems,
+def update_kernel(
+    step_ref, master_h, moment_h, second_h, gradient_h,
+    new_master_h, new_moment_h, new_second_h, spread_h,
+    master, moment, second, gradient, new_master, new_moment, new_second, fresh, sems, out_sems, spread_sems,
 ):
-    part = wa.shape[1]
-    half = x.shape[0] // 2
-    columns = [w_h.at[:, pl.ds(pl.multiple_of(ids[k] * part, part), part)] for k in range(3)]
-    sources = [master_h, moment_h, second_h, gradient_h, x_h] + columns
-    places = [master, moment, second, gradient, x, wa, wb, wc]
+    sources = [moment_h, gradient_h, second_h, master_h]
+    places = [moment, gradient, second, master]
     loads = [
         pltpu.make_async_copy(source, place, sems.at[k])
         for k, (source, place) in enumerate(zip(sources, places))
@@ -75,19 +71,19 @@
 
     one = jnp.float32(1.0)
     first, other = lax.fori_loop(0, step_ref[0], times, (one, one))
-    for load in loads[:4]:
-        load.wait()
     ones = jnp.ones((1, master.shape[1]), jnp.float32)
     first_fix, second_fix = ones * (1.0 - first), ones * (1.0 - other)
+    for load in loads:
+        load.wait()
     g, old = gradient[...], master[...]
     m = 0.9 * moment[...] + 0.1 * g
     v = 0.95 * second[...] + 0.05 * g * g
     update = m / first_fix / (jnp.sqrt(v / second_fix) + 1e-08)
     new = old - learn_rate * (update + decay_rate * old)
+    fresh[...] = new.astype(jnp.bfloat16)
     new_moment[...] = m
     new_second[...] = v
     new_master[...] = new
-    fresh[...] = new.astype(jnp.bfloat16)
     stores = [
         pltpu.make_async_copy(fresh, spread_h.at[k], spread_sems.at[k])
         for k in range(spread_h.shape[0])
@@ -99,93 +95,99 @@
     ]
     for store in stores:
         store.start()
-
-    def send(k, source, place):
-        store = pltpu.make_async_copy(source, place, out_sems.at[3 + k])
-        store.start()
-        stores.append(store)
-
-    for load in loads[4:7]:
-        load.wait()
-    above, below = pair_product(x, wa, wb)
-    put_coded(up, above)
-    send(0, up, up_h)
-    put_coded(down, below)
-    send(1, down, down_h)
-    loads[7].wait()
-    far = product(x, wc)
-    put_coded(far_up, far[:half])
-    send(2, far_up, far_up_h)
-    put_coded(far_down, far[half:])
-    send(3, far_down, far_down_h)
     for store in stores:
         store.wait()
 
 
-def head(step_count, ids, master, moment, second, gradient, x, w, chips):
-    rows, depth = x.shape
-    part = w.shape[1] // 8
+def updated(step_count, master, moment, second, gradient, chips):
     anywhere = pl.BlockSpec(memory_space=pl.ANY)
-    scalar = pl.BlockSpec(memory_space=pltpu.SMEM)
     shard = master.shape
-    codes = [(rows + TAIL, part)] * 2 + [(rows // 2 + TAIL, part)] * 2
     outs = [jax.ShapeDtypeStruct(shard, jnp.float32)] * 3
     outs += [jax.ShapeDtypeStruct((chips,) + shard, jnp.bfloat16)]
-    outs += [jax.ShapeDtypeStruct(c, jnp.int16) for c in codes]
     return pl.pallas_call(
-        head_kernel,
+        update_kernel,
         out_shape=outs,
-        in_specs=[scalar] * 2 + [anywhere] * 6,
-        out_specs=[anywhere] * len(outs),
+        in_specs=[pl.BlockSpec(memory_space=pltpu.SMEM)] + [anywhere] * 4,
+        out_specs=[anywhere] * 4,
         scratch_shapes=[pltpu.VMEM(shard, jnp.float32)] * 7
-        + [pltpu.VMEM(shard, jnp.bfloat16), pltpu.VMEM((rows, depth), x.dtype)]
-        + [pltpu.VMEM((depth, part), w.dtype)] * 3
-        + [pltpu.VMEM(c, jnp.int16) for c in codes]
         + [
-            pltpu.SemaphoreType.DMA((8,)),
-            pltpu.SemaphoreType.DMA((7,)),
+            pltpu.VMEM(shard, jnp.bfloat16),
+            pltpu.SemaphoreType.DMA((4,)),
+            pltpu.SemaphoreType.DMA((3,)),
             pltpu.SemaphoreType.DMA((chips,)),
         ],
         compiler_params=pltpu.CompilerParams(vmem_limit_bytes=60 * 2**20),
         cost_estimate=pl.CostEstimate(
-            flops=6 * rows * depth * part + 30 * master.size,
-            bytes_accessed=2 * x.size + 6 * depth * part + 60 * master.size,
-            transcendentals=3 * master.size,
+            flops=30 * master.size, bytes_accessed=60 * master.size, transcendentals=3 * master.size
         ),
-    )(step_count, ids, master, moment, second, gradient, x, w)
-
-
-def near_kernel(ids, x, wa, wb, wc, wd, we, qa, qb, pc, pd, pe):
-    above, below = pair_product(x, wa, wb)
-    put_coded(qa, above)
-    put_coded(qb, below)
-    pc[...], pd[...] = pair_product(x, wc, wd)
-    pe[...] = product(x, we)
-
-
-def products(kernel, x, w, ids, count, width, outs):
+    )(step_count, master, moment, second, gradient)
+
+
+def loading(steps, kernel, me, x_h, w_h, *refs):
+    x, w, x_sems, w_sems = refs[-4:]
+    part = w.shape[2]
+    rows = x.shape[0] // 2
+    loads = []
+    for k in range(2):
+        half = pl.ds(k * rows, rows)
+        loads.append(pltpu.make_async_copy(x_h.at[half], x.at[half], x_sems.at[k]))
+    for k, step in enumerate(steps):
+        block = lax.rem(me[0] + step, w_h.shape[1] // part)
+        columns = pl.ds(pl.multiple_of(block * part, part), part)
+        loads.append(pltpu.make_async_copy(w_h.at[:, columns], w.at[k], w_sems.at[k]))
+    for load in loads:
+        load.start()
+    for load in loads[:2]:
+        load.wait()
+
+    def columns(k):
+        loads[2 + k].wait()
+        return w.at[k]
+
+    kernel(x, columns, *refs[:-4])
+
+
+def far_kernel(x, columns, up, down, far_up, far_down):
+    half = x.shape[0] // 2
+    above, below = pair_product(x, columns(0), columns(1))
+    put_coded(up, above)
+    put_coded(down, below)
+    far = product(x, columns(2))
+    put_coded(far_up, far[:half])
+    put_coded(far_down, far[half:])
+
+
+def near_kernel(x, columns, up, down, next_up, next_down, own):
+    above, below = pair_product(x, columns(0), columns(1))
+    put_coded(up, above)
+    put_coded(down, below)
+    next_up[...], next_down[...] = pair_product(x, columns(2), columns(3))
+    own[...] = product(x, columns(4))
+
+
+def products(kernel, x, w, me, steps, outs):
     rows, depth = x.shape
-    whole = lambda g, ids: (0, 0)
-    columns = [
-        pl.BlockSpec((depth, width), functools.partial(lambda k, g, ids: (0, ids[k]), k))
-        for k in range(count)
-    ]
+    count = len(steps)
+    part = w.shape[1] // 8
+    anywhere = pl.BlockSpec(memory_space=pl.ANY)
     return pl.pallas_call(
-        kernel,
+        functools.partial(loading, steps, kernel),
         out_shape=outs,
-        grid_spec=pltpu.PrefetchScalarGridSpec(
-            num_scalar_prefetch=1,
-            grid=(1,),
-            in_specs=[pl.BlockSpec((rows, depth), whole)] + columns,
-            out_specs=[pl.BlockSpec(o.shape, whole) for o in outs],
-        ),
-        compiler_params=pltpu.CompilerParams(vmem_limit_bytes=40 * 2**20),
+        in_specs=[pl.BlockSpec(memory_space=pltpu.SMEM), anywhere, anywhere],
+        out_specs=[pl.BlockSpec(memory_space=pltpu.VMEM)] * len(outs),
+        scratch_shapes=[
+            pltpu.VMEM((rows, depth), x.dtype),
+            pltpu.VMEM((count, depth, part), w.dtype),
+            pltpu.SemaphoreType.DMA((2,)),
+            pltpu.SemaphoreType.DMA((count,)),
+        ],
+        compiler_params=pltpu.CompilerParams(vmem_limit_bytes=52 * 2**20),
         cost_estimate=pl.CostEstimate(
-            flops=2 * rows * depth * width * count,
-            bytes_accessed=2 * depth * (rows + width * count),
+            flops=2 * rows * depth * part * count,
+            bytes_accessed=2 * depth * (rows + part * count),
             transcendentals=0,
         ),
-    )(ids, x, *([w] * count))
+    )(me, x, w)
 
 
 def local_call(kernel, outs, *args, flops=0):
@@ -263,20 +265,23 @@
     rows, width = master.shape
     chips = lax.axis_size(CHIPS)
     size = lax.axis_size("tp")
-    me = lax.axis_index("tp")
+    me = jnp.reshape(lax.axis_index("tp"), (1,)).astype(jnp.int32)
     count = branch_rows.shape[0]
     part = old_weights.shape[1] // size
     code = lambda n: jax.ShapeDtypeStruct((n + TAIL, part), jnp.int16)
     full = jax.ShapeDtypeStruct((count, part), jnp.float32)
-    at = lambda *steps: jnp.stack([lax.rem(me + k, size) for k in steps]).astype(jnp.int32)
-    new_master, new_moment, new_second, spread, q3, q5, q4a, q4b = head(
-        step_count, at(3, 5, 4), master, moment, second, gradient, branch_rows, old_weights, chips
+    new_master, new_moment, new_second, spread = updated(
+        step_count, master, moment, second, gradient, chips
     )
     mine = lax.all_to_all(spread, CHIPS, split_axis=0, concat_axis=0, tiled=True)
+    q3, q5, q4a, q4b = products(
+        far_kernel, branch_rows, old_weights, me, (3, 5, 4),
+        [code(count), code(count), code(count // 2), code(count // 2)],
+    )
     r3, r5 = along_tp(q3, 1), along_tp(q5, -1)
     r4a, r4b = along_tp(q4a, 2), along_tp(q4b, -2)
     q1, q7, p2, p6, p0 = products(
-        near_kernel, branch_rows, old_weights, at(1, 7, 2, 6, 0), 5, part,
+        near_kernel, branch_rows, old_weights, me, (1, 7, 2, 6, 0),
         [code(count), code(count), full, full, full],
     )
     r1, r7 = along_tp(q1, 1), along_tp(q7, -1)

time: 65.6 us -> 65.1 us (level)
  Pallas kernels: 17 us -> 21.2 us
  local copies, waits for them, and re-layouts: 4.59 us -> 0.71 us
  waiting for transfers between devices: 9.72 us -> 8.18 us
  starting transfers between devices: 31.9 us -> 33.2 us
    pallas_call x2 -> x3, Pallas kernels: 9.18 us -> 13.4 us  [the longest x2 10.2 us: products(): pl.pallas_call(functools.partial(loading, steps, kernel), out_shape=outs,...]
    unnamed x15 -> x3, local copies, waits for them, and re-layouts: 4.5 us -> 0.71 us
    all_to_all x1, waiting for transfers between devices: 1.55 us -> 0.01 us  [local(): lax.all_to_all(spread, CHIPS, split_axis=0, concat_axis=0, tiled=True)]
    all_to_all x1, starting transfers between devices: 6.25 us -> 7.4 us  [local(): lax.all_to_all(placed, PLANE, split_axis=0, concat_axis=0, tiled=True)]
  transfers between devices with their start and end apart: 11 -> 11, of which waited for: 3 -> 2; matrix products, arithmetic and copies ran while one was open for 0% -> 0% of each run, Pallas kernels for 16% -> 28%
where the time goes in v7:
time: 65.1 us; the launch traced here: 64.7 us
  starting transfers between devices  33.2 us (51%)
  Pallas kernels  21.2 us (33%)
  waiting for transfers between devices  8.18 us (13%)
  between operations  1.39 us (2%)
  local copies, waits for them, and re-layouts  0.71 us (1%)
    ppermute x8, starting transfers between devices, along_tp(): lax.ppermute(value, 'tp', [(i, (i + step) % size) for i in range(size)])  15.7 us
    pallas_call x2, Pallas kernels, products(): pl.pallas_call(functools.partial(loading, steps, kernel), out_shape=outs,...  10.2 us
    all_to_all x1, starting transfers between devices, local(): lax.all_to_all(spread, CHIPS, split_axis=0, concat_axis=0, tiled=True)  7.6 us
    all_to_all x1, starting transfers between devices, local(): lax.all_to_all(placed, PLANE, split_axis=0, concat_axis=0, tiled=True)  7.4 us
    pallas_call x2, Pallas kernels, set_half(): pl.pallas_call(half_kernel, out_shape=jax.ShapeDtypeStruct((lanes, 2, row...  5.64 us
    ppermute x8, waiting for transfers between devices, along_tp(): lax.ppermute(value, 'tp', [(i, (i + step) % size) for i in range(size)])  4.77 us
    all_to_all x1, waiting for transfers between devices, local(): lax.all_to_all(placed, PLANE, split_axis=0, concat_axis=0, tiled=True)  3.41 us
    pallas_call x1, Pallas kernels, updated(): pl.pallas_call(update_kernel, out_shape=outs, in_specs=[pl.BlockSpec(memo...  3.16 us
  transfers between devices with their start and end apart: 11, of which 2 were waited for; matrix products, arithmetic and copies ran while one was open for 0% of the time, Pallas kernels for 28%

profile of v7, /device:TPU:1, one launch (start us, length us, event | category | flops | bytes accessed | tf_op | source)
XLA Modules:
  0.0 64.7 jit_solution(2039146296103621549)
XLA Ops:
  1.3 3.2 %shard_map.119 = (f32[64,1024]{1,0:T(8,128)}, f32[64,1024]{1,0:T(8,128)}, f32[64,1024]{1,0:T(8,128)}, bf16[16,64,1024]{2,1,0:T(8,128)(2,1)}) custom-call(s32[1]{0:T(128)S(6)} %copy.16.step_ref, f32[64,1024]{1,0:T(8,128)} %master_h.1, f32[64,1024]{1,0:T(8,128)} %moment_h.1, f32[64,1024]{1,0:T(8,128)} %second_h.1, f32[64,1024]{1,0:T(8,128)} %gradient_h.1), custom_call_target="tpu_custom_call" | custom-call | flops 1966080 | bytes 3932160 | tf_op jit(solution)/shard_map/pallas_call | solution.py:107
  4.4 7.6 %all-to-all-start = ((bf16[16,64,1024]{2,1,0:T(8,128)(2,1)}), bf16[16,64,1024]{2,1,0:T(8,128)(2,1)S(1)}, u32[]{:S(2)}, u32[]{:S(2)}) async-start(bf16[16,64,1024]{2,1,0:T(8,128)(2,1)} %get-tuple-element.26), calls=%async_computation | async-start | bytes 4194304 | tf_op jit(solution)/shard_map/all_to_all | solution.py:276
  12.1 4.6 %shard_map.121 = (s16[528,128]{1,0:T(8,128)(2,1)S(1)}, s16[528,128]{1,0:T(8,128)(2,1)S(1)}, s16[272,128]{1,0:T(8,128)(2,1)S(1)}, s16[272,128]{1,0:T(8,128)(2,1)S(1)}) custom-call(s32[1]{0:T(128)} %bitcast.1.me, bf16[512,2048]{1,0:T(8,128)(2,1)} %x_h.3, bf16[2048,1024]{1,0:T(8,128)(2,1)} %w_h.3), custom_call_target="tpu_custom_call" | custom-call | flops 805306368 | bytes 3670016 | tf_op jit(solution)/shard_map/pallas_call | solution.py:173
  16.7 1.7 %collective-permute-start.2 = (s16[528,128]{1,0:T(8,128)(2,1)S(1)}, s16[528,128]{1,0:T(8,128)(2,1)S(1)}, u32[]{:S(2)}, u32[]{:S(2)}) collective-permute-start(s16[528,128]{1,0:T(8,128)(2,1)S(1)} %get-tuple-element.31), channel_id=1, source_target_pairs={{0,1},{1,2},{2,3},{3,4},{4,5},{5,6},{6,7},{7,0},{8,9},{9,10},{10,1... | collective-permute-start | bytes 405512 | tf_op jit(solution)/shard_map/ppermute | solution.py:261
  18.4 4.0 %collective-permute-start.4 = (s16[528,128]{1,0:T(8,128)(2,1)S(1)}, s16[528,128]{1,0:T(8,128)(2,1)S(1)}, u32[]{:S(2)}, u32[]{:S(2)}) collective-permute-start(s16[528,128]{1,0:T(8,128)(2,1)S(1)} %get-tuple-element.34), channel_id=1, source_target_pairs={{0,7},{1,0},{2,1},{3,2},{4,3},{5,4},{6,5},{7,6},{8,15},{9,8},{10,9... | collective-permute-start | bytes 405512 | tf_op jit(solution)/shard_map/ppermute | solution.py:261
  22.4 0.0 collective-permute-start.3
  22.4 0.0 copy-start
  22.4 3.6 %collective-permute-start.5 = (s16[272,128]{1,0:T(8,128)(2,1)S(1)}, s16[272,128]{1,0:T(8,128)(2,1)S(1)}, u32[]{:S(2)}, u32[]{:S(2)}) collective-permute-start(s16[272,128]{1,0:T(8,128)(2,1)S(1)} %get-tuple-element.35), channel_id=1, source_target_pairs={{0,6},{1,7},{2,0},{3,1},{4,2},{5,3},{6,4},{7,5},{8,14},{9,15},{10,... | collective-permute-start | bytes 208904 | tf_op jit(solution)/shard_map/ppermute | solution.py:261
  26.0 5.6 %shard_map.120 = (s16[528,128]{1,0:T(8,128)(2,1)S(1)}, s16[528,128]{1,0:T(8,128)(2,1)S(1)}, f32[512,128]{1,0:T(8,128)S(1)}, f32[512,128]{1,0:T(8,128)S(1)}, f32[512,128]{1,0:T(8,128)S(1)}) custom-call(s32[1]{0:T(128)} %bitcast.1.me, bf16[512,2048]{1,0:T(8,128)(2,1)} %x_h.3, bf16[2048,1024]{1,0:T(8,128)(2,1)} %w_h.3), custom_call_target="tpu_custom_call" | custom-call | flops 1342177280 | bytes 4718592 | tf_op jit(solution)/shard_map/pallas_call | solution.py:173
  31.6 0.1 collective-permute-start
  31.7 0.0 collective-permute-done.3.far_a
  31.7 2.7 %collective-permute-start.1 = (s16[528,128]{1,0:T(8,128)(2,1)S(1)}, s16[528,128]{1,0:T(8,128)(2,1)S(1)}, u32[]{:S(2)}, u32[]{:S(2)}) collective-permute-start(s16[528,128]{1,0:T(8,128)(2,1)S(1)} %get-tuple-element.29), channel_id=1, source_target_pairs={{0,7},{1,0},{2,1},{3,2},{4,3},{5,4},{6,5},{7,6},{8,15},{9,8},{10,9... | collective-permute-start | bytes 405512 | tf_op jit(solution)/shard_map/ppermute | solution.py:261
  34.3 0.0 collective-permute-done.5.far_b
  34.4 0.0 collective-permute-done.2.next_a
  34.4 0.0 collective-permute-done.4.next_b
  34.4 0.3 shard_map.122
  34.6 0.1 collective-permute-start.6
  34.7 3.6 %collective-permute-start.7 = (s16[528,128]{1,0:T(8,128)(2,1)S(1)}, s16[528,128]{1,0:T(8,128)(2,1)S(1)}, u32[]{:S(2)}, u32[]{:S(2)}) collective-permute-start(s16[528,128]{1,0:T(8,128)(2,1)S(1)} %get-tuple-element.37), channel_id=1, source_target_pairs={{0,6},{1,7},{2,0},{3,1},{4,2},{5,3},{6,4},{7,5},{8,14},{9,15},{10,... | collective-permute-start | bytes 405512 | tf_op jit(solution)/shard_map/ppermute | solution.py:261
  38.3 0.0 copy-done
  38.3 0.6 %shard_map.123.selector = bf16[1024,512]{1,0:T(8,128)(2,1)S(1)} custom-call(s32[1,512]{1,0:T(1,128)S(1)} %bitcast.9), custom_call_target="tpu_custom_call" | custom-call | bytes 1048576 | tf_op jit(solution)/shard_map/pallas_call | solution.py:194
  39.0 0.0 collective-permute-done.ra
  39.0 0.0 collective-permute-done.1.rb
  39.0 4.7 %collective-permute-done.6.rc = s16[528,128]{1,0:T(8,128)(2,1)S(1)} collective-permute-done((s16[528,128]{1,0:T(8,128)(2,1)S(1)}, s16[528,128]{1,0:T(8,128)(2,1)S(1)}, u32[]{:S(2)}, u32[]{:S(2)}) %collective-permute-start.6) | collective-permute-done | bytes 135200 | tf_op jit(solution)/shard_map/ppermute | solution.py:261
  43.7 0.0 collective-permute-done.7.rd
  43.7 1.3 %shard_map.124 = bf16[1024,128]{1,0:T(8,128)(2,1)} custom-call(f32[512,128]{1,0:T(8,128)S(1)} %get-tuple-element.27.own, s16[528,128]{1,0:T(8,128)(2,1)S(1)} %collective-permute-done.ra, s16[528,128]{1,0:T(8,128)(2,1)S(1)} %collective-permute-done.1.rb, s16[528,128]{1,0:T(8,128)(2,1)S(1)} %collective-permute-done.6.rc, ...), custom_call_target="tpu_custom_call" | custom-call | bytes 1048576 | tf_op jit(solution)/shard_map/pallas_call | solution.py:194
  45.0 0.0 all-to-all-done
  45.0 2.5 %collective-permute-start.8 = (bf16[16,64,1024]{2,1,0:T(8,128)(2,1)S(1)}, bf16[16,64,1024]{2,1,0:T(8,128)(2,1)}, u32[]{:S(2)}, u32[]{:S(2)}) collective-permute-start(bf16[16,64,1024]{2,1,0:T(8,128)(2,1)S(1)} %all-to-all-done), channel_id=1, source_target_pairs={{0,64},{64,0},{1,65},{65,1},{2,66},{66,2},{3,67},{67,3},{4,68},{68... | collective-permute-start | bytes 6291464 | tf_op jit(solution)/shard_map/ppermute | solution.py:302
  47.6 7.4 %all-to-all-start.1 = ((bf16[32,32,128]{2,1,0:T(8,128)(2,1)}), bf16[32,32,128]{2,1,0:T(8,128)(2,1)S(1)}, u32[]{:S(2)}, u32[]{:S(2)}) async-start(bf16[32,32,128]{2,1,0:T(8,128)(2,1)} %bitcast.5), calls=%async_computation.1 | async-start | bytes 524288 | tf_op jit(solution)/shard_map/all_to_all | solution.py:301
  55.0 1.9 %shard_map.125.refs_0_ = bf16[2,2,512,1024]{3,2,1,0:T(8,128)(2,1)} custom-call(s32[1]{0:T(128)} %bitcast.place, bf16[2,512,1024]{2,1,0:T(8,128)(2,1)S(1)} %bitcast.8), custom_call_target="tpu_custom_call" | custom-call | bytes 4194304 | tf_op jit(solution)/shard_map/pallas_call | solution.py:243
  56.8 0.0 collective-permute-done.8
  56.8 3.8 %shard_map.126 = bf16[2,2,512,1024]{3,2,1,0:T(8,128)(2,1)} custom-call(s32[1]{0:T(128)S(6)} %sub.3.place, bf16[2,512,1024]{2,1,0:T(8,128)(2,1)} %bitcast.3.half, bf16[2,2,512,1024]{3,2,1,0:T(8,128)(2,1)} %shard_map.125.refs_0_), custom_call_target="tpu_custom_call", output_to_operand_aliasing={{}: (2, {})} | custom-call | bytes 4194304 | tf_op jit(solution)/shard_map/pallas_call | solution.py:243
  60.6 3.4 %all-to-all-done.1 = bf16[32,32,128]{2,1,0:T(8,128)(2,1)S(1)} async-done(((bf16[32,32,128]{2,1,0:T(8,128)(2,1)}), bf16[32,32,128]{2,1,0:T(8,128)(2,1)S(1)}, u32[]{:S(2)}, u32[]{:S(2)}) %all-to-all-start.1) | async-done | bytes 262176 | tf_op jit(solution)/shard_map/all_to_all | solution.py:301
  64.0 0.7 %copy.17 = bf16[1,32,32,128]{3,2,1,0:T(8,128)(2,1)} copy(bf16[1,32,32,128]{3,2,1,0:T(8,128)(2,1)S(1)} %bitcast.11) | data formatting | bytes 524288
Async XLA Ops:
  4.4 40.6 %all-to-all-start = ((bf16[16,64,1024]{2,1,0:T(8,128)(2,1)}), bf16[16,64,1024]{2,1,0:T(8,128)(2,1)S(1)}, u32[]{:S(2)}, u32[]{:S(2)}) async-start(bf16[16,64,1024]{2,1,0:T(8,128)(2,1)} %get-tuple-element.26), calls=%async_computation | async-start | bytes 4194304 | tf_op jit(solution)/shard_map/all_to_all | solution.py:276
  16.7 17.7 %collective-permute-start.2 = (s16[528,128]{1,0:T(8,128)(2,1)S(1)}, s16[528,128]{1,0:T(8,128)(2,1)S(1)}, u32[]{:S(2)}, u32[]{:S(2)}) collective-permute-start(s16[528,128]{1,0:T(8,128)(2,1)S(1)} %get-tuple-element.31), channel_id=1, source_target_pairs={{0,1},{1,2},{2,3},{3,4},{4,5},{5,6},{6,7},{7,0},{8,9},{9,10},{10,1... | collective-permute-start | bytes 405512 | tf_op jit(solution)/shard_map/ppermute | solution.py:261
  18.4 16.0 %collective-permute-start.4 = (s16[528,128]{1,0:T(8,128)(2,1)S(1)}, s16[528,128]{1,0:T(8,128)(2,1)S(1)}, u32[]{:S(2)}, u32[]{:S(2)}) collective-permute-start(s16[528,128]{1,0:T(8,128)(2,1)S(1)} %get-tuple-element.34), channel_id=1, source_target_pairs={{0,7},{1,0},{2,1},{3,2},{4,3},{5,4},{6,5},{7,6},{8,15},{9,8},{10,9... | collective-permute-start | bytes 405512 | tf_op jit(solution)/shard_map/ppermute | solution.py:261
  22.4 9.3 %collective-permute-start.3 = (s16[272,128]{1,0:T(8,128)(2,1)S(1)}, s16[272,128]{1,0:T(8,128)(2,1)S(1)}, u32[]{:S(2)}, u32[]{:S(2)}) collective-permute-start(s16[272,128]{1,0:T(8,128)(2,1)S(1)} %get-tuple-element.32), channel_id=1, source_target_pairs={{0,2},{1,3},{2,4},{3,5},{4,6},{5,7},{6,0},{7,1},{8,10},{9,11},{10,... | collective-permute-start | bytes 208904 | tf_op jit(solution)/shard_map/ppermute | solution.py:261
  22.4 15.9 %copy-start = (s32[512,1]{0,1:T(1,128)S(1)}, s32[512,1]{0,1:T(1,128)}, u32[]{:S(2)}) copy-start(s32[512,1]{0,1:T(1,128)} %param.15) | copy-start | bytes 6148
  22.4 12.0 %collective-permute-start.5 = (s16[272,128]{1,0:T(8,128)(2,1)S(1)}, s16[272,128]{1,0:T(8,128)(2,1)S(1)}, u32[]{:S(2)}, u32[]{:S(2)}) collective-permute-start(s16[272,128]{1,0:T(8,128)(2,1)S(1)} %get-tuple-element.35), channel_id=1, source_target_pairs={{0,6},{1,7},{2,0},{3,1},{4,2},{5,3},{6,4},{7,5},{8,14},{9,15},{10,... | collective-permute-start | bytes 208904 | tf_op jit(solution)/shard_map/ppermute | solution.py:261
  31.6 7.4 %collective-permute-start = (s16[528,128]{1,0:T(8,128)(2,1)S(1)}, s16[528,128]{1,0:T(8,128)(2,1)S(1)}, u32[]{:S(2)}, u32[]{:S(2)}) collective-permute-start(s16[528,128]{1,0:T(8,128)(2,1)S(1)} %get-tuple-element.28), channel_id=1, source_target_pairs={{0,1},{1,2},{2,3},{3,4},{4,5},{5,6},{6,7},{7,0},{8,9},{9,10},{10,1... | collective-permute-start | bytes 405512 | tf_op jit(solution)/shard_map/ppermute | solution.py:261
  31.7 7.3 %collective-permute-start.1 = (s16[528,128]{1,0:T(8,128)(2,1)S(1)}, s16[528,128]{1,0:T(8,128)(2,1)S(1)}, u32[]{:S(2)}, u32[]{:S(2)}) collective-permute-start(s16[528,128]{1,0:T(8,128)(2,1)S(1)} %get-tuple-element.29), channel_id=1, source_target_pairs={{0,7},{1,0},{2,1},{3,2},{4,3},{5,4},{6,5},{7,6},{8,15},{9,8},{10,9... | collective-permute-start | bytes 405512 | tf_op jit(solution)/shard_map/ppermute | solution.py:261
  34.6 9.1 %collective-permute-start.6 = (s16[528,128]{1,0:T(8,128)(2,1)S(1)}, s16[528,128]{1,0:T(8,128)(2,1)S(1)}, u32[]{:S(2)}, u32[]{:S(2)}) collective-permute-start(s16[528,128]{1,0:T(8,128)(2,1)S(1)} %get-tuple-element.36), channel_id=1, source_target_pairs={{0,2},{1,3},{2,4},{3,5},{4,6},{5,7},{6,0},{7,1},{8,10},{9,11},{10,... | collective-permute-start | bytes 405512 | tf_op jit(solution)/shard_map/ppermute | solution.py:261
  34.7 9.0 %collective-permute-start.7 = (s16[528,128]{1,0:T(8,128)(2,1)S(1)}, s16[528,128]{1,0:T(8,128)(2,1)S(1)}, u32[]{:S(2)}, u32[]{:S(2)}) collective-permute-start(s16[528,128]{1,0:T(8,128)(2,1)S(1)} %get-tuple-element.37), channel_id=1, source_target_pairs={{0,6},{1,7},{2,0},{3,1},{4,2},{5,3},{6,4},{7,5},{8,14},{9,15},{10,... | collective-permute-start | bytes 405512 | tf_op jit(solution)/shard_map/ppermute | solution.py:261
  45.0 11.8 %collective-permute-start.8 = (bf16[16,64,1024]{2,1,0:T(8,128)(2,1)S(1)}, bf16[16,64,1024]{2,1,0:T(8,128)(2,1)}, u32[]{:S(2)}, u32[]{:S(2)}) collective-permute-start(bf16[16,64,1024]{2,1,0:T(8,128)(2,1)S(1)} %all-to-all-done), channel_id=1, source_target_pairs={{0,64},{64,0},{1,65},{65,1},{2,66},{66,2},{3,67},{67,3},{4,68},{68... | collective-permute-start | bytes 6291464 | tf_op jit(solution)/shard_map/ppermute | solution.py:302
  47.6 16.5 %all-to-all-start.1 = ((bf16[32,32,128]{2,1,0:T(8,128)(2,1)}), bf16[32,32,128]{2,1,0:T(8,128)(2,1)S(1)}, u32[]{:S(2)}, u32[]{:S(2)}) async-start(bf16[32,32,128]{2,1,0:T(8,128)(2,1)} %bitcast.5), calls=%async_computation.1 | async-start | bytes 524288 | tf_op jit(solution)/shard_map/all_to_all | solution.py:301

commit v8 on v7

--- a/solution.py
+++ b/solution.py
@@ -15,6 +15,9 @@
 CHIPS = ("xlo", "y", "xhi")
 LEVELS = 32767.0
 TAIL = 16
+PIECES = 2
+CHUNKS = 4
+MOST_STEPS = 8
 
 
 def coded(value):
@@ -41,60 +44,61 @@
     return codes * (1.0 / LEVELS) * jnp.exp2(power * (1.0 / 256.0))
 
 
-def product(rows_ref, columns_ref):
-    return jnp.dot(rows_ref[...], columns_ref[...], preferred_element_type=jnp.float32)
-
-
-def pair_product(rows_ref, first_ref, second_ref):
-    part = first_ref.shape[1]
-    columns = jnp.concatenate([first_ref[...], second_ref[...]], axis=1)
-    both = jnp.dot(rows_ref[...], columns, preferred_element_type=jnp.float32)
-    return both[:, :part], both[:, part:]
-
-
 def update_kernel(
-    step_ref, master_h, moment_h, second_h, gradient_h,
+    step_h, master_h, moment_h, second_h, gradient_h,
     new_master_h, new_moment_h, new_second_h, spread_h,
-    master, moment, second, gradient, new_master, new_moment, new_second, fresh, sems, out_sems, spread_sems,
+    step, master, moment, second, gradient, new_master, new_moment, new_second, fresh,
+    step_sem, sems, out_sems, spread_sems,
 ):
     sources = [moment_h, gradient_h, second_h, master_h]
     places = [moment, gradient, second, master]
+    rows = master.shape[0] // PIECES
+    pieces = [pl.ds(p * rows, rows) for p in range(PIECES)]
+    load_step = pltpu.make_async_copy(step_h, step, step_sem)
+    load_step.start()
     loads = [
-        pltpu.make_async_copy(source, place, sems.at[k])
-        for k, (source, place) in enumerate(zip(sources, places))
+        [
+            pltpu.make_async_copy(source.at[piece], place.at[piece], sems.at[p, k])
+            for k, (source, place) in enumerate(zip(sources, places))
+        ]
+        for p, piece in enumerate(pieces)
     ]
-    for load in loads:
-        load.start()
-
-    def times(k, fixes):
-        return fixes[0] * 0.9, fixes[1] * 0.95
-
-    one = jnp.float32(1.0)
-    first, other = lax.fori_loop(0, step_ref[0], times, (one, one))
-    ones = jnp.ones((1, master.shape[1]), jnp.float32)
-    first_fix, second_fix = ones * (1.0 - first), ones * (1.0 - other)
-    for load in loads:
-        load.wait()
-    g, old = gradient[...], master[...]
-    m = 0.9 * moment[...] + 0.1 * g
-    v = 0.95 * second[...] + 0.05 * g * g
-    update = m / first_fix / (jnp.sqrt(v / second_fix) + 1e-08)
-    new = old - learn_rate * (update + decay_rate * old)
-    fresh[...] = new.astype(jnp.bfloat16)
-    new_moment[...] = m
-    new_second[...] = v
-    new_master[...] = new
-    stores = [
-        pltpu.make_async_copy(fresh, spread_h.at[k], spread_sems.at[k])
-        for k in range(spread_h.shape[0])
-    ]
+    for group in loads:
+        for load in group:
+            load.start()
+
+    load_step.wait()
+    steps = jnp.broadcast_to(step[...], (1, master.shape[1]))
+    first = other = jnp.ones(steps.shape, jnp.float32)
+    for k in range(MOST_STEPS):
+        first = jnp.where(steps > k, first * 0.9, first)
+        other = jnp.where(steps > k, other * 0.95, other)
+    first_fix, second_fix = 1.0 - first, 1.0 - other
     finished = [(new_master, new_master_h), (new_moment, new_moment_h), (new_second, new_second_h)]
-    stores += [
-        pltpu.make_async_copy(source, place, out_sems.at[k])
-        for k, (source, place) in enumerate(finished)
-    ]
-    for store in stores:
-        store.start()
+    stores = []
+    for p, piece in enumerate(pieces):
+        for load in loads[p]:
+            load.wait()
+        g, old = gradient[piece, :], master[piece, :]
+        m = 0.9 * moment[piece, :] + 0.1 * g
+        v = 0.95 * second[piece, :] + 0.05 * g * g
+        update = m / first_fix / (jnp.sqrt(v / second_fix) + 1e-08)
+        new = old - learn_rate * (update + decay_rate * old)
+        fresh[piece, :] = new.astype(jnp.bfloat16)
+        new_moment[piece, :] = m
+        new_second[piece, :] = v
+        new_master[piece, :] = new
+        group = [
+            pltpu.make_async_copy(fresh.at[piece], spread_h.at[k, piece], spread_sems.at[p, k])
+            for k in range(spread_h.shape[0])
+        ]
+        group += [
+            pltpu.make_async_copy(source.at[piece], place.at[piece], out_sems.at[p, k])
+            for k, (source, place) in enumerate(finished)
+        ]
+        for store in group:
+            store.start()
+        stores += group
     for store in stores:
         store.wait()
 
@@ -107,79 +111,91 @@
     return pl.pallas_call(
         update_kernel,
         out_shape=outs,
-        in_specs=[pl.BlockSpec(memory_space=pltpu.SMEM)] + [anywhere] * 4,
+        in_specs=[anywhere] * 5,
         out_specs=[anywhere] * 4,
-        scratch_shapes=[pltpu.VMEM(shard, jnp.float32)] * 7
+        scratch_shapes=[pltpu.VMEM((1, 1), jnp.int32)]
+        + [pltpu.VMEM(shard, jnp.float32)] * 7
         + [
             pltpu.VMEM(shard, jnp.bfloat16),
-            pltpu.SemaphoreType.DMA((4,)),
-            pltpu.SemaphoreType.DMA((3,)),
-            pltpu.SemaphoreType.DMA((chips,)),
+            pltpu.SemaphoreType.DMA,
+            pltpu.SemaphoreType.DMA((PIECES, 4)),
+            pltpu.SemaphoreType.DMA((PIECES, 3)),
+            pltpu.SemaphoreType.DMA((PIECES, chips)),
         ],
         compiler_params=pltpu.CompilerParams(vmem_limit_bytes=60 * 2**20),
         cost_estimate=pl.CostEstimate(
             flops=30 * master.size, bytes_accessed=60 * master.size, transcendentals=3 * master.size
         ),
-    )(step_count, master, moment, second, gradient)
-
-
-def loading(steps, kernel, me, x_h, w_h, *refs):
-    x, w, x_sems, w_sems = refs[-4:]
+    )(step_count.reshape(1, 1), master, moment, second, gradient)
+
+
+def loading(steps, groups, kernel, me, x_h, w_h, *refs):
+    x, w, totals, x_sems, w_sems = refs[-5:]
     part = w.shape[2]
-    rows = x.shape[0] // 2
+    depth = x.shape[1] // CHUNKS
     loads = []
-    for k in range(2):
-        half = pl.ds(k * rows, rows)
-        loads.append(pltpu.make_async_copy(x_h.at[half], x.at[half], x_sems.at[k]))
-    for k, step in enumerate(steps):
-        block = lax.rem(me[0] + step, w_h.shape[1] // part)
-        columns = pl.ds(pl.multiple_of(block * part, part), part)
-        loads.append(pltpu.make_async_copy(w_h.at[:, columns], w.at[k], w_sems.at[k]))
-    for load in loads:
-        load.start()
-    for load in loads[:2]:
-        load.wait()
-
-    def columns(k):
-        loads[2 + k].wait()
-        return w.at[k]
-
-    kernel(x, columns, *refs[:-4])
-
-
-def far_kernel(x, columns, up, down, far_up, far_down):
-    half = x.shape[0] // 2
-    above, below = pair_product(x, columns(0), columns(1))
-    put_coded(up, above)
-    put_coded(down, below)
-    far = product(x, columns(2))
-    put_coded(far_up, far[:half])
-    put_coded(far_down, far[half:])
-
-
-def near_kernel(x, columns, up, down, next_up, next_down, own):
-    above, below = pair_product(x, columns(0), columns(1))
-    put_coded(up, above)
-    put_coded(down, below)
-    next_up[...], next_down[...] = pair_product(x, columns(2), columns(3))
-    own[...] = product(x, columns(4))
-
-
-def products(kernel, x, w, me, steps, outs):
+    for c in range(CHUNKS):
+        chunk = pl.ds(c * depth, depth)
+        group = [pltpu.make_async_copy(x_h.at[:, chunk], x.at[:, chunk], x_sems.at[c])]
+        for k, step in enumerate(steps):
+            block = lax.rem(me[0] + step, w_h.shape[1] // part)
+            columns = pl.ds(pl.multiple_of(block * part, part), part)
+            group.append(
+                pltpu.make_async_copy(w_h.at[chunk, columns], w.at[k, chunk], w_sems.at[c, k])
+            )
+        loads.append(group)
+        for load in group:
+            load.start()
+    for c in range(CHUNKS):
+        chunk = slice(c * depth, (c + 1) * depth)
+        for load in loads[c]:
+            load.wait()
+        for group in groups:
+            columns = jnp.concatenate([w[k, chunk, :] for k in group], axis=1)
+            value = jnp.dot(x[:, chunk], columns, preferred_element_type=jnp.float32)
+            for i, k in enumerate(group):
+                share = value[:, i * part : (i + 1) * part]
+                totals[k] = share if c == 0 else totals[k] + share
+    kernel(totals, *refs[:-5])
+
+
+def far_kernel(totals, up, down, far_up, far_down):
+    half = totals.shape[1] // 2
+    put_coded(up, totals[0])
+    put_coded(down, totals[1])
+    put_coded(far_up, totals[2, :half])
+    put_coded(far_down, totals[2, half:])
+
+
+def near_kernel(totals, up, down, next_up, next_down, own):
+    put_coded(up, totals[0])
+    put_coded(down, totals[1])
+    next_up[...] = totals[2]
+    next_down[...] = totals[3]
+    own[...] = totals[4]
+
+
+def products(kernel, x, w, me, groups, outs):
     rows, depth = x.shape
+    steps = [step for group in groups for step in group]
     count = len(steps)
     part = w.shape[1] // 8
+    places, at = [], 0
+    for group in groups:
+        places.append(tuple(range(at, at + len(group))))
+        at += len(group)
     anywhere = pl.BlockSpec(memory_space=pl.ANY)
     return pl.pallas_call(
-        functools.partial(loading, steps, kernel),
+        functools.partial(loading, steps, places, kernel),
         out_shape=outs,
         in_specs=[pl.BlockSpec(memory_space=pltpu.SMEM), anywhere, anywhere],
         out_specs=[pl.BlockSpec(memory_space=pltpu.VMEM)] * len(outs),
         scratch_shapes=[
             pltpu.VMEM((rows, depth), x.dtype),
             pltpu.VMEM((count, depth, part), w.dtype),
-            pltpu.SemaphoreType.DMA((2,)),
-            pltpu.SemaphoreType.DMA((count,)),
+            pltpu.VMEM((count, rows, part), jnp.float32),
+            pltpu.SemaphoreType.DMA((CHUNKS,)),
+            pltpu.SemaphoreType.DMA((CHUNKS, count)),
         ],
         compiler_params=pltpu.CompilerParams(vmem_limit_bytes=52 * 2**20),
         cost_estimate=pl.CostEstimate(
@@ -275,13 +291,13 @@
     )
     mine = lax.all_to_all(spread, CHIPS, split_axis=0, concat_axis=0, tiled=True)
     q3, q5, q4a, q4b = products(
-        far_kernel, branch_rows, old_weights, me, (3, 5, 4),
+        far_kernel, branch_rows, old_weights, me, ((3, 5), (4,)),
         [code(count), code(count), code(count // 2), code(count // 2)],
     )
     r3, r5 = along_tp(q3, 1), along_tp(q5, -1)
     r4a, r4b = along_tp(q4a, 2), along_tp(q4b, -2)
     q1, q7, p2, p6, p0 = products(
-        near_kernel, branch_rows, old_weights, me, (1, 7, 2, 6, 0),
+        near_kernel, branch_rows, old_weights, me, ((1, 7), (2, 6), (0,)),
         [code(count), code(count), full, full, full],
     )
     r1, r7 = along_tp(q1, 1), along_tp(q7, -1)
@@ -293,10 +309,10 @@
     selector = local_call(
         selector_kernel, jax.ShapeDtypeStruct((places, count), jnp.bfloat16), assignment.reshape(1, count)
     )
+    mine = lax.optimization_barrier((mine, r1, r7, r2, r6))[0]
     placed = local_call(
         final_kernel, jax.ShapeDtypeStruct((places, part), jnp.bfloat16), p0, r1, r7, r2, r6, selector
     )
-    mine, _ = lax.optimization_barrier((mine, placed))
     placed = placed.reshape(replicas, slots_each, part)
     arrived = lax.all_to_all(placed, PLANE, split_axis=0, concat_axis=0, tiled=True)
     other = lax.ppermute(mine, "core", [(0, 1), (1, 0)])

time: 65.1 us -> 63.8 us (0.980)
  waiting for transfers between devices: 8.18 us -> 10.1 us
  Pallas kernels: 21.2 us -> 19.3 us
  starting transfers between devices: 33.2 us -> 32 us
    pallas_call x3, Pallas kernels: 13.4 us -> 11.5 us  [the longest x2 8.28 us: products(): pl.pallas_call(functools.partial(loading, steps, places, kernel), out_sha...]
    all_to_all x1, waiting for transfers between devices: 0.01 us -> 1.22 us  [local(): lax.all_to_all(spread, CHIPS, split_axis=0, concat_axis=0, tiled=True)]
    all_to_all x1, starting transfers between devices: 7.4 us -> 6.56 us  [local(): lax.all_to_all(placed, PLANE, split_axis=0, concat_axis=0, tiled=True)]
    ppermute x8, waiting for transfers between devices: 4.77 us -> 5.44 us  [along_tp(): lax.ppermute(value, 'tp', [(i, (i + step) % size) for i in range(size)])]
  transfers between devices with their start and end apart: 11 -> 11, of which waited for: 2 -> 3; matrix products, arithmetic and copies ran while one was open for 0% -> 0% of each run, Pallas kernels for 28% -> 25%
where the time goes in v8:
time: 63.8 us; the launch traced here: 63.5 us
  starting transfers between devices  32 us (50%)
  Pallas kernels  19.3 us (30%)
  waiting for transfers between devices  10.1 us (16%)
  between operations  1.38 us (2%)
  local copies, waits for them, and re-layouts  0.71 us (1%)
    ppermute x8, starting transfers between devices, along_tp(): lax.ppermute(value, 'tp', [(i, (i + step) % size) for i in range(size)])  15.7 us
    pallas_call x2, Pallas kernels, products(): pl.pallas_call(functools.partial(loading, steps, places, kernel), out_sha...  8.28 us
    all_to_all x1, starting transfers between devices, local(): lax.all_to_all(spread, CHIPS, split_axis=0, concat_axis=0, tiled=True)  7.6 us
    all_to_all x1, starting transfers between devices, local(): lax.all_to_all(placed, PLANE, split_axis=0, concat_axis=0, tiled=True)  6.56 us
    pallas_call x2, Pallas kernels, set_half(): pl.pallas_call(half_kernel, out_shape=jax.ShapeDtypeStruct((lanes, 2, row...  5.64 us
    ppermute x8, waiting for transfers between devices, along_tp(): lax.ppermute(value, 'tp', [(i, (i + step) % size) for i in range(size)])  5.44 us
    all_to_all x1, waiting for transfers between devices, local(): lax.all_to_all(placed, PLANE, split_axis=0, concat_axis=0, tiled=True)  3.41 us
    pallas_call x1, Pallas kernels, updated(): pl.pallas_call(update_kernel, out_shape=outs, in_specs=[anywhere] * 5, ou...  3.17 us
  transfers between devices with their start and end apart: 11, of which 3 were waited for; matrix products, arithmetic and copies ran while one was open for 0% of the time, Pallas kernels for 25%

profile of v8, /device:TPU:1, one launch (start us, length us, event | category | flops | bytes accessed | tf_op | source)
XLA Modules:
  0.0 63.5 jit_solution(18140509815647128391)
XLA Ops:
  1.3 3.2 %shard_map.119 = (f32[64,1024]{1,0:T(8,128)}, f32[64,1024]{1,0:T(8,128)}, f32[64,1024]{1,0:T(8,128)}, bf16[16,64,1024]{2,1,0:T(8,128)(2,1)}) custom-call(s32[1,1]{1,0:T(1,128)} %bitcast.9.step_h, f32[64,1024]{1,0:T(8,128)} %master_h.1, f32[64,1024]{1,0:T(8,128)} %moment_h.1, f32[64,1024]{1,0:T(8,128)} %second_h.1, f32[64,1024]{1,0:T(8,128)} %gradient_h.1), custom_call_target="tpu_custom_call" | custom-call | flops 1966080 | bytes 3932160 | tf_op jit(solution)/shard_map/pallas_call | solution.py:111
  4.5 7.6 %all-to-all-start = ((bf16[16,64,1024]{2,1,0:T(8,128)(2,1)}), bf16[16,64,1024]{2,1,0:T(8,128)(2,1)S(1)}, u32[]{:S(2)}, u32[]{:S(2)}) async-start(bf16[16,64,1024]{2,1,0:T(8,128)(2,1)} %get-tuple-element.26), calls=%async_computation | async-start | bytes 4194304 | tf_op jit(solution)/shard_map/all_to_all | solution.py:292
  12.1 3.2 %shard_map.121 = (s16[528,128]{1,0:T(8,128)(2,1)S(1)}, s16[528,128]{1,0:T(8,128)(2,1)S(1)}, s16[272,128]{1,0:T(8,128)(2,1)S(1)}, s16[272,128]{1,0:T(8,128)(2,1)S(1)}) custom-call(s32[1]{0:T(128)} %bitcast.2.me, bf16[512,2048]{1,0:T(8,128)(2,1)} %x_h.3, bf16[2048,1024]{1,0:T(8,128)(2,1)} %w_h.3), custom_call_target="tpu_custom_call" | custom-call | flops 805306368 | bytes 3670016 | tf_op jit(solution)/shard_map/pallas_call | solution.py:188
  15.3 1.7 %collective-permute-start.2 = (s16[528,128]{1,0:T(8,128)(2,1)S(1)}, s16[528,128]{1,0:T(8,128)(2,1)S(1)}, u32[]{:S(2)}, u32[]{:S(2)}) collective-permute-start(s16[528,128]{1,0:T(8,128)(2,1)S(1)} %get-tuple-element.30), channel_id=1, source_target_pairs={{0,1},{1,2},{2,3},{3,4},{4,5},{5,6},{6,7},{7,0},{8,9},{9,10},{10,1... | collective-permute-start | bytes 405512 | tf_op jit(solution)/shard_map/ppermute | solution.py:277
  17.0 4.0 %collective-permute-start.4 = (s16[528,128]{1,0:T(8,128)(2,1)S(1)}, s16[528,128]{1,0:T(8,128)(2,1)S(1)}, u32[]{:S(2)}, u32[]{:S(2)}) collective-permute-start(s16[528,128]{1,0:T(8,128)(2,1)S(1)} %get-tuple-element.33), channel_id=1, source_target_pairs={{0,7},{1,0},{2,1},{3,2},{4,3},{5,4},{6,5},{7,6},{8,15},{9,8},{10,9... | collective-permute-start | bytes 405512 | tf_op jit(solution)/shard_map/ppermute | solution.py:277
  21.0 0.0 collective-permute-start.3
  21.1 0.0 copy-start
  21.1 3.6 %collective-permute-start.5 = (s16[272,128]{1,0:T(8,128)(2,1)S(1)}, s16[272,128]{1,0:T(8,128)(2,1)S(1)}, u32[]{:S(2)}, u32[]{:S(2)}) collective-permute-start(s16[272,128]{1,0:T(8,128)(2,1)S(1)} %get-tuple-element.34), channel_id=1, source_target_pairs={{0,6},{1,7},{2,0},{3,1},{4,2},{5,3},{6,4},{7,5},{8,14},{9,15},{10,... | collective-permute-start | bytes 208904 | tf_op jit(solution)/shard_map/ppermute | solution.py:277
  24.6 5.0 %shard_map.120 = (s16[528,128]{1,0:T(8,128)(2,1)S(1)}, s16[528,128]{1,0:T(8,128)(2,1)S(1)}, f32[512,128]{1,0:T(8,128)S(1)}, f32[512,128]{1,0:T(8,128)S(1)}, f32[512,128]{1,0:T(8,128)S(1)}) custom-call(s32[1]{0:T(128)} %bitcast.2.me, bf16[512,2048]{1,0:T(8,128)(2,1)} %x_h.3, bf16[2048,1024]{1,0:T(8,128)(2,1)} %w_h.3), custom_call_target="tpu_custom_call" | custom-call | flops 1342177280 | bytes 4718592 | tf_op jit(solution)/shard_map/pallas_call | solution.py:188
  29.7 0.1 collective-permute-start
  29.8 0.0 collective-permute-done.3.far_a
  29.8 2.7 %collective-permute-start.1 = (s16[528,128]{1,0:T(8,128)(2,1)S(1)}, s16[528,128]{1,0:T(8,128)(2,1)S(1)}, u32[]{:S(2)}, u32[]{:S(2)}) collective-permute-start(s16[528,128]{1,0:T(8,128)(2,1)S(1)} %get-tuple-element.28), channel_id=1, source_target_pairs={{0,7},{1,0},{2,1},{3,2},{4,3},{5,4},{6,5},{7,6},{8,15},{9,8},{10,9... | collective-permute-start | bytes 405512 | tf_op jit(solution)/shard_map/ppermute | solution.py:277
  32.4 0.0 collective-permute-done.5.far_b
  32.4 0.0 collective-permute-done.2.next_a
  32.4 0.0 collective-permute-done.4.next_b
  32.5 0.3 shard_map.122
  32.7 0.1 collective-permute-start.6
  32.8 3.6 %collective-permute-start.7 = (s16[528,128]{1,0:T(8,128)(2,1)S(1)}, s16[528,128]{1,0:T(8,128)(2,1)S(1)}, u32[]{:S(2)}, u32[]{:S(2)}) collective-permute-start(s16[528,128]{1,0:T(8,128)(2,1)S(1)} %get-tuple-element.36), channel_id=1, source_target_pairs={{0,6},{1,7},{2,0},{3,1},{4,2},{5,3},{6,4},{7,5},{8,14},{9,15},{10,... | collective-permute-start | bytes 405512 | tf_op jit(solution)/shard_map/ppermute | solution.py:277
  36.4 0.0 collective-permute-done.ra
  36.4 0.0 collective-permute-done.1.rb
  36.4 5.4 %collective-permute-done.6.rc = s16[528,128]{1,0:T(8,128)(2,1)S(1)} collective-permute-done((s16[528,128]{1,0:T(8,128)(2,1)S(1)}, s16[528,128]{1,0:T(8,128)(2,1)S(1)}, u32[]{:S(2)}, u32[]{:S(2)}) %collective-permute-start.6) | collective-permute-done | bytes 135200 | tf_op jit(solution)/shard_map/ppermute | solution.py:277
  41.8 0.0 collective-permute-done.7.rd
  41.8 1.2 %all-to-all-done = bf16[16,64,1024]{2,1,0:T(8,128)(2,1)S(1)} async-done(((bf16[16,64,1024]{2,1,0:T(8,128)(2,1)}), bf16[16,64,1024]{2,1,0:T(8,128)(2,1)S(1)}, u32[]{:S(2)}, u32[]{:S(2)}) %all-to-all-start) | async-done | bytes 2097184 | tf_op jit(solution)/shard_map/all_to_all | solution.py:292
  43.0 2.2 %collective-permute-start.8 = (bf16[16,64,1024]{2,1,0:T(8,128)(2,1)S(1)}, bf16[16,64,1024]{2,1,0:T(8,128)(2,1)}, u32[]{:S(2)}, u32[]{:S(2)}) collective-permute-start(bf16[16,64,1024]{2,1,0:T(8,128)(2,1)S(1)} %all-to-all-done), channel_id=1, source_target_pairs={{0,64},{64,0},{1,65},{65,1},{2,66},{66,2},{3,67},{67,3},{4,68},{68... | collective-permute-start | bytes 6291464 | tf_op jit(solution)/shard_map/ppermute | solution.py:318
  45.2 0.0 copy-done
  45.2 0.6 %shard_map.125.selector = bf16[1024,512]{1,0:T(8,128)(2,1)S(1)} custom-call(s32[1,512]{1,0:T(1,128)S(1)} %bitcast.11), custom_call_target="tpu_custom_call" | custom-call | bytes 1048576 | tf_op jit(solution)/shard_map/pallas_call | solution.py:210
  45.9 1.3 %shard_map.126 = bf16[1024,128]{1,0:T(8,128)(2,1)} custom-call(f32[512,128]{1,0:T(8,128)S(1)} %get-tuple-element.38.own, s16[528,128]{1,0:T(8,128)(2,1)S(1)} %collective-permute-done.ra, s16[528,128]{1,0:T(8,128)(2,1)S(1)} %collective-permute-done.1.rb, s16[528,128]{1,0:T(8,128)(2,1)S(1)} %collective-permute-done.6.rc, ...), custom_call_target="tpu_custom_call" | custom-call | bytes 1048576 | tf_op jit(solution)/shard_map/pallas_call | solution.py:210
  47.2 6.6 %all-to-all-start.1 = ((bf16[32,32,128]{2,1,0:T(8,128)(2,1)}), bf16[32,32,128]{2,1,0:T(8,128)(2,1)S(1)}, u32[]{:S(2)}, u32[]{:S(2)}) async-start(bf16[32,32,128]{2,1,0:T(8,128)(2,1)} %bitcast.6), calls=%async_computation.1 | async-start | bytes 524288 | tf_op jit(solution)/shard_map/all_to_all | solution.py:317
  53.7 1.9 %shard_map.123.refs_0_ = bf16[2,2,512,1024]{3,2,1,0:T(8,128)(2,1)} custom-call(s32[1]{0:T(128)} %bitcast.1.place, bf16[2,512,1024]{2,1,0:T(8,128)(2,1)S(1)} %bitcast.10), custom_call_target="tpu_custom_call" | custom-call | bytes 4194304 | tf_op jit(solution)/shard_map/pallas_call | solution.py:259
  55.6 0.0 collective-permute-done.8
  55.6 3.8 %shard_map.124 = bf16[2,2,512,1024]{3,2,1,0:T(8,128)(2,1)} custom-call(s32[1]{0:T(128)S(6)} %sub.3.place, bf16[2,512,1024]{2,1,0:T(8,128)(2,1)} %bitcast.3.half, bf16[2,2,512,1024]{3,2,1,0:T(8,128)(2,1)} %shard_map.123.refs_0_), custom_call_target="tpu_custom_call", output_to_operand_aliasing={{}: (2, {})} | custom-call | bytes 4194304 | tf_op jit(solution)/shard_map/pallas_call | solution.py:259
  59.4 3.4 %all-to-all-done.1 = bf16[32,32,128]{2,1,0:T(8,128)(2,1)S(1)} async-done(((bf16[32,32,128]{2,1,0:T(8,128)(2,1)}), bf16[32,32,128]{2,1,0:T(8,128)(2,1)S(1)}, u32[]{:S(2)}, u32[]{:S(2)}) %all-to-all-start.1) | async-done | bytes 262176 | tf_op jit(solution)/shard_map/all_to_all | solution.py:317
  62.8 0.7 %copy.17 = bf16[1,32,32,128]{3,2,1,0:T(8,128)(2,1)} copy(bf16[1,32,32,128]{3,2,1,0:T(8,128)(2,1)S(1)} %bitcast.13) | data formatting | bytes 524288
Async XLA Ops:
  4.5 38.6 %all-to-all-start = ((bf16[16,64,1024]{2,1,0:T(8,128)(2,1)}), bf16[16,64,1024]{2,1,0:T(8,128)(2,1)S(1)}, u32[]{:S(2)}, u32[]{:S(2)}) async-start(bf16[16,64,1024]{2,1,0:T(8,128)(2,1)} %get-tuple-element.26), calls=%async_computation | async-start | bytes 4194304 | tf_op jit(solution)/shard_map/all_to_all | solution.py:292
  15.3 17.1 %collective-permute-start.2 = (s16[528,128]{1,0:T(8,128)(2,1)S(1)}, s16[528,128]{1,0:T(8,128)(2,1)S(1)}, u32[]{:S(2)}, u32[]{:S(2)}) collective-permute-start(s16[528,128]{1,0:T(8,128)(2,1)S(1)} %get-tuple-element.30), channel_id=1, source_target_pairs={{0,1},{1,2},{2,3},{3,4},{4,5},{5,6},{6,7},{7,0},{8,9},{9,10},{10,1... | collective-permute-start | bytes 405512 | tf_op jit(solution)/shard_map/ppermute | solution.py:277
  17.0 15.4 %collective-permute-start.4 = (s16[528,128]{1,0:T(8,128)(2,1)S(1)}, s16[528,128]{1,0:T(8,128)(2,1)S(1)}, u32[]{:S(2)}, u32[]{:S(2)}) collective-permute-start(s16[528,128]{1,0:T(8,128)(2,1)S(1)} %get-tuple-element.33), channel_id=1, source_target_pairs={{0,7},{1,0},{2,1},{3,2},{4,3},{5,4},{6,5},{7,6},{8,15},{9,8},{10,9... | collective-permute-start | bytes 405512 | tf_op jit(solution)/shard_map/ppermute | solution.py:277
  21.0 8.7 %collective-permute-start.3 = (s16[272,128]{1,0:T(8,128)(2,1)S(1)}, s16[272,128]{1,0:T(8,128)(2,1)S(1)}, u32[]{:S(2)}, u32[]{:S(2)}) collective-permute-start(s16[272,128]{1,0:T(8,128)(2,1)S(1)} %get-tuple-element.31), channel_id=1, source_target_pairs={{0,2},{1,3},{2,4},{3,5},{4,6},{5,7},{6,0},{7,1},{8,10},{9,11},{10,... | collective-permute-start | bytes 208904 | tf_op jit(solution)/shard_map/ppermute | solution.py:277
  21.1 24.2 %copy-start = (s32[512,1]{0,1:T(1,128)S(1)}, s32[512,1]{0,1:T(1,128)}, u32[]{:S(2)}) copy-start(s32[512,1]{0,1:T(1,128)} %param.15) | copy-start | bytes 6148
  21.1 11.4 %collective-permute-start.5 = (s16[272,128]{1,0:T(8,128)(2,1)S(1)}, s16[272,128]{1,0:T(8,128)(2,1)S(1)}, u32[]{:S(2)}, u32[]{:S(2)}) collective-permute-start(s16[272,128]{1,0:T(8,128)(2,1)S(1)} %get-tuple-element.34), channel_id=1, source_target_pairs={{0,6},{1,7},{2,0},{3,1},{4,2},{5,3},{6,4},{7,5},{8,14},{9,15},{10,... | collective-permute-start | bytes 208904 | tf_op jit(solution)/shard_map/ppermute | solution.py:277
  29.7 6.7 %collective-permute-start = (s16[528,128]{1,0:T(8,128)(2,1)S(1)}, s16[528,128]{1,0:T(8,128)(2,1)S(1)}, u32[]{:S(2)}, u32[]{:S(2)}) collective-permute-start(s16[528,128]{1,0:T(8,128)(2,1)S(1)} %get-tuple-element.27), channel_id=1, source_target_pairs={{0,1},{1,2},{2,3},{3,4},{4,5},{5,6},{6,7},{7,0},{8,9},{9,10},{10,1... | collective-permute-start | bytes 405512 | tf_op jit(solution)/shard_map/ppermute | solution.py:277
  29.8 6.6 %collective-permute-start.1 = (s16[528,128]{1,0:T(8,128)(2,1)S(1)}, s16[528,128]{1,0:T(8,128)(2,1)S(1)}, u32[]{:S(2)}, u32[]{:S(2)}) collective-permute-start(s16[528,128]{1,0:T(8,128)(2,1)S(1)} %get-tuple-element.28), channel_id=1, source_target_pairs={{0,7},{1,0},{2,1},{3,2},{4,3},{5,4},{6,5},{7,6},{8,15},{9,8},{10,9... | collective-permute-start | bytes 405512 | tf_op jit(solution)/shard_map/ppermute | solution.py:277
  32.7 9.1 %collective-permute-start.6 = (s16[528,128]{1,0:T(8,128)(2,1)S(1)}, s16[528,128]{1,0:T(8,128)(2,1)S(1)}, u32[]{:S(2)}, u32[]{:S(2)}) collective-permute-start(s16[528,128]{1,0:T(8,128)(2,1)S(1)} %get-tuple-element.35), channel_id=1, source_target_pairs={{0,2},{1,3},{2,4},{3,5},{4,6},{5,7},{6,0},{7,1},{8,10},{9,11},{10,... | collective-permute-start | bytes 405512 | tf_op jit(solution)/shard_map/ppermute | solution.py:277
  32.8 9.0 %collective-permute-start.7 = (s16[528,128]{1,0:T(8,128)(2,1)S(1)}, s16[528,128]{1,0:T(8,128)(2,1)S(1)}, u32[]{:S(2)}, u32[]{:S(2)}) collective-permute-start(s16[528,128]{1,0:T(8,128)(2,1)S(1)} %get-tuple-element.36), channel_id=1, source_target_pairs={{0,6},{1,7},{2,0},{3,1},{4,2},{5,3},{6,4},{7,5},{8,14},{9,15},{10,... | collective-permute-start | bytes 405512 | tf_op jit(solution)/shard_map/ppermute | solution.py:277
  43.0 12.5 %collective-permute-start.8 = (bf16[16,64,1024]{2,1,0:T(8,128)(2,1)S(1)}, bf16[16,64,1024]{2,1,0:T(8,128)(2,1)}, u32[]{:S(2)}, u32[]{:S(2)}) collective-permute-start(bf16[16,64,1024]{2,1,0:T(8,128)(2,1)S(1)} %all-to-all-done), channel_id=1, source_target_pairs={{0,64},{64,0},{1,65},{65,1},{2,66},{66,2},{3,67},{67,3},{4,68},{68... | collective-permute-start | bytes 6291464 | tf_op jit(solution)/shard_map/ppermute | solution.py:318
  47.2 15.6 %all-to-all-start.1 = ((bf16[32,32,128]{2,1,0:T(8,128)(2,1)}), bf16[32,32,128]{2,1,0:T(8,128)(2,1)S(1)}, u32[]{:S(2)}, u32[]{:S(2)}) async-start(bf16[32,32,128]{2,1,0:T(8,128)(2,1)} %bitcast.6), calls=%async_computation.1 | async-start | bytes 524288 | tf_op jit(solution)/shard_map/all_to_all | solution.py:317

commit v9 on v8

--- a/solution.py
+++ b/solution.py
@@ -159,20 +159,17 @@
     kernel(totals, *refs[:-5])
 
 
-def far_kernel(totals, up, down, far_up, far_down):
+def products_kernel(totals, up, down, far_up, far_down, next_up, next_down, two_up, two_down, own):
     half = totals.shape[1] // 2
     put_coded(up, totals[0])
     put_coded(down, totals[1])
     put_coded(far_up, totals[2, :half])
     put_coded(far_down, totals[2, half:])
-
-
-def near_kernel(totals, up, down, next_up, next_down, own):
-    put_coded(up, totals[0])
-    put_coded(down, totals[1])
-    next_up[...] = totals[2]
-    next_down[...] = totals[3]
-    own[...] = totals[4]
+    own[...] = totals[3]
+    two_up[...] = totals[4]
+    two_down[...] = totals[5]
+    put_coded(next_up, totals[6])
+    put_coded(next_down, totals[7])
 
 
 def products(kernel, x, w, me, groups, outs):
@@ -290,16 +287,12 @@
         step_count, master, moment, second, gradient, chips
     )
     mine = lax.all_to_all(spread, CHIPS, split_axis=0, concat_axis=0, tiled=True)
-    q3, q5, q4a, q4b = products(
-        far_kernel, branch_rows, old_weights, me, ((3, 5), (4,)),
-        [code(count), code(count), code(count // 2), code(count // 2)],
+    q3, q5, q4a, q4b, q1, q7, p2, p6, p0 = products(
+        products_kernel, branch_rows, old_weights, me, ((3, 5), (4, 0), (2, 6), (1, 7)),
+        [code(count)] * 2 + [code(count // 2)] * 2 + [code(count)] * 2 + [full] * 3,
     )
     r3, r5 = along_tp(q3, 1), along_tp(q5, -1)
     r4a, r4b = along_tp(q4a, 2), along_tp(q4b, -2)
-    q1, q7, p2, p6, p0 = products(
-        near_kernel, branch_rows, old_weights, me, ((1, 7), (2, 6), (0,)),
-        [code(count), code(count), full, full, full],
-    )
     r1, r7 = along_tp(q1, 1), along_tp(q7, -1)
     q2, q6 = local_call(merge_kernel, [code(count), code(count)], p2, r3, r4a, p6, r5, r4b)
     r2, r6 = along_tp(q2, 2), along_tp(q6, -2)
@@ -309,10 +302,10 @@
     selector = local_call(
         selector_kernel, jax.ShapeDtypeStruct((places, count), jnp.bfloat16), assignment.reshape(1, count)
     )
-    mine = lax.optimization_barrier((mine, r1, r7, r2, r6))[0]
     placed = local_call(
         final_kernel, jax.ShapeDtypeStruct((places, part), jnp.bfloat16), p0, r1, r7, r2, r6, selector
     )
+    mine = lax.optimization_barrier((mine, placed))[0]
     placed = placed.reshape(replicas, slots_each, part)
     arrived = lax.all_to_all(placed, PLANE, split_axis=0, concat_axis=0, tiled=True)
     other = lax.ppermute(mine, "core", [(0, 1), (1, 0)])

time: 63.8 us -> 62.8 us (0.984)
  waiting for transfers between devices: 10.1 us -> 13 us
  Pallas kernels: 19.3 us -> 16.6 us
  starting transfers between devices: 32 us -> 30.8 us
    pallas_call x2 -> x1, Pallas kernels: 8.28 us -> 5.53 us  [products(): pl.pallas_call(functools.partial(loading, steps, places, kernel), out_sha...]
    ppermute x8, starting transfers between devices: 15.7 us -> 13.5 us  [along_tp(): lax.ppermute(value, 'tp', [(i, (i + step) % size) for i in range(size)])]
    ppermute x8, waiting for transfers between devices: 5.44 us -> 7.58 us  [along_tp(): lax.ppermute(value, 'tp', [(i, (i + step) % size) for i in range(size)])]
    all_to_all x1, starting transfers between devices: 6.56 us -> 7.52 us  [local(): lax.all_to_all(placed, PLANE, split_axis=0, concat_axis=0, tiled=True)]
    all_to_all x1, waiting for transfers between devices: 1.22 us -> 2.05 us  [local(): lax.all_to_all(spread, CHIPS, split_axis=0, concat_axis=0, tiled=True)]
  transfers between devices with their start and end apart: 11 -> 11, of which waited for: 3 -> 5; matrix products, arithmetic and copies ran while one was open for 0% -> 0% of each run, Pallas kernels for 25% -> 21%
where the time goes in v9:
time: 62.8 us; the launch traced here: 62.5 us
  starting transfers between devices  30.8 us (49%)
  Pallas kernels  16.6 us (26%)
  waiting for transfers between devices  13 us (21%)
  between operations  1.37 us (2%)
  local copies, waits for them, and re-layouts  0.71 us (1%)
    ppermute x8, starting transfers between devices, along_tp(): lax.ppermute(value, 'tp', [(i, (i + step) % size) for i in range(size)])  13.5 us
    all_to_all x1, starting transfers between devices, local(): lax.all_to_all(spread, CHIPS, split_axis=0, concat_axis=0, tiled=True)  7.6 us
    ppermute x8, waiting for transfers between devices, along_tp(): lax.ppermute(value, 'tp', [(i, (i + step) % size) for i in range(size)])  7.58 us
    all_to_all x1, starting transfers between devices, local(): lax.all_to_all(placed, PLANE, split_axis=0, concat_axis=0, tiled=True)  7.52 us
    pallas_call x2, Pallas kernels, set_half(): pl.pallas_call(half_kernel, out_shape=jax.ShapeDtypeStruct((lanes, 2, row...  5.64 us
    pallas_call x1, Pallas kernels, products(): pl.pallas_call(functools.partial(loading, steps, places, kernel), out_sha...  5.53 us
    all_to_all x1, waiting for transfers between devices, local(): lax.all_to_all(placed, PLANE, split_axis=0, concat_axis=0, tiled=True)  3.41 us
    pallas_call x1, Pallas kernels, updated(): pl.pallas_call(update_kernel, out_shape=outs, in_specs=[anywhere] * 5, ou...  3.17 us
  transfers between devices with their start and end apart: 11, of which 5 were waited for; matrix products, arithmetic and copies ran while one was open for 0% of the time, Pallas kernels for 21%

profile of v9, /device:TPU:1, one launch (start us, length us, event | category | flops | bytes accessed | tf_op | source)
XLA Modules:
  0.0 62.5 jit_solution(10641301580620488985)
XLA Ops:
  1.3 3.2 %shard_map.119 = (f32[64,1024]{1,0:T(8,128)}, f32[64,1024]{1,0:T(8,128)}, f32[64,1024]{1,0:T(8,128)}, bf16[16,64,1024]{2,1,0:T(8,128)(2,1)}) custom-call(s32[1,1]{1,0:T(1,128)} %bitcast.9.step_h, f32[64,1024]{1,0:T(8,128)} %master_h.1, f32[64,1024]{1,0:T(8,128)} %moment_h.1, f32[64,1024]{1,0:T(8,128)} %second_h.1, f32[64,1024]{1,0:T(8,128)} %gradient_h.1), custom_call_target="tpu_custom_call" | custom-call | flops 1966080 | bytes 3932160 | tf_op jit(solution)/shard_map/pallas_call | solution.py:111
  4.5 7.6 %all-to-all-start = ((bf16[16,64,1024]{2,1,0:T(8,128)(2,1)}), bf16[16,64,1024]{2,1,0:T(8,128)(2,1)S(1)}, u32[]{:S(2)}, u32[]{:S(2)}) async-start(bf16[16,64,1024]{2,1,0:T(8,128)(2,1)} %get-tuple-element.26), calls=%async_computation | async-start | bytes 4194304 | tf_op jit(solution)/shard_map/all_to_all | solution.py:289
  12.1 0.0 copy-start
  12.1 5.5 %shard_map.120 = (s16[528,128]{1,0:T(8,128)(2,1)S(1)}, s16[528,128]{1,0:T(8,128)(2,1)S(1)}, s16[272,128]{1,0:T(8,128)(2,1)S(1)}, s16[272,128]{1,0:T(8,128)(2,1)S...) custom-call(s32[1]{0:T(128)} %bitcast.2.me, ...), custom_call_target="tpu_custom_call" | custom-call | flops 2147483648 | bytes 6291456 | tf_op jit(solution)/shard_map/pallas_call | solution.py:185
  17.6 1.7 %collective-permute-start.2 = (s16[528,128]{1,0:T(8,128)(2,1)S(1)}, s16[528,128]{1,0:T(8,128)(2,1)S(1)}, u32[]{:S(2)}, u32[]{:S(2)}) collective-permute-start(s16[528,128]{1,0:T(8,128)(2,1)S(1)} %get-tuple-element.31), channel_id=1, source_target_pairs={{0,1},{1,2},{2,3},{3,4},{4,5},{5,6},{6,7},{7,0},{8,9},{9,10},{10,1... | collective-permute-start | bytes 405512 | tf_op jit(solution)/shard_map/ppermute | solution.py:274
  19.3 4.0 %collective-permute-start.4 = (s16[528,128]{1,0:T(8,128)(2,1)S(1)}, s16[528,128]{1,0:T(8,128)(2,1)S(1)}, u32[]{:S(2)}, u32[]{:S(2)}) collective-permute-start(s16[528,128]{1,0:T(8,128)(2,1)S(1)} %get-tuple-element.34), channel_id=1, source_target_pairs={{0,7},{1,0},{2,1},{3,2},{4,3},{5,4},{6,5},{7,6},{8,15},{9,8},{10,9... | collective-permute-start | bytes 405512 | tf_op jit(solution)/shard_map/ppermute | solution.py:274
  23.4 0.0 collective-permute-start.3
  23.4 3.6 %collective-permute-start.5 = (s16[272,128]{1,0:T(8,128)(2,1)S(1)}, s16[272,128]{1,0:T(8,128)(2,1)S(1)}, u32[]{:S(2)}, u32[]{:S(2)}) collective-permute-start(s16[272,128]{1,0:T(8,128)(2,1)S(1)} %get-tuple-element.35), channel_id=1, source_target_pairs={{0,6},{1,7},{2,0},{3,1},{4,2},{5,3},{6,4},{7,5},{8,14},{9,15},{10,... | collective-permute-start | bytes 208904 | tf_op jit(solution)/shard_map/ppermute | solution.py:274
  26.9 0.0 collective-permute-start
  26.9 3.0 %collective-permute-done.3.far_a = s16[272,128]{1,0:T(8,128)(2,1)S(1)} collective-permute-done((s16[272,128]{1,0:T(8,128)(2,1)S(1)}, s16[272,128]{1,0:T(8,128)(2,1)S(1)}, u32[]{:S(2)}, u32[]{:S(2)}) %collective-permute-start.3) | collective-permute-done | bytes 69664 | tf_op jit(solution)/shard_map/ppermute | solution.py:274
  29.9 0.6 collective-permute-start.1
  30.5 0.0 collective-permute-done.5.far_b
  30.5 0.0 collective-permute-done.2.next_a
  30.5 0.0 collective-permute-done.4.next_b
  30.5 0.3 shard_map.121
  30.8 3.0 %collective-permute-start.6 = (s16[528,128]{1,0:T(8,128)(2,1)S(1)}, s16[528,128]{1,0:T(8,128)(2,1)S(1)}, u32[]{:S(2)}, u32[]{:S(2)}) collective-permute-start(s16[528,128]{1,0:T(8,128)(2,1)S(1)} %get-tuple-element.36), channel_id=1, source_target_pairs={{0,2},{1,3},{2,4},{3,5},{4,6},{5,7},{6,0},{7,1},{8,10},{9,11},{10,... | collective-permute-start | bytes 405512 | tf_op jit(solution)/shard_map/ppermute | solution.py:274
  33.8 0.6 %collective-permute-start.7 = (s16[528,128]{1,0:T(8,128)(2,1)S(1)}, s16[528,128]{1,0:T(8,128)(2,1)S(1)}, u32[]{:S(2)}, u32[]{:S(2)}) collective-permute-start(s16[528,128]{1,0:T(8,128)(2,1)S(1)} %get-tuple-element.37), channel_id=1, source_target_pairs={{0,6},{1,7},{2,0},{3,1},{4,2},{5,3},{6,4},{7,5},{8,14},{9,15},{10,... | collective-permute-start | bytes 405512 | tf_op jit(solution)/shard_map/ppermute | solution.py:274
  34.5 0.0 copy-done
  34.5 0.6 %shard_map.122.selector = bf16[1024,512]{1,0:T(8,128)(2,1)S(1)} custom-call(s32[1,512]{1,0:T(1,128)S(1)} %bitcast.11), custom_call_target="tpu_custom_call" | custom-call | bytes 1048576 | tf_op jit(solution)/shard_map/pallas_call | solution.py:207
  35.1 0.0 collective-permute-done.ra
  35.1 0.0 collective-permute-done.1.rb
  35.1 2.6 %collective-permute-done.6.rc = s16[528,128]{1,0:T(8,128)(2,1)S(1)} collective-permute-done((s16[528,128]{1,0:T(8,128)(2,1)S(1)}, s16[528,128]{1,0:T(8,128)(2,1)S(1)}, u32[]{:S(2)}, u32[]{:S(2)}) %collective-permute-start.6) | collective-permute-done | bytes 135200 | tf_op jit(solution)/shard_map/ppermute | solution.py:274
  37.7 2.0 %collective-permute-done.7.rd = s16[528,128]{1,0:T(8,128)(2,1)S(1)} collective-permute-done((s16[528,128]{1,0:T(8,128)(2,1)S(1)}, s16[528,128]{1,0:T(8,128)(2,1)S(1)}, u32[]{:S(2)}, u32[]{:S(2)}) %collective-permute-start.7) | collective-permute-done | bytes 135200 | tf_op jit(solution)/shard_map/ppermute | solution.py:274
  39.7 1.3 %shard_map.123 = bf16[1024,128]{1,0:T(8,128)(2,1)} custom-call(f32[512,128]{1,0:T(8,128)S(1)} %get-tuple-element.27.own, s16[528,128]{1,0:T(8,128)(2,1)S(1)} %collective-permute-done.ra, s16[528,128]{1,0:T(8,128)(2,1)S(1)} %collective-permute-done.1.rb, s16[528,128]{1,0:T(8,128)(2,1)S(1)} %collective-permute-done.6.rc, ...), custom_call_target="tpu_custom_call" | custom-call | bytes 1048576 | tf_op jit(solution)/shard_map/pallas_call | solution.py:207
  41.0 2.1 %all-to-all-done = bf16[16,64,1024]{2,1,0:T(8,128)(2,1)S(1)} async-done(((bf16[16,64,1024]{2,1,0:T(8,128)(2,1)}), bf16[16,64,1024]{2,1,0:T(8,128)(2,1)S(1)}, u32[]{:S(2)}, u32[]{:S(2)}) %all-to-all-start) | async-done | bytes 2097184 | tf_op jit(solution)/shard_map/all_to_all | solution.py:289
  43.0 2.2 %collective-permute-start.8 = (bf16[16,64,1024]{2,1,0:T(8,128)(2,1)S(1)}, bf16[16,64,1024]{2,1,0:T(8,128)(2,1)}, u32[]{:S(2)}, u32[]{:S(2)}) collective-permute-start(bf16[16,64,1024]{2,1,0:T(8,128)(2,1)S(1)} %all-to-all-done), channel_id=1, source_target_pairs={{0,64},{64,0},{1,65},{65,1},{2,66},{66,2},{3,67},{67,3},{4,68},{68... | collective-permute-start | bytes 6291464 | tf_op jit(solution)/shard_map/ppermute | solution.py:311
  45.2 7.5 %all-to-all-start.1 = ((bf16[32,32,128]{2,1,0:T(8,128)(2,1)}), bf16[32,32,128]{2,1,0:T(8,128)(2,1)S(1)}, u32[]{:S(2)}, u32[]{:S(2)}) async-start(bf16[32,32,128]{2,1,0:T(8,128)(2,1)} %bitcast.6), calls=%async_computation.1 | async-start | bytes 524288 | tf_op jit(solution)/shard_map/all_to_all | solution.py:310
  52.7 1.9 %shard_map.124.refs_0_ = bf16[2,2,512,1024]{3,2,1,0:T(8,128)(2,1)} custom-call(s32[1]{0:T(128)} %bitcast.1.place, bf16[2,512,1024]{2,1,0:T(8,128)(2,1)S(1)} %bitcast.10), custom_call_target="tpu_custom_call" | custom-call | bytes 4194304 | tf_op jit(solution)/shard_map/pallas_call | solution.py:256
  54.6 0.0 collective-permute-done.8
  54.6 3.8 %shard_map.125 = bf16[2,2,512,1024]{3,2,1,0:T(8,128)(2,1)} custom-call(s32[1]{0:T(128)S(6)} %sub.3.place, bf16[2,512,1024]{2,1,0:T(8,128)(2,1)} %bitcast.4.half, bf16[2,2,512,1024]{3,2,1,0:T(8,128)(2,1)} %shard_map.124.refs_0_), custom_call_target="tpu_custom_call", output_to_operand_aliasing={{}: (2, {})} | custom-call | bytes 4194304 | tf_op jit(solution)/shard_map/pallas_call | solution.py:256
  58.4 3.4 %all-to-all-done.1 = bf16[32,32,128]{2,1,0:T(8,128)(2,1)S(1)} async-done(((bf16[32,32,128]{2,1,0:T(8,128)(2,1)}), bf16[32,32,128]{2,1,0:T(8,128)(2,1)S(1)}, u32[]{:S(2)}, u32[]{:S(2)}) %all-to-all-start.1) | async-done | bytes 262176 | tf_op jit(solution)/shard_map/all_to_all | solution.py:310
  61.8 0.7 %copy.17 = bf16[1,32,32,128]{3,2,1,0:T(8,128)(2,1)} copy(bf16[1,32,32,128]{3,2,1,0:T(8,128)(2,1)S(1)} %bitcast.13) | data formatting | bytes 524288
Async XLA Ops:
  4.5 38.6 %all-to-all-start = ((bf16[16,64,1024]{2,1,0:T(8,128)(2,1)}), bf16[16,64,1024]{2,1,0:T(8,128)(2,1)S(1)}, u32[]{:S(2)}, u32[]{:S(2)}) async-start(bf16[16,64,1024]{2,1,0:T(8,128)(2,1)} %get-tuple-element.26), calls=%async_computation | async-start | bytes 4194304 | tf_op jit(solution)/shard_map/all_to_all | solution.py:289
  12.1 22.4 %copy-start = (s32[512,1]{0,1:T(1,128)S(1)}, s32[512,1]{0,1:T(1,128)}, u32[]{:S(2)}) copy-start(s32[512,1]{0,1:T(1,128)} %param.15) | copy-start | bytes 6148
  17.6 12.9 %collective-permute-start.2 = (s16[528,128]{1,0:T(8,128)(2,1)S(1)}, s16[528,128]{1,0:T(8,128)(2,1)S(1)}, u32[]{:S(2)}, u32[]{:S(2)}) collective-permute-start(s16[528,128]{1,0:T(8,128)(2,1)S(1)} %get-tuple-element.31), channel_id=1, source_target_pairs={{0,1},{1,2},{2,3},{3,4},{4,5},{5,6},{6,7},{7,0},{8,9},{9,10},{10,1... | collective-permute-start | bytes 405512 | tf_op jit(solution)/shard_map/ppermute | solution.py:274
  19.3 11.2 %collective-permute-start.4 = (s16[528,128]{1,0:T(8,128)(2,1)S(1)}, s16[528,128]{1,0:T(8,128)(2,1)S(1)}, u32[]{:S(2)}, u32[]{:S(2)}) collective-permute-start(s16[528,128]{1,0:T(8,128)(2,1)S(1)} %get-tuple-element.34), channel_id=1, source_target_pairs={{0,7},{1,0},{2,1},{3,2},{4,3},{5,4},{6,5},{7,6},{8,15},{9,8},{10,9... | collective-permute-start | bytes 405512 | tf_op jit(solution)/shard_map/ppermute | solution.py:274
  23.4 6.6 %collective-permute-start.3 = (s16[272,128]{1,0:T(8,128)(2,1)S(1)}, s16[272,128]{1,0:T(8,128)(2,1)S(1)}, u32[]{:S(2)}, u32[]{:S(2)}) collective-permute-start(s16[272,128]{1,0:T(8,128)(2,1)S(1)} %get-tuple-element.32), channel_id=1, source_target_pairs={{0,2},{1,3},{2,4},{3,5},{4,6},{5,7},{6,0},{7,1},{8,10},{9,11},{10,... | collective-permute-start | bytes 208904 | tf_op jit(solution)/shard_map/ppermute | solution.py:274
  23.4 7.2 %collective-permute-start.5 = (s16[272,128]{1,0:T(8,128)(2,1)S(1)}, s16[272,128]{1,0:T(8,128)(2,1)S(1)}, u32[]{:S(2)}, u32[]{:S(2)}) collective-permute-start(s16[272,128]{1,0:T(8,128)(2,1)S(1)} %get-tuple-element.35), channel_id=1, source_target_pairs={{0,6},{1,7},{2,0},{3,1},{4,2},{5,3},{6,4},{7,5},{8,14},{9,15},{10,... | collective-permute-start | bytes 208904 | tf_op jit(solution)/shard_map/ppermute | solution.py:274
  26.9 8.2 %collective-permute-start = (s16[528,128]{1,0:T(8,128)(2,1)S(1)}, s16[528,128]{1,0:T(8,128)(2,1)S(1)}, u32[]{:S(2)}, u32[]{:S(2)}) collective-permute-start(s16[528,128]{1,0:T(8,128)(2,1)S(1)} %get-tuple-element.28), channel_id=1, source_target_pairs={{0,1},{1,2},{2,3},{3,4},{4,5},{5,6},{6,7},{7,0},{8,9},{9,10},{10,1... | collective-permute-start | bytes 405512 | tf_op jit(solution)/shard_map/ppermute | solution.py:274
  29.9 5.2 %collective-permute-start.1 = (s16[528,128]{1,0:T(8,128)(2,1)S(1)}, s16[528,128]{1,0:T(8,128)(2,1)S(1)}, u32[]{:S(2)}, u32[]{:S(2)}) collective-permute-start(s16[528,128]{1,0:T(8,128)(2,1)S(1)} %get-tuple-element.29), channel_id=1, source_target_pairs={{0,7},{1,0},{2,1},{3,2},{4,3},{5,4},{6,5},{7,6},{8,15},{9,8},{10,9... | collective-permute-start | bytes 405512 | tf_op jit(solution)/shard_map/ppermute | solution.py:274
  30.8 6.9 %collective-permute-start.6 = (s16[528,128]{1,0:T(8,128)(2,1)S(1)}, s16[528,128]{1,0:T(8,128)(2,1)S(1)}, u32[]{:S(2)}, u32[]{:S(2)}) collective-permute-start(s16[528,128]{1,0:T(8,128)(2,1)S(1)} %get-tuple-element.36), channel_id=1, source_target_pairs={{0,2},{1,3},{2,4},{3,5},{4,6},{5,7},{6,0},{7,1},{8,10},{9,11},{10,... | collective-permute-start | bytes 405512 | tf_op jit(solution)/shard_map/ppermute | solution.py:274
  33.8 5.9 %collective-permute-start.7 = (s16[528,128]{1,0:T(8,128)(2,1)S(1)}, s16[528,128]{1,0:T(8,128)(2,1)S(1)}, u32[]{:S(2)}, u32[]{:S(2)}) collective-permute-start(s16[528,128]{1,0:T(8,128)(2,1)S(1)} %get-tuple-element.37), channel_id=1, source_target_pairs={{0,6},{1,7},{2,0},{3,1},{4,2},{5,3},{6,4},{7,5},{8,14},{9,15},{10,... | collective-permute-start | bytes 405512 | tf_op jit(solution)/shard_map/ppermute | solution.py:274
  43.0 11.6 %collective-permute-start.8 = (bf16[16,64,1024]{2,1,0:T(8,128)(2,1)S(1)}, bf16[16,64,1024]{2,1,0:T(8,128)(2,1)}, u32[]{:S(2)}, u32[]{:S(2)}) collective-permute-start(bf16[16,64,1024]{2,1,0:T(8,128)(2,1)S(1)} %all-to-all-done), channel_id=1, source_target_pairs={{0,64},{64,0},{1,65},{65,1},{2,66},{66,2},{3,67},{67,3},{4,68},{68... | collective-permute-start | bytes 6291464 | tf_op jit(solution)/shard_map/ppermute | solution.py:311
  45.2 16.6 %all-to-all-start.1 = ((bf16[32,32,128]{2,1,0:T(8,128)(2,1)}), bf16[32,32,128]{2,1,0:T(8,128)(2,1)S(1)}, u32[]{:S(2)}, u32[]{:S(2)}) async-start(bf16[32,32,128]{2,1,0:T(8,128)(2,1)} %bitcast.6), calls=%async_computation.1 | async-start | bytes 524288 | tf_op jit(solution)/shard_map/all_to_all | solution.py:310

commit v10 on v9

--- a/solution.py
+++ b/solution.py
@@ -131,18 +131,16 @@
 
 def loading(steps, groups, kernel, me, x_h, w_h, *refs):
     x, w, totals, x_sems, w_sems = refs[-5:]
-    part = w.shape[2]
+    part = totals.shape[2]
+    blocks = [lax.rem(me[0] + step, len(steps)) * part for step in steps]
     depth = x.shape[1] // CHUNKS
     loads = []
     for c in range(CHUNKS):
         chunk = pl.ds(c * depth, depth)
-        group = [pltpu.make_async_copy(x_h.at[:, chunk], x.at[:, chunk], x_sems.at[c])]
-        for k, step in enumerate(steps):
-            block = lax.rem(me[0] + step, w_h.shape[1] // part)
-            columns = pl.ds(pl.multiple_of(block * part, part), part)
-            group.append(
-                pltpu.make_async_copy(w_h.at[chunk, columns], w.at[k, chunk], w_sems.at[c, k])
-            )
+        group = [
+            pltpu.make_async_copy(x_h.at[:, chunk], x.at[:, chunk], x_sems.at[c]),
+            pltpu.make_async_copy(w_h.at[chunk], w.at[chunk], w_sems.at[c]),
+        ]
         loads.append(group)
         for load in group:
             load.start()
@@ -151,7 +149,9 @@
         for load in loads[c]:
             load.wait()
         for group in groups:
-            columns = jnp.concatenate([w[k, chunk, :] for k in group], axis=1)
+            columns = jnp.concatenate(
+                [w[chunk, pl.ds(pl.multiple_of(blocks[k], part), part)] for k in group], axis=1
+            )
             value = jnp.dot(x[:, chunk], columns, preferred_element_type=jnp.float32)
             for i, k in enumerate(group):
                 share = value[:, i * part : (i + 1) * part]
@@ -189,10 +189,10 @@
         out_specs=[pl.BlockSpec(memory_space=pltpu.VMEM)] * len(outs),
         scratch_shapes=[
             pltpu.VMEM((rows, depth), x.dtype),
-            pltpu.VMEM((count, depth, part), w.dtype),
+            pltpu.VMEM(w.shape, w.dtype),
             pltpu.VMEM((count, rows, part), jnp.float32),
             pltpu.SemaphoreType.DMA((CHUNKS,)),
-            pltpu.SemaphoreType.DMA((CHUNKS, count)),
+            pltpu.SemaphoreType.DMA((CHUNKS,)),
         ],
         compiler_params=pltpu.CompilerParams(vmem_limit_bytes=52 * 2**20),
         cost_estimate=pl.CostEstimate(

time: 62.8 us -> 61.8 us (0.984)
  waiting for transfers between devices: 13 us -> 14.1 us
  Pallas kernels: 16.6 us -> 15.6 us
  starting transfers between devices: 30.8 us -> 29.8 us
    all_to_all x1, starting transfers between devices: 7.52 us -> 6.5 us  [local(): lax.all_to_all(placed, PLANE, split_axis=0, concat_axis=0, tiled=True)]
    pallas_call x1, Pallas kernels: 5.53 us -> 4.55 us  [products(): pl.pallas_call(functools.partial(loading, steps, places, kernel), out_sha...]
    all_to_all x1, waiting for transfers between devices: 2.05 us -> 3.03 us  [local(): lax.all_to_all(spread, CHIPS, split_axis=0, concat_axis=0, tiled=True)]
  transfers between devices with their start and end apart: 11 -> 11, of which waited for: 5 -> 5; matrix products, arithmetic and copies ran while one was open for 0% -> 0% of each run, Pallas kernels for 21% -> 20%
where the time goes in v10:
time: 61.8 us; the launch traced here: 61.5 us
  starting transfers between devices  29.8 us (48%)
  Pallas kernels  15.6 us (25%)
  waiting for transfers between devices  14.1 us (23%)
  between operations  1.37 us (2%)
  local copies, waits for them, and re-layouts  0.71 us (1%)
    ppermute x8, starting transfers between devices, along_tp(): lax.ppermute(value, 'tp', [(i, (i + step) % size) for i in range(size)])  13.5 us
    ppermute x8, waiting for transfers between devices, along_tp(): lax.ppermute(value, 'tp', [(i, (i + step) % size) for i in range(size)])  7.61 us
    all_to_all x1, starting transfers between devices, local(): lax.all_to_all(spread, CHIPS, split_axis=0, concat_axis=0, tiled=True)  7.6 us
    all_to_all x1, starting transfers between devices, local(): lax.all_to_all(placed, PLANE, split_axis=0, concat_axis=0, tiled=True)  6.5 us
    pallas_call x2, Pallas kernels, set_half(): pl.pallas_call(half_kernel, out_shape=jax.ShapeDtypeStruct((lanes, 2, row...  5.64 us
    pallas_call x1, Pallas kernels, products(): pl.pallas_call(functools.partial(loading, steps, places, kernel), out_sha...  4.55 us
    all_to_all x1, waiting for transfers between devices, local(): lax.all_to_all(placed, PLANE, split_axis=0, concat_axis=0, tiled=True)  3.41 us
    pallas_call x1, Pallas kernels, updated(): pl.pallas_call(update_kernel, out_shape=outs, in_specs=[anywhere] * 5, ou...  3.17 us
  transfers between devices with their start and end apart: 11, of which 5 were waited for; matrix products, arithmetic and copies ran while one was open for 0% of the time, Pallas kernels for 20%

profile of v10, /device:TPU:1, one launch (start us, length us, event | category | flops | bytes accessed | tf_op | source)
XLA Modules:
  0.0 61.5 jit_solution(4577228427647511342)
XLA Ops:
  1.3 3.2 %shard_map.119 = (f32[64,1024]{1,0:T(8,128)}, f32[64,1024]{1,0:T(8,128)}, f32[64,1024]{1,0:T(8,128)}, bf16[16,64,1024]{2,1,0:T(8,128)(2,1)}) custom-call(s32[1,1]{1,0:T(1,128)} %bitcast.9.step_h, f32[64,1024]{1,0:T(8,128)} %master_h.1, f32[64,1024]{1,0:T(8,128)} %moment_h.1, f32[64,1024]{1,0:T(8,128)} %second_h.1, f32[64,1024]{1,0:T(8,128)} %gradient_h.1), custom_call_target="tpu_custom_call" | custom-call | flops 1966080 | bytes 3932160 | tf_op jit(solution)/shard_map/pallas_call | solution.py:111
  4.5 7.6 %all-to-all-start = ((bf16[16,64,1024]{2,1,0:T(8,128)(2,1)}), bf16[16,64,1024]{2,1,0:T(8,128)(2,1)S(1)}, u32[]{:S(2)}, u32[]{:S(2)}) async-start(bf16[16,64,1024]{2,1,0:T(8,128)(2,1)} %get-tuple-element.26), calls=%async_computation | async-start | bytes 4194304 | tf_op jit(solution)/shard_map/all_to_all | solution.py:289
  12.1 0.0 copy-start
  12.1 4.5 %shard_map.120 = (s16[528,128]{1,0:T(8,128)(2,1)S(1)}, s16[528,128]{1,0:T(8,128)(2,1)S(1)}, s16[272,128]{1,0:T(8,128)(2,1)S(1)}, s16[272,128]{1,0:T(8,128)(2,1)S...) custom-call(s32[1]{0:T(128)} %bitcast.2.me, ...), custom_call_target="tpu_custom_call" | custom-call | flops 2147483648 | bytes 6291456 | tf_op jit(solution)/shard_map/pallas_call | solution.py:185
  16.6 1.7 %collective-permute-start.2 = (s16[528,128]{1,0:T(8,128)(2,1)S(1)}, s16[528,128]{1,0:T(8,128)(2,1)S(1)}, u32[]{:S(2)}, u32[]{:S(2)}) collective-permute-start(s16[528,128]{1,0:T(8,128)(2,1)S(1)} %get-tuple-element.31), channel_id=1, source_target_pairs={{0,1},{1,2},{2,3},{3,4},{4,5},{5,6},{6,7},{7,0},{8,9},{9,10},{10,1... | collective-permute-start | bytes 405512 | tf_op jit(solution)/shard_map/ppermute | solution.py:274
  18.4 4.0 %collective-permute-start.4 = (s16[528,128]{1,0:T(8,128)(2,1)S(1)}, s16[528,128]{1,0:T(8,128)(2,1)S(1)}, u32[]{:S(2)}, u32[]{:S(2)}) collective-permute-start(s16[528,128]{1,0:T(8,128)(2,1)S(1)} %get-tuple-element.34), channel_id=1, source_target_pairs={{0,7},{1,0},{2,1},{3,2},{4,3},{5,4},{6,5},{7,6},{8,15},{9,8},{10,9... | collective-permute-start | bytes 405512 | tf_op jit(solution)/shard_map/ppermute | solution.py:274
  22.4 0.0 collective-permute-start.3
  22.4 3.6 %collective-permute-start.5 = (s16[272,128]{1,0:T(8,128)(2,1)S(1)}, s16[272,128]{1,0:T(8,128)(2,1)S(1)}, u32[]{:S(2)}, u32[]{:S(2)}) collective-permute-start(s16[272,128]{1,0:T(8,128)(2,1)S(1)} %get-tuple-element.35), channel_id=1, source_target_pairs={{0,6},{1,7},{2,0},{3,1},{4,2},{5,3},{6,4},{7,5},{8,14},{9,15},{10,... | collective-permute-start | bytes 208904 | tf_op jit(solution)/shard_map/ppermute | solution.py:274
  25.9 0.0 collective-permute-start
  25.9 3.0 %collective-permute-done.3.far_a = s16[272,128]{1,0:T(8,128)(2,1)S(1)} collective-permute-done((s16[272,128]{1,0:T(8,128)(2,1)S(1)}, s16[272,128]{1,0:T(8,128)(2,1)S(1)}, u32[]{:S(2)}, u32[]{:S(2)}) %collective-permute-start.3) | collective-permute-done | bytes 69664 | tf_op jit(solution)/shard_map/ppermute | solution.py:274
  29.0 0.6 collective-permute-start.1
  29.5 0.0 collective-permute-done.5.far_b
  29.5 0.0 collective-permute-done.2.next_a
  29.5 0.0 collective-permute-done.4.next_b
  29.5 0.3 shard_map.121
  29.8 3.0 %collective-permute-start.6 = (s16[528,128]{1,0:T(8,128)(2,1)S(1)}, s16[528,128]{1,0:T(8,128)(2,1)S(1)}, u32[]{:S(2)}, u32[]{:S(2)}) collective-permute-start(s16[528,128]{1,0:T(8,128)(2,1)S(1)} %get-tuple-element.36), channel_id=1, source_target_pairs={{0,2},{1,3},{2,4},{3,5},{4,6},{5,7},{6,0},{7,1},{8,10},{9,11},{10,... | collective-permute-start | bytes 405512 | tf_op jit(solution)/shard_map/ppermute | solution.py:274
  32.8 0.6 %collective-permute-start.7 = (s16[528,128]{1,0:T(8,128)(2,1)S(1)}, s16[528,128]{1,0:T(8,128)(2,1)S(1)}, u32[]{:S(2)}, u32[]{:S(2)}) collective-permute-start(s16[528,128]{1,0:T(8,128)(2,1)S(1)} %get-tuple-element.37), channel_id=1, source_target_pairs={{0,6},{1,7},{2,0},{3,1},{4,2},{5,3},{6,4},{7,5},{8,14},{9,15},{10,... | collective-permute-start | bytes 405512 | tf_op jit(solution)/shard_map/ppermute | solution.py:274
  33.5 0.0 copy-done
  33.5 0.6 %shard_map.122.selector = bf16[1024,512]{1,0:T(8,128)(2,1)S(1)} custom-call(s32[1,512]{1,0:T(1,128)S(1)} %bitcast.11), custom_call_target="tpu_custom_call" | custom-call | bytes 1048576 | tf_op jit(solution)/shard_map/pallas_call | solution.py:207
  34.1 0.0 collective-permute-done.ra
  34.1 0.0 collective-permute-done.1.rb
  34.1 2.3 %collective-permute-done.6.rc = s16[528,128]{1,0:T(8,128)(2,1)S(1)} collective-permute-done((s16[528,128]{1,0:T(8,128)(2,1)S(1)}, s16[528,128]{1,0:T(8,128)(2,1)S(1)}, u32[]{:S(2)}, u32[]{:S(2)}) %collective-permute-start.6) | collective-permute-done | bytes 135200 | tf_op jit(solution)/shard_map/ppermute | solution.py:274
  36.5 2.3 %collective-permute-done.7.rd = s16[528,128]{1,0:T(8,128)(2,1)S(1)} collective-permute-done((s16[528,128]{1,0:T(8,128)(2,1)S(1)}, s16[528,128]{1,0:T(8,128)(2,1)S(1)}, u32[]{:S(2)}, u32[]{:S(2)}) %collective-permute-start.7) | collective-permute-done | bytes 135200 | tf_op jit(solution)/shard_map/ppermute | solution.py:274
  38.7 1.3 %shard_map.123 = bf16[1024,128]{1,0:T(8,128)(2,1)} custom-call(f32[512,128]{1,0:T(8,128)S(1)} %get-tuple-element.27.own, s16[528,128]{1,0:T(8,128)(2,1)S(1)} %collective-permute-done.ra, s16[528,128]{1,0:T(8,128)(2,1)S(1)} %collective-permute-done.1.rb, s16[528,128]{1,0:T(8,128)(2,1)S(1)} %collective-permute-done.6.rc, ...), custom_call_target="tpu_custom_call" | custom-call | bytes 1048576 | tf_op jit(solution)/shard_map/pallas_call | solution.py:207
  40.0 3.0 %all-to-all-done = bf16[16,64,1024]{2,1,0:T(8,128)(2,1)S(1)} async-done(((bf16[16,64,1024]{2,1,0:T(8,128)(2,1)}), bf16[16,64,1024]{2,1,0:T(8,128)(2,1)S(1)}, u32[]{:S(2)}, u32[]{:S(2)}) %all-to-all-start) | async-done | bytes 2097184 | tf_op jit(solution)/shard_map/all_to_all | solution.py:289
  43.0 2.2 %collective-permute-start.8 = (bf16[16,64,1024]{2,1,0:T(8,128)(2,1)S(1)}, bf16[16,64,1024]{2,1,0:T(8,128)(2,1)}, u32[]{:S(2)}, u32[]{:S(2)}) collective-permute-start(bf16[16,64,1024]{2,1,0:T(8,128)(2,1)S(1)} %all-to-all-done), channel_id=1, source_target_pairs={{0,64},{64,0},{1,65},{65,1},{2,66},{66,2},{3,67},{67,3},{4,68},{68... | collective-permute-start | bytes 6291464 | tf_op jit(solution)/shard_map/ppermute | solution.py:311
  45.2 6.5 %all-to-all-start.1 = ((bf16[32,32,128]{2,1,0:T(8,128)(2,1)}), bf16[32,32,128]{2,1,0:T(8,128)(2,1)S(1)}, u32[]{:S(2)}, u32[]{:S(2)}) async-start(bf16[32,32,128]{2,1,0:T(8,128)(2,1)} %bitcast.6), calls=%async_computation.1 | async-start | bytes 524288 | tf_op jit(solution)/shard_map/all_to_all | solution.py:310
  51.7 1.9 %shard_map.124.refs_0_ = bf16[2,2,512,1024]{3,2,1,0:T(8,128)(2,1)} custom-call(s32[1]{0:T(128)} %bitcast.1.place, bf16[2,512,1024]{2,1,0:T(8,128)(2,1)S(1)} %bitcast.10), custom_call_target="tpu_custom_call" | custom-call | bytes 4194304 | tf_op jit(solution)/shard_map/pallas_call | solution.py:256
  53.6 0.0 collective-permute-done.8
  53.6 3.8 %shard_map.125 = bf16[2,2,512,1024]{3,2,1,0:T(8,128)(2,1)} custom-call(s32[1]{0:T(128)S(6)} %sub.3.place, bf16[2,512,1024]{2,1,0:T(8,128)(2,1)} %bitcast.4.half, bf16[2,2,512,1024]{3,2,1,0:T(8,128)(2,1)} %shard_map.124.refs_0_), custom_call_target="tpu_custom_call", output_to_operand_aliasing={{}: (2, {})} | custom-call | bytes 4194304 | tf_op jit(solution)/shard_map/pallas_call | solution.py:256
  57.4 3.4 %all-to-all-done.1 = bf16[32,32,128]{2,1,0:T(8,128)(2,1)S(1)} async-done(((bf16[32,32,128]{2,1,0:T(8,128)(2,1)}), bf16[32,32,128]{2,1,0:T(8,128)(2,1)S(1)}, u32[]{:S(2)}, u32[]{:S(2)}) %all-to-all-start.1) | async-done | bytes 262176 | tf_op jit(solution)/shard_map/all_to_all | solution.py:310
  60.8 0.7 %copy.17 = bf16[1,32,32,128]{3,2,1,0:T(8,128)(2,1)} copy(bf16[1,32,32,128]{3,2,1,0:T(8,128)(2,1)S(1)} %bitcast.13) | data formatting | bytes 524288
Async XLA Ops:
  4.5 38.6 %all-to-all-start = ((bf16[16,64,1024]{2,1,0:T(8,128)(2,1)}), bf16[16,64,1024]{2,1,0:T(8,128)(2,1)S(1)}, u32[]{:S(2)}, u32[]{:S(2)}) async-start(bf16[16,64,1024]{2,1,0:T(8,128)(2,1)} %get-tuple-element.26), calls=%async_computation | async-start | bytes 4194304 | tf_op jit(solution)/shard_map/all_to_all | solution.py:289
  12.1 21.4 %copy-start = (s32[512,1]{0,1:T(1,128)S(1)}, s32[512,1]{0,1:T(1,128)}, u32[]{:S(2)}) copy-start(s32[512,1]{0,1:T(1,128)} %param.15) | copy-start | bytes 6148
  16.6 12.9 %collective-permute-start.2 = (s16[528,128]{1,0:T(8,128)(2,1)S(1)}, s16[528,128]{1,0:T(8,128)(2,1)S(1)}, u32[]{:S(2)}, u32[]{:S(2)}) collective-permute-start(s16[528,128]{1,0:T(8,128)(2,1)S(1)} %get-tuple-element.31), channel_id=1, source_target_pairs={{0,1},{1,2},{2,3},{3,4},{4,5},{5,6},{6,7},{7,0},{8,9},{9,10},{10,1... | collective-permute-start | bytes 405512 | tf_op jit(solution)/shard_map/ppermute | solution.py:274
  18.4 11.2 %collective-permute-start.4 = (s16[528,128]{1,0:T(8,128)(2,1)S(1)}, s16[528,128]{1,0:T(8,128)(2,1)S(1)}, u32[]{:S(2)}, u32[]{:S(2)}) collective-permute-start(s16[528,128]{1,0:T(8,128)(2,1)S(1)} %get-tuple-element.34), channel_id=1, source_target_pairs={{0,7},{1,0},{2,1},{3,2},{4,3},{5,4},{6,5},{7,6},{8,15},{9,8},{10,9... | collective-permute-start | bytes 405512 | tf_op jit(solution)/shard_map/ppermute | solution.py:274
  22.4 6.6 %collective-permute-start.3 = (s16[272,128]{1,0:T(8,128)(2,1)S(1)}, s16[272,128]{1,0:T(8,128)(2,1)S(1)}, u32[]{:S(2)}, u32[]{:S(2)}) collective-permute-start(s16[272,128]{1,0:T(8,128)(2,1)S(1)} %get-tuple-element.32), channel_id=1, source_target_pairs={{0,2},{1,3},{2,4},{3,5},{4,6},{5,7},{6,0},{7,1},{8,10},{9,11},{10,... | collective-permute-start | bytes 208904 | tf_op jit(solution)/shard_map/ppermute | solution.py:274
  22.4 7.1 %collective-permute-start.5 = (s16[272,128]{1,0:T(8,128)(2,1)S(1)}, s16[272,128]{1,0:T(8,128)(2,1)S(1)}, u32[]{:S(2)}, u32[]{:S(2)}) collective-permute-start(s16[272,128]{1,0:T(8,128)(2,1)S(1)} %get-tuple-element.35), channel_id=1, source_target_pairs={{0,6},{1,7},{2,0},{3,1},{4,2},{5,3},{6,4},{7,5},{8,14},{9,15},{10,... | collective-permute-start | bytes 208904 | tf_op jit(solution)/shard_map/ppermute | solution.py:274
  25.9 8.2 %collective-permute-start = (s16[528,128]{1,0:T(8,128)(2,1)S(1)}, s16[528,128]{1,0:T(8,128)(2,1)S(1)}, u32[]{:S(2)}, u32[]{:S(2)}) collective-permute-start(s16[528,128]{1,0:T(8,128)(2,1)S(1)} %get-tuple-element.28), channel_id=1, source_target_pairs={{0,1},{1,2},{2,3},{3,4},{4,5},{5,6},{6,7},{7,0},{8,9},{9,10},{10,1... | collective-permute-start | bytes 405512 | tf_op jit(solution)/shard_map/ppermute | solution.py:274
  29.0 5.2 %collective-permute-start.1 = (s16[528,128]{1,0:T(8,128)(2,1)S(1)}, s16[528,128]{1,0:T(8,128)(2,1)S(1)}, u32[]{:S(2)}, u32[]{:S(2)}) collective-permute-start(s16[528,128]{1,0:T(8,128)(2,1)S(1)} %get-tuple-element.29), channel_id=1, source_target_pairs={{0,7},{1,0},{2,1},{3,2},{4,3},{5,4},{6,5},{7,6},{8,15},{9,8},{10,9... | collective-permute-start | bytes 405512 | tf_op jit(solution)/shard_map/ppermute | solution.py:274
  29.8 6.6 %collective-permute-start.6 = (s16[528,128]{1,0:T(8,128)(2,1)S(1)}, s16[528,128]{1,0:T(8,128)(2,1)S(1)}, u32[]{:S(2)}, u32[]{:S(2)}) collective-permute-start(s16[528,128]{1,0:T(8,128)(2,1)S(1)} %get-tuple-element.36), channel_id=1, source_target_pairs={{0,2},{1,3},{2,4},{3,5},{4,6},{5,7},{6,0},{7,1},{8,10},{9,11},{10,... | collective-permute-start | bytes 405512 | tf_op jit(solution)/shard_map/ppermute | solution.py:274
  32.8 5.9 %collective-permute-start.7 = (s16[528,128]{1,0:T(8,128)(2,1)S(1)}, s16[528,128]{1,0:T(8,128)(2,1)S(1)}, u32[]{:S(2)}, u32[]{:S(2)}) collective-permute-start(s16[528,128]{1,0:T(8,128)(2,1)S(1)} %get-tuple-element.37), channel_id=1, source_target_pairs={{0,6},{1,7},{2,0},{3,1},{4,2},{5,3},{6,4},{7,5},{8,14},{9,15},{10,... | collective-permute-start | bytes 405512 | tf_op jit(solution)/shard_map/ppermute | solution.py:274
  43.0 10.5 %collective-permute-start.8 = (bf16[16,64,1024]{2,1,0:T(8,128)(2,1)S(1)}, bf16[16,64,1024]{2,1,0:T(8,128)(2,1)}, u32[]{:S(2)}, u32[]{:S(2)}) collective-permute-start(bf16[16,64,1024]{2,1,0:T(8,128)(2,1)S(1)} %all-to-all-done), channel_id=1, source_target_pairs={{0,64},{64,0},{1,65},{65,1},{2,66},{66,2},{3,67},{67,3},{4,68},{68... | collective-permute-start | bytes 6291464 | tf_op jit(solution)/shard_map/ppermute | solution.py:311
  45.2 15.6 %all-to-all-start.1 = ((bf16[32,32,128]{2,1,0:T(8,128)(2,1)}), bf16[32,32,128]{2,1,0:T(8,128)(2,1)S(1)}, u32[]{:S(2)}, u32[]{:S(2)}) async-start(bf16[32,32,128]{2,1,0:T(8,128)(2,1)} %bitcast.6), calls=%async_computation.1 | async-start | bytes 524288 | tf_op jit(solution)/shard_map/all_to_all | solution.py:310

commit v11 on v10

--- a/solution.py
+++ b/solution.py
@@ -159,17 +159,17 @@
     kernel(totals, *refs[:-5])
 
 
-def products_kernel(totals, up, down, far_up, far_down, next_up, next_down, two_up, two_down, own):
+def products_kernel(totals, up, down, far_up, far_down, two_up, two_down, own):
     half = totals.shape[1] // 2
-    put_coded(up, totals[0])
-    put_coded(down, totals[1])
+    put_coded(up.at[0], totals[0])
+    put_coded(down.at[0], totals[1])
     put_coded(far_up, totals[2, :half])
     put_coded(far_down, totals[2, half:])
     own[...] = totals[3]
     two_up[...] = totals[4]
     two_down[...] = totals[5]
-    put_coded(next_up, totals[6])
-    put_coded(next_down, totals[7])
+    put_coded(up.at[1], totals[6])
+    put_coded(down.at[1], totals[7])
 
 
 def products(kernel, x, w, me, groups, outs):
@@ -214,10 +214,10 @@
 
 def merge_kernel(own_a, next_a, far_a, own_b, next_b, far_b, qa, qb):
     half = own_a.shape[0] // 2
-    total = own_a[...] + take_coded(next_a)
+    total = own_a[...] + take_coded(next_a.at[0])
     total = jnp.concatenate([total[:half] + take_coded(far_a), total[half:]], axis=0)
     put_coded(qa, total)
-    total = own_b[...] + take_coded(next_b)
+    total = own_b[...] + take_coded(next_b.at[0])
     total = jnp.concatenate([total[:half], total[half:] + take_coded(far_b)], axis=0)
     put_coded(qb, total)
 
@@ -239,7 +239,7 @@
 
 
 def final_kernel(own, ra, rb, rc, rd, selector, out):
-    keys = own[...] + take_coded(ra) + take_coded(rb) + take_coded(rc) + take_coded(rd)
+    keys = own[...] + take_coded(ra.at[1]) + take_coded(rb.at[1]) + take_coded(rc) + take_coded(rd)
     out[...] = jnp.dot(
         selector[...], keys.astype(jnp.bfloat16), preferred_element_type=jnp.float32
     ).astype(jnp.bfloat16)
@@ -281,20 +281,19 @@
     me = jnp.reshape(lax.axis_index("tp"), (1,)).astype(jnp.int32)
     count = branch_rows.shape[0]
     part = old_weights.shape[1] // size
-    code = lambda n: jax.ShapeDtypeStruct((n + TAIL, part), jnp.int16)
+    code = lambda *n: jax.ShapeDtypeStruct(n[:-1] + (n[-1] + TAIL, part), jnp.int16)
     full = jax.ShapeDtypeStruct((count, part), jnp.float32)
     new_master, new_moment, new_second, spread = updated(
         step_count, master, moment, second, gradient, chips
     )
     mine = lax.all_to_all(spread, CHIPS, split_axis=0, concat_axis=0, tiled=True)
-    q3, q5, q4a, q4b, q1, q7, p2, p6, p0 = products(
+    up, down, far_up, far_down, p2, p6, p0 = products(
         products_kernel, branch_rows, old_weights, me, ((3, 5), (4, 0), (2, 6), (1, 7)),
-        [code(count)] * 2 + [code(count // 2)] * 2 + [code(count)] * 2 + [full] * 3,
-    )
-    r3, r5 = along_tp(q3, 1), along_tp(q5, -1)
-    r4a, r4b = along_tp(q4a, 2), along_tp(q4b, -2)
-    r1, r7 = along_tp(q1, 1), along_tp(q7, -1)
-    q2, q6 = local_call(merge_kernel, [code(count), code(count)], p2, r3, r4a, p6, r5, r4b)
+        [code(2, count)] * 2 + [code(count // 2)] * 2 + [full] * 3,
+    )
+    up, down = along_tp(up, 1), along_tp(down, -1)
+    far_up, far_down = along_tp(far_up, 2), along_tp(far_down, -2)
+    q2, q6 = local_call(merge_kernel, [code(count), code(count)], p2, up, far_up, p6, down, far_down)
     r2, r6 = along_tp(q2, 2), along_tp(q6, -2)
     replicas = lax.axis_size(PLANE)
     slots_each = 2 * count // replicas
@@ -303,7 +302,7 @@
         selector_kernel, jax.ShapeDtypeStruct((places, count), jnp.bfloat16), assignment.reshape(1, count)
     )
     placed = local_call(
-        final_kernel, jax.ShapeDtypeStruct((places, part), jnp.bfloat16), p0, r1, r7, r2, r6, selector
+        final_kernel, jax.ShapeDtypeStruct((places, part), jnp.bfloat16), p0, up, down, r2, r6, selector
     )
     mine = lax.optimization_barrier((mine, placed))[0]
     placed = placed.reshape(replicas, slots_each, part)

time: 61.8 us -> 62.7 us (1.015)
    ppermute x8 -> x6, waiting for transfers between devices: 7.61 us -> 10 us  [along_tp(): lax.ppermute(value, 'tp', [(i, (i + step) % size) for i in range(size)])]
    all_to_all x1, waiting for transfers between devices: 3.03 us -> 1.2 us  [local(): lax.all_to_all(spread, CHIPS, split_axis=0, concat_axis=0, tiled=True)]
    ppermute x8 -> x6, starting transfers between devices: 13.5 us -> 13 us  [along_tp(): lax.ppermute(value, 'tp', [(i, (i + step) % size) for i in range(size)])]
  transfers between devices with their start and end apart: 11 -> 9, of which waited for: 5 -> 5; matrix products, arithmetic and copies ran while one was open for 0% -> 0% of each run, Pallas kernels for 20% -> 20%
where the time goes in v11:
time: 62.7 us; the launch traced here: 62.4 us
  starting transfers between devices  30.2 us (48%)
  Pallas kernels  15.6 us (25%)
  waiting for transfers between devices  14.6 us (23%)
  between operations  1.36 us (2%)
  local copies, waits for them, and re-layouts  0.71 us (1%)
    ppermute x6, starting transfers between devices, along_tp(): lax.ppermute(value, 'tp', [(i, (i + step) % size) for i in range(size)])  13 us
    ppermute x6, waiting for transfers between devices, along_tp(): lax.ppermute(value, 'tp', [(i, (i + step) % size) for i in range(size)])  10 us
    all_to_all x1, starting transfers between devices, local(): lax.all_to_all(spread, CHIPS, split_axis=0, concat_axis=0, tiled=True)  7.6 us
    all_to_all x1, starting transfers between devices, local(): lax.all_to_all(placed, PLANE, split_axis=0, concat_axis=0, tiled=True)  7.1 us
    pallas_call x2, Pallas kernels, set_half(): pl.pallas_call(half_kernel, out_shape=jax.ShapeDtypeStruct((lanes, 2, row...  5.64 us
    pallas_call x1, Pallas kernels, products(): pl.pallas_call(functools.partial(loading, steps, places, kernel), out_sha...  4.55 us
    all_to_all x1, waiting for transfers between devices, local(): lax.all_to_all(placed, PLANE, split_axis=0, concat_axis=0, tiled=True)  3.41 us
    pallas_call x1, Pallas kernels, updated(): pl.pallas_call(update_kernel, out_shape=outs, in_specs=[anywhere] * 5, ou...  3.17 us
  transfers between devices with their start and end apart: 9, of which 5 were waited for; matrix products, arithmetic and copies ran while one was open for 0% of the time, Pallas kernels for 20%

profile of v11, /device:TPU:1, one launch (start us, length us, event | category | flops | bytes accessed | tf_op | source)
XLA Modules:
  0.0 62.4 jit_solution(11893117412246233557)
XLA Ops:
  1.3 3.2 %shard_map.119 = (f32[64,1024]{1,0:T(8,128)}, f32[64,1024]{1,0:T(8,128)}, f32[64,1024]{1,0:T(8,128)}, bf16[16,64,1024]{2,1,0:T(8,128)(2,1)}) custom-call(s32[1,1]{1,0:T(1,128)} %bitcast.9.step_h, f32[64,1024]{1,0:T(8,128)} %master_h.1, f32[64,1024]{1,0:T(8,128)} %moment_h.1, f32[64,1024]{1,0:T(8,128)} %second_h.1, f32[64,1024]{1,0:T(8,128)} %gradient_h.1), custom_call_target="tpu_custom_call" | custom-call | flops 1966080 | bytes 3932160 | tf_op jit(solution)/shard_map/pallas_call | solution.py:111
  4.5 7.6 %all-to-all-start = ((bf16[16,64,1024]{2,1,0:T(8,128)(2,1)}), bf16[16,64,1024]{2,1,0:T(8,128)(2,1)S(1)}, u32[]{:S(2)}, u32[]{:S(2)}) async-start(bf16[16,64,1024]{2,1,0:T(8,128)(2,1)} %get-tuple-element.24), calls=%async_computation | async-start | bytes 4194304 | tf_op jit(solution)/shard_map/all_to_all | solution.py:289
  12.1 0.0 copy-start
  12.1 4.6 %shard_map.120 = (s16[2,528,128]{2,1,0:T(8,128)(2,1)S(1)}, s16[2,528,128]{2,1,0:T(8,128)(2,1)S(1)}, s16[272,128]{1,0:T(8,128)(2,1)S(1)}, s16[272,128]{1,0:T(8,12...) custom-call(s32[1]{0:T(128)} %bitcast.2.me, bf16[512,2048]{1,0:T(8,128)(2,1)} %x_h.1, ...), custom_call_target="tpu_custom_call" | custom-call | flops 2147483648 | bytes 6291456 | tf_op jit(solution)/shard_map/pallas_call | solution.py:185
  16.6 1.7 %collective-permute-start = (s16[2,528,128]{2,1,0:T(8,128)(2,1)S(1)}, s16[2,528,128]{2,1,0:T(8,128)(2,1)S(1)}, u32[]{:S(2)}, u32[]{:S(2)}) collective-permute-start(s16[2,528,128]{2,1,0:T(8,128)(2,1)S(1)} %get-tuple-element.26), channel_id=1, source_target_pairs={{0,1},{1,2},{2,3},{3,4},{4,5},{5,6},{6,7},{7,0},{8,9},{9,10},{10,1... | collective-permute-start | bytes 811016 | tf_op jit(solution)/shard_map/ppermute | solution.py:274
  18.4 4.0 %collective-permute-start.1 = (s16[2,528,128]{2,1,0:T(8,128)(2,1)S(1)}, s16[2,528,128]{2,1,0:T(8,128)(2,1)S(1)}, u32[]{:S(2)}, u32[]{:S(2)}) collective-permute-start(s16[2,528,128]{2,1,0:T(8,128)(2,1)S(1)} %get-tuple-element.27), channel_id=1, source_target_pairs={{0,7},{1,0},{2,1},{3,2},{4,3},{5,4},{6,5},{7,6},{8,15},{9,8},{10,9... | collective-permute-start | bytes 811016 | tf_op jit(solution)/shard_map/ppermute | solution.py:274
  22.4 0.0 collective-permute-start.2
  22.4 3.6 %collective-permute-start.3 = (s16[272,128]{1,0:T(8,128)(2,1)S(1)}, s16[272,128]{1,0:T(8,128)(2,1)S(1)}, u32[]{:S(2)}, u32[]{:S(2)}) collective-permute-start(s16[272,128]{1,0:T(8,128)(2,1)S(1)} %get-tuple-element.31), channel_id=1, source_target_pairs={{0,6},{1,7},{2,0},{3,1},{4,2},{5,3},{6,4},{7,5},{8,14},{9,15},{10,... | collective-permute-start | bytes 208904 | tf_op jit(solution)/shard_map/ppermute | solution.py:274
  25.9 5.1 %collective-permute-done.2.far_a = s16[272,128]{1,0:T(8,128)(2,1)S(1)} collective-permute-done((s16[272,128]{1,0:T(8,128)(2,1)S(1)}, s16[272,128]{1,0:T(8,128)(2,1)S(1)}, u32[]{:S(2)}, u32[]{:S(2)}) %collective-permute-start.2) | collective-permute-done | bytes 69664 | tf_op jit(solution)/shard_map/ppermute | solution.py:274
  31.0 0.0 collective-permute-done.3.far_b
  31.0 0.0 collective-permute-done.next_a.ra
  31.0 0.0 collective-permute-done.1.next_b.rb
  31.0 0.3 shard_map.121
  31.3 3.2 %collective-permute-start.4 = (s16[528,128]{1,0:T(8,128)(2,1)S(1)}, s16[528,128]{1,0:T(8,128)(2,1)S(1)}, u32[]{:S(2)}, u32[]{:S(2)}) collective-permute-start(s16[528,128]{1,0:T(8,128)(2,1)S(1)} %get-tuple-element.32), channel_id=1, source_target_pairs={{0,2},{1,3},{2,4},{3,5},{4,6},{5,7},{6,0},{7,1},{8,10},{9,11},{10,... | collective-permute-start | bytes 405512 | tf_op jit(solution)/shard_map/ppermute | solution.py:274
  34.5 0.5 collective-permute-start.5
  34.9 0.0 copy-done
  35.0 0.6 %shard_map.122.selector = bf16[1024,512]{1,0:T(8,128)(2,1)S(1)} custom-call(s32[1,512]{1,0:T(1,128)S(1)} %bitcast.11), custom_call_target="tpu_custom_call" | custom-call | bytes 1048576 | tf_op jit(solution)/shard_map/pallas_call | solution.py:207
  35.6 3.8 %collective-permute-done.4.rc = s16[528,128]{1,0:T(8,128)(2,1)S(1)} collective-permute-done((s16[528,128]{1,0:T(8,128)(2,1)S(1)}, s16[528,128]{1,0:T(8,128)(2,1)S(1)}, u32[]{:S(2)}, u32[]{:S(2)}) %collective-permute-start.4) | collective-permute-done | bytes 135200 | tf_op jit(solution)/shard_map/ppermute | solution.py:274
  39.4 1.1 %collective-permute-done.5.rd = s16[528,128]{1,0:T(8,128)(2,1)S(1)} collective-permute-done((s16[528,128]{1,0:T(8,128)(2,1)S(1)}, s16[528,128]{1,0:T(8,128)(2,1)S(1)}, u32[]{:S(2)}, u32[]{:S(2)}) %collective-permute-start.5) | collective-permute-done | bytes 135200 | tf_op jit(solution)/shard_map/ppermute | solution.py:274
  40.6 1.3 %shard_map.123 = bf16[1024,128]{1,0:T(8,128)(2,1)} custom-call(f32[512,128]{1,0:T(8,128)S(1)} %get-tuple-element.25.own, s16[2,528,128]{2,1,0:T(8,128)(2,1)S(1)} %collective-permute-done.next_a.ra, s16[2,528,128]{2,1,0:T(8,128)(2,1)S(1)} %collective-permute-done.1.next_b.rb, s16[528,128]{1,0:T(8,128)(2,1)S(1)} %collective-permute-done.4.rc, ...), custom_call_target="tpu_custom_call" | custom-call | bytes 1048576 | tf_op jit(solution)/shard_map/pallas_call | solution.py:207
  41.8 1.2 %all-to-all-done = bf16[16,64,1024]{2,1,0:T(8,128)(2,1)S(1)} async-done(((bf16[16,64,1024]{2,1,0:T(8,128)(2,1)}), bf16[16,64,1024]{2,1,0:T(8,128)(2,1)S(1)}, u32[]{:S(2)}, u32[]{:S(2)}) %all-to-all-start) | async-done | bytes 2097184 | tf_op jit(solution)/shard_map/all_to_all | solution.py:289
  43.0 2.5 %collective-permute-start.6 = (bf16[16,64,1024]{2,1,0:T(8,128)(2,1)S(1)}, bf16[16,64,1024]{2,1,0:T(8,128)(2,1)}, u32[]{:S(2)}, u32[]{:S(2)}) collective-permute-start(bf16[16,64,1024]{2,1,0:T(8,128)(2,1)S(1)} %all-to-all-done), channel_id=1, source_target_pairs={{0,64},{64,0},{1,65},{65,1},{2,66},{66,2},{3,67},{67,3},{4,68},{68... | collective-permute-start | bytes 6291464 | tf_op jit(solution)/shard_map/ppermute | solution.py:310
  45.6 7.1 %all-to-all-start.1 = ((bf16[32,32,128]{2,1,0:T(8,128)(2,1)}), bf16[32,32,128]{2,1,0:T(8,128)(2,1)S(1)}, u32[]{:S(2)}, u32[]{:S(2)}) async-start(bf16[32,32,128]{2,1,0:T(8,128)(2,1)} %bitcast.6), calls=%async_computation.1 | async-start | bytes 524288 | tf_op jit(solution)/shard_map/all_to_all | solution.py:309
  52.7 1.9 %shard_map.124.refs_0_ = bf16[2,2,512,1024]{3,2,1,0:T(8,128)(2,1)} custom-call(s32[1]{0:T(128)} %bitcast.1.place, bf16[2,512,1024]{2,1,0:T(8,128)(2,1)S(1)} %bitcast.10), custom_call_target="tpu_custom_call" | custom-call | bytes 4194304 | tf_op jit(solution)/shard_map/pallas_call | solution.py:256
  54.5 0.0 collective-permute-done.6
  54.5 3.8 %shard_map.125 = bf16[2,2,512,1024]{3,2,1,0:T(8,128)(2,1)} custom-call(s32[1]{0:T(128)S(6)} %sub.3.place, bf16[2,512,1024]{2,1,0:T(8,128)(2,1)} %bitcast.4.half, bf16[2,2,512,1024]{3,2,1,0:T(8,128)(2,1)} %shard_map.124.refs_0_), custom_call_target="tpu_custom_call", output_to_operand_aliasing={{}: (2, {})} | custom-call | bytes 4194304 | tf_op jit(solution)/shard_map/pallas_call | solution.py:256
  58.3 3.4 %all-to-all-done.1 = bf16[32,32,128]{2,1,0:T(8,128)(2,1)S(1)} async-done(((bf16[32,32,128]{2,1,0:T(8,128)(2,1)}), bf16[32,32,128]{2,1,0:T(8,128)(2,1)S(1)}, u32[]{:S(2)}, u32[]{:S(2)}) %all-to-all-start.1) | async-done | bytes 262176 | tf_op jit(solution)/shard_map/all_to_all | solution.py:309
  61.7 0.7 %copy.17 = bf16[1,32,32,128]{3,2,1,0:T(8,128)(2,1)} copy(bf16[1,32,32,128]{3,2,1,0:T(8,128)(2,1)S(1)} %bitcast.13) | data formatting | bytes 524288
Async XLA Ops:
  4.5 38.6 %all-to-all-start = ((bf16[16,64,1024]{2,1,0:T(8,128)(2,1)}), bf16[16,64,1024]{2,1,0:T(8,128)(2,1)S(1)}, u32[]{:S(2)}, u32[]{:S(2)}) async-start(bf16[16,64,1024]{2,1,0:T(8,128)(2,1)} %get-tuple-element.24), calls=%async_computation | async-start | bytes 4194304 | tf_op jit(solution)/shard_map/all_to_all | solution.py:289
  12.1 22.9 %copy-start = (s32[512,1]{0,1:T(1,128)S(1)}, s32[512,1]{0,1:T(1,128)}, u32[]{:S(2)}) copy-start(s32[512,1]{0,1:T(1,128)} %param.15) | copy-start | bytes 6148
  16.6 14.4 %collective-permute-start = (s16[2,528,128]{2,1,0:T(8,128)(2,1)S(1)}, s16[2,528,128]{2,1,0:T(8,128)(2,1)S(1)}, u32[]{:S(2)}, u32[]{:S(2)}) collective-permute-start(s16[2,528,128]{2,1,0:T(8,128)(2,1)S(1)} %get-tuple-element.26), channel_id=1, source_target_pairs={{0,1},{1,2},{2,3},{3,4},{4,5},{5,6},{6,7},{7,0},{8,9},{9,10},{10,1... | collective-permute-start | bytes 811016 | tf_op jit(solution)/shard_map/ppermute | solution.py:274
  18.4 12.7 %collective-permute-start.1 = (s16[2,528,128]{2,1,0:T(8,128)(2,1)S(1)}, s16[2,528,128]{2,1,0:T(8,128)(2,1)S(1)}, u32[]{:S(2)}, u32[]{:S(2)}) collective-permute-start(s16[2,528,128]{2,1,0:T(8,128)(2,1)S(1)} %get-tuple-element.27), channel_id=1, source_target_pairs={{0,7},{1,0},{2,1},{3,2},{4,3},{5,4},{6,5},{7,6},{8,15},{9,8},{10,9... | collective-permute-start | bytes 811016 | tf_op jit(solution)/shard_map/ppermute | solution.py:274
  22.4 8.6 %collective-permute-start.2 = (s16[272,128]{1,0:T(8,128)(2,1)S(1)}, s16[272,128]{1,0:T(8,128)(2,1)S(1)}, u32[]{:S(2)}, u32[]{:S(2)}) collective-permute-start(s16[272,128]{1,0:T(8,128)(2,1)S(1)} %get-tuple-element.29), channel_id=1, source_target_pairs={{0,2},{1,3},{2,4},{3,5},{4,6},{5,7},{6,0},{7,1},{8,10},{9,11},{10,... | collective-permute-start | bytes 208904 | tf_op jit(solution)/shard_map/ppermute | solution.py:274
  22.4 8.6 %collective-permute-start.3 = (s16[272,128]{1,0:T(8,128)(2,1)S(1)}, s16[272,128]{1,0:T(8,128)(2,1)S(1)}, u32[]{:S(2)}, u32[]{:S(2)}) collective-permute-start(s16[272,128]{1,0:T(8,128)(2,1)S(1)} %get-tuple-element.31), channel_id=1, source_target_pairs={{0,6},{1,7},{2,0},{3,1},{4,2},{5,3},{6,4},{7,5},{8,14},{9,15},{10,... | collective-permute-start | bytes 208904 | tf_op jit(solution)/shard_map/ppermute | solution.py:274
  31.3 8.1 %collective-permute-start.4 = (s16[528,128]{1,0:T(8,128)(2,1)S(1)}, s16[528,128]{1,0:T(8,128)(2,1)S(1)}, u32[]{:S(2)}, u32[]{:S(2)}) collective-permute-start(s16[528,128]{1,0:T(8,128)(2,1)S(1)} %get-tuple-element.32), channel_id=1, source_target_pairs={{0,2},{1,3},{2,4},{3,5},{4,6},{5,7},{6,0},{7,1},{8,10},{9,11},{10,... | collective-permute-start | bytes 405512 | tf_op jit(solution)/shard_map/ppermute | solution.py:274
  34.5 6.1 %collective-permute-start.5 = (s16[528,128]{1,0:T(8,128)(2,1)S(1)}, s16[528,128]{1,0:T(8,128)(2,1)S(1)}, u32[]{:S(2)}, u32[]{:S(2)}) collective-permute-start(s16[528,128]{1,0:T(8,128)(2,1)S(1)} %get-tuple-element.33), channel_id=1, source_target_pairs={{0,6},{1,7},{2,0},{3,1},{4,2},{5,3},{6,4},{7,5},{8,14},{9,15},{10,... | collective-permute-start | bytes 405512 | tf_op jit(solution)/shard_map/ppermute | solution.py:274
  43.0 11.5 %collective-permute-start.6 = (bf16[16,64,1024]{2,1,0:T(8,128)(2,1)S(1)}, bf16[16,64,1024]{2,1,0:T(8,128)(2,1)}, u32[]{:S(2)}, u32[]{:S(2)}) collective-permute-start(bf16[16,64,1024]{2,1,0:T(8,128)(2,1)S(1)} %all-to-all-done), channel_id=1, source_target_pairs={{0,64},{64,0},{1,65},{65,1},{2,66},{66,2},{3,67},{67,3},{4,68},{68... | collective-permute-start | bytes 6291464 | tf_op jit(solution)/shard_map/ppermute | solution.py:310
  45.6 16.2 %all-to-all-start.1 = ((bf16[32,32,128]{2,1,0:T(8,128)(2,1)}), bf16[32,32,128]{2,1,0:T(8,128)(2,1)S(1)}, u32[]{:S(2)}, u32[]{:S(2)}) async-start(bf16[32,32,128]{2,1,0:T(8,128)(2,1)} %bitcast.6), calls=%async_computation.1 | async-start | bytes 524288 | tf_op jit(solution)/shard_map/all_to_all | solution.py:309

commit v12 on v10

--- a/solution.py
+++ b/solution.py
@@ -15,7 +15,6 @@
 CHIPS = ("xlo", "y", "xhi")
 LEVELS = 32767.0
 TAIL = 16
-PIECES = 2
 CHUNKS = 4
 MOST_STEPS = 8
 
@@ -44,87 +43,72 @@
     return codes * (1.0 / LEVELS) * jnp.exp2(power * (1.0 / 256.0))
 
 
-def update_kernel(
-    step_h, master_h, moment_h, second_h, gradient_h,
-    new_master_h, new_moment_h, new_second_h, spread_h,
-    step, master, moment, second, gradient, new_master, new_moment, new_second, fresh,
-    step_sem, sems, out_sems, spread_sems,
-):
-    sources = [moment_h, gradient_h, second_h, master_h]
-    places = [moment, gradient, second, master]
-    rows = master.shape[0] // PIECES
-    pieces = [pl.ds(p * rows, rows) for p in range(PIECES)]
-    load_step = pltpu.make_async_copy(step_h, step, step_sem)
-    load_step.start()
-    loads = [
-        [
-            pltpu.make_async_copy(source.at[piece], place.at[piece], sems.at[p, k])
-            for k, (source, place) in enumerate(zip(sources, places))
-        ]
-        for p, piece in enumerate(pieces)
-    ]
-    for group in loads:
-        for load in group:
-            load.start()
-
-    load_step.wait()
-    steps = jnp.broadcast_to(step[...], (1, master.shape[1]))
+def adamw(steps, master, moment, second, gradient):
     first = other = jnp.ones(steps.shape, jnp.float32)
     for k in range(MOST_STEPS):
         first = jnp.where(steps > k, first * 0.9, first)
         other = jnp.where(steps > k, other * 0.95, other)
-    first_fix, second_fix = 1.0 - first, 1.0 - other
-    finished = [(new_master, new_master_h), (new_moment, new_moment_h), (new_second, new_second_h)]
-    stores = []
-    for p, piece in enumerate(pieces):
-        for load in loads[p]:
-            load.wait()
-        g, old = gradient[piece, :], master[piece, :]
-        m = 0.9 * moment[piece, :] + 0.1 * g
-        v = 0.95 * second[piece, :] + 0.05 * g * g
-        update = m / first_fix / (jnp.sqrt(v / second_fix) + 1e-08)
-        new = old - learn_rate * (update + decay_rate * old)
-        fresh[piece, :] = new.astype(jnp.bfloat16)
-        new_moment[piece, :] = m
-        new_second[piece, :] = v
-        new_master[piece, :] = new
-        group = [
-            pltpu.make_async_copy(fresh.at[piece], spread_h.at[k, piece], spread_sems.at[p, k])
-            for k in range(spread_h.shape[0])
-        ]
-        group += [
-            pltpu.make_async_copy(source.at[piece], place.at[piece], out_sems.at[p, k])
-            for k, (source, place) in enumerate(finished)
-        ]
-        for store in group:
-            store.start()
-        stores += group
+    first_part, second_part = 1.0 / (1.0 - first), 1.0 / (1.0 - other)
+    m = 0.9 * moment + 0.1 * gradient
+    v = 0.95 * second + 0.05 * gradient * gradient
+    update = m * first_part / (jnp.sqrt(v * second_part) + 1e-08)
+    return master - learn_rate * (update + decay_rate * master), m, v
+
+
+def update_kernel(step_h, master_h, moment_h, second_h, gradient_h, *refs):
+    count = len(refs) - 8
+    outs, (step, master, moment, second, gradient, results, sems, out_sems) = refs[:count], refs[count:]
+    sources = [step_h, moment_h, gradient_h, second_h, master_h]
+    places = [step, moment, gradient, second, master]
+    loads = [
+        pltpu.make_async_copy(source, place, sems.at[k])
+        for k, (source, place) in enumerate(zip(sources, places))
+    ]
+    for load in loads:
+        load.start()
+    for load in loads:
+        load.wait()
+    steps = jnp.broadcast_to(step[...], (1, master.shape[1]))
+    values = adamw(steps, master[...], moment[...], second[...], gradient[...])
+    if count == 1:
+        results[0] = values[0].astype(results.dtype)
+        pairs = [(results.at[0], outs[0].at[k]) for k in range(outs[0].shape[0])]
+    else:
+        for k, value in enumerate(values):
+            results[k] = value
+        pairs = [(results.at[k], out) for k, out in enumerate(outs)]
+    stores = [
+        pltpu.make_async_copy(source, place, out_sems.at[k])
+        for k, (source, place) in enumerate(pairs)
+    ]
+    for store in stores:
+        store.start()
     for store in stores:
         store.wait()
 
 
-def updated(step_count, master, moment, second, gradient, chips):
+def updated(step_count, master, moment, second, gradient, chips=None):
     anywhere = pl.BlockSpec(memory_space=pl.ANY)
     shard = master.shape
-    outs = [jax.ShapeDtypeStruct(shard, jnp.float32)] * 3
-    outs += [jax.ShapeDtypeStruct((chips,) + shard, jnp.bfloat16)]
+    if chips is None:
+        outs, kind, copies = [jax.ShapeDtypeStruct(shard, jnp.float32)] * 3, jnp.float32, 3
+    else:
+        outs, kind, copies = [jax.ShapeDtypeStruct((chips,) + shard, jnp.bfloat16)], jnp.bfloat16, chips
     return pl.pallas_call(
         update_kernel,
         out_shape=outs,
         in_specs=[anywhere] * 5,
-        out_specs=[anywhere] * 4,
+        out_specs=[anywhere] * len(outs),
         scratch_shapes=[pltpu.VMEM((1, 1), jnp.int32)]
-        + [pltpu.VMEM(shard, jnp.float32)] * 7
+        + [pltpu.VMEM(shard, jnp.float32)] * 4
         + [
-            pltpu.VMEM(shard, jnp.bfloat16),
-            pltpu.SemaphoreType.DMA,
-            pltpu.SemaphoreType.DMA((PIECES, 4)),
-            pltpu.SemaphoreType.DMA((PIECES, 3)),
-            pltpu.SemaphoreType.DMA((PIECES, chips)),
+            pltpu.VMEM((len(outs),) + shard, kind),
+            pltpu.SemaphoreType.DMA((5,)),
+            pltpu.SemaphoreType.DMA((copies,)),
         ],
-        compiler_params=pltpu.CompilerParams(vmem_limit_bytes=60 * 2**20),
+        compiler_params=pltpu.CompilerParams(vmem_limit_bytes=(60 if chips else 54) * 2**20),
         cost_estimate=pl.CostEstimate(
-            flops=30 * master.size, bytes_accessed=60 * master.size, transcendentals=3 * master.size
+            flops=30 * master.size, bytes_accessed=28 * master.size, transcendentals=3 * master.size
         ),
     )(step_count.reshape(1, 1), master, moment, second, gradient)
 
@@ -283,9 +267,7 @@
     part = old_weights.shape[1] // size
     code = lambda n: jax.ShapeDtypeStruct((n + TAIL, part), jnp.int16)
     full = jax.ShapeDtypeStruct((count, part), jnp.float32)
-    new_master, new_moment, new_second, spread = updated(
-        step_count, master, moment, second, gradient, chips
-    )
+    (spread,) = updated(step_count, master, moment, second, gradient, chips)
     mine = lax.all_to_all(spread, CHIPS, split_axis=0, concat_axis=0, tiled=True)
     q3, q5, q4a, q4b, q1, q7, p2, p6, p0 = products(
         products_kernel, branch_rows, old_weights, me, ((3, 5), (4, 0), (2, 6), (1, 7)),
@@ -296,6 +278,9 @@
     r1, r7 = along_tp(q1, 1), along_tp(q7, -1)
     q2, q6 = local_call(merge_kernel, [code(count), code(count)], p2, r3, r4a, p6, r5, r4b)
     r2, r6 = along_tp(q2, 2), along_tp(q6, -2)
+    late = lax.optimization_barrier((master, q2, q6))[0]
+    new_master, new_moment, new_second = updated(step_count, late, moment, second, gradient)
+    p0 = lax.optimization_barrier((p0, new_master))[0]
     replicas = lax.axis_size(PLANE)
     slots_each = 2 * count // replicas
     places = replicas * slots_each

time: 61.8 us -> 61.6 us (level)
  waiting for transfers between devices: 14.1 us -> 11.6 us
  Pallas kernels: 15.6 us -> 17.8 us
    ppermute x8, waiting for transfers between devices: 7.61 us -> 5.15 us  [along_tp(): lax.ppermute(value, 'tp', [(i, (i + step) % size) for i in range(size)])]
    pallas_call x1 -> x2, Pallas kernels: 3.17 us -> 5.44 us  [updated(): pl.pallas_call(update_kernel, out_shape=outs, in_specs=[anywhere] * 5, ou...]
  transfers between devices with their start and end apart: 11 -> 11, of which waited for: 5 -> 4; matrix products, arithmetic and copies ran while one was open for 0% -> 0% of each run, Pallas kernels for 20% -> 24%
where the time goes in v12:
time: 61.6 us; the launch traced here: 61.3 us
  starting transfers between devices  29.7 us (48%)
  Pallas kernels  17.8 us (29%)
  waiting for transfers between devices  11.6 us (19%)
  between operations  1.39 us (2%)
  local copies, waits for them, and re-layouts  0.71 us (1%)
    ppermute x8, starting transfers between devices, along_tp(): lax.ppermute(value, 'tp', [(i, (i + step) % size) for i in range(size)])  13.5 us
    all_to_all x1, starting transfers between devices, local(): lax.all_to_all(spread, CHIPS, split_axis=0, concat_axis=0, tiled=True)  7.6 us
    all_to_all x1, starting transfers between devices, local(): lax.all_to_all(placed, PLANE, split_axis=0, concat_axis=0, tiled=True)  6.48 us
    pallas_call x2, Pallas kernels, set_half(): pl.pallas_call(half_kernel, out_shape=jax.ShapeDtypeStruct((lanes, 2, row...  5.64 us
    pallas_call x2, Pallas kernels, updated(): pl.pallas_call(update_kernel, out_shape=outs, in_specs=[anywhere] * 5, ou...  5.44 us
    ppermute x8, waiting for transfers between devices, along_tp(): lax.ppermute(value, 'tp', [(i, (i + step) % size) for i in range(size)])  5.15 us
    pallas_call x1, Pallas kernels, products(): pl.pallas_call(functools.partial(loading, steps, places, kernel), out_sha...  4.56 us
    all_to_all x1, waiting for transfers between devices, local(): lax.all_to_all(placed, PLANE, split_axis=0, concat_axis=0, tiled=True)  3.41 us
  transfers between devices with their start and end apart: 11, of which 4 were waited for; matrix products, arithmetic and copies ran while one was open for 0% of the time, Pallas kernels for 24%

profile of v12, /device:TPU:1, one launch (start us, length us, event | category | flops | bytes accessed | tf_op | source)
XLA Modules:
  0.0 61.3 jit_solution(6302243268887995799)
XLA Ops:
  1.3 3.0 %shard_map.122 = bf16[16,64,1024]{2,1,0:T(8,128)(2,1)} custom-call(s32[1,1]{1,0:T(1,128)} %bitcast.10.step_h, f32[64,1024]{1,0:T(8,128)} %master_h.2, f32[64,1024]{1,0:T(8,128)} %moment_h.3, f32[64,1024]{1,0:T(8,128)} %second_h.3, f32[64,1024]{1,0:T(8,128)} %gradient_h.3), custom_call_target="tpu_custom_call" | custom-call | flops 1966080 | bytes 1835008 | tf_op jit(solution)/shard_map/pallas_call | solution.py:97
  4.3 7.6 %all-to-all-start = ((bf16[16,64,1024]{2,1,0:T(8,128)(2,1)}), bf16[16,64,1024]{2,1,0:T(8,128)(2,1)S(1)}, u32[]{:S(2)}, u32[]{:S(2)}) async-start(bf16[16,64,1024]{2,1,0:T(8,128)(2,1)} %shard_map.122), calls=%async_computation | async-start | bytes 4194304 | tf_op jit(solution)/shard_map/all_to_all | solution.py:271
  11.9 0.0 copy-start
  11.9 4.6 %shard_map.119 = (s16[528,128]{1,0:T(8,128)(2,1)S(1)}, s16[528,128]{1,0:T(8,128)(2,1)S(1)}, s16[272,128]{1,0:T(8,128)(2,1)S(1)}, s16[272,128]{1,0:T(8,128)(2,1)S...) custom-call(s32[1]{0:T(128)} %bitcast.1.me, ...), custom_call_target="tpu_custom_call" | custom-call | flops 2147483648 | bytes 6291456 | tf_op jit(solution)/shard_map/pallas_call | solution.py:169
  16.5 1.7 %collective-permute-start = (s16[528,128]{1,0:T(8,128)(2,1)S(1)}, s16[528,128]{1,0:T(8,128)(2,1)S(1)}, u32[]{:S(2)}, u32[]{:S(2)}) collective-permute-start(s16[528,128]{1,0:T(8,128)(2,1)S(1)} %get-tuple-element.25), channel_id=1, source_target_pairs={{0,1},{1,2},{2,3},{3,4},{4,5},{5,6},{6,7},{7,0},{8,9},{9,10},{10,1... | collective-permute-start | bytes 405512 | tf_op jit(solution)/shard_map/ppermute | solution.py:258
  18.2 4.0 %collective-permute-start.2 = (s16[528,128]{1,0:T(8,128)(2,1)S(1)}, s16[528,128]{1,0:T(8,128)(2,1)S(1)}, u32[]{:S(2)}, u32[]{:S(2)}) collective-permute-start(s16[528,128]{1,0:T(8,128)(2,1)S(1)} %get-tuple-element.28), channel_id=1, source_target_pairs={{0,7},{1,0},{2,1},{3,2},{4,3},{5,4},{6,5},{7,6},{8,15},{9,8},{10,9... | collective-permute-start | bytes 405512 | tf_op jit(solution)/shard_map/ppermute | solution.py:258
  22.2 0.0 collective-permute-start.1
  22.2 3.6 %collective-permute-start.3 = (s16[272,128]{1,0:T(8,128)(2,1)S(1)}, s16[272,128]{1,0:T(8,128)(2,1)S(1)}, u32[]{:S(2)}, u32[]{:S(2)}) collective-permute-start(s16[272,128]{1,0:T(8,128)(2,1)S(1)} %get-tuple-element.29), channel_id=1, source_target_pairs={{0,6},{1,7},{2,0},{3,1},{4,2},{5,3},{6,4},{7,5},{8,14},{9,15},{10,... | collective-permute-start | bytes 208904 | tf_op jit(solution)/shard_map/ppermute | solution.py:258
  25.8 0.0 collective-permute-start.4
  25.8 3.0 %collective-permute-done.1.far_a = s16[272,128]{1,0:T(8,128)(2,1)S(1)} collective-permute-done((s16[272,128]{1,0:T(8,128)(2,1)S(1)}, s16[272,128]{1,0:T(8,128)(2,1)S(1)}, u32[]{:S(2)}, u32[]{:S(2)}) %collective-permute-start.1) | collective-permute-done | bytes 69664 | tf_op jit(solution)/shard_map/ppermute | solution.py:258
  28.8 0.6 collective-permute-start.5
  29.3 0.0 collective-permute-done.3.far_b
  29.3 0.0 collective-permute-done.next_a
  29.3 0.0 collective-permute-done.2.next_b
  29.4 0.3 shard_map.120
  29.6 3.0 %collective-permute-start.6 = (s16[528,128]{1,0:T(8,128)(2,1)S(1)}, s16[528,128]{1,0:T(8,128)(2,1)S(1)}, u32[]{:S(2)}, u32[]{:S(2)}) collective-permute-start(s16[528,128]{1,0:T(8,128)(2,1)S(1)} %get-tuple-element.30), channel_id=1, source_target_pairs={{0,2},{1,3},{2,4},{3,5},{4,6},{5,7},{6,0},{7,1},{8,10},{9,11},{10,... | collective-permute-start | bytes 405512 | tf_op jit(solution)/shard_map/ppermute | solution.py:258
  32.7 0.6 %collective-permute-start.7 = (s16[528,128]{1,0:T(8,128)(2,1)S(1)}, s16[528,128]{1,0:T(8,128)(2,1)S(1)}, u32[]{:S(2)}, u32[]{:S(2)}) collective-permute-start(s16[528,128]{1,0:T(8,128)(2,1)S(1)} %get-tuple-element.31), channel_id=1, source_target_pairs={{0,6},{1,7},{2,0},{3,1},{4,2},{5,3},{6,4},{7,5},{8,14},{9,15},{10,... | collective-permute-start | bytes 405512 | tf_op jit(solution)/shard_map/ppermute | solution.py:258
  33.3 0.0 copy-done
  33.3 0.6 %shard_map.123.selector = bf16[1024,512]{1,0:T(8,128)(2,1)S(1)} custom-call(s32[1,512]{1,0:T(1,128)S(1)} %bitcast.12), custom_call_target="tpu_custom_call" | custom-call | bytes 1048576 | tf_op jit(solution)/shard_map/pallas_call | solution.py:191
  33.9 2.4 %shard_map.121 = (f32[64,1024]{1,0:T(8,128)}, f32[64,1024]{1,0:T(8,128)}, f32[64,1024]{1,0:T(8,128)}) custom-call(s32[1,1]{1,0:T(1,128)} %bitcast.9.step_h, f32[64,1024]{1,0:T(8,128)} %master_h.2, f32[64,1024]{1,0:T(8,128)} %moment_h.3, f32[64,1024]{1,0:T(8,128)} %second_h.3, f32[64,1024]{1,0:T(8,128)} %gradient_h.3), custom_call_target="tpu_custom_call" | custom-call | flops 1966080 | bytes 1835008 | tf_op jit(solution)/shard_map/pallas_call | solution.py:97
  36.4 0.0 collective-permute-done.4.ra
  36.4 0.0 collective-permute-done.5.rb
  36.4 0.0 collective-permute-done.6.rc
  36.4 2.1 %collective-permute-done.7.rd = s16[528,128]{1,0:T(8,128)(2,1)S(1)} collective-permute-done((s16[528,128]{1,0:T(8,128)(2,1)S(1)}, s16[528,128]{1,0:T(8,128)(2,1)S(1)}, u32[]{:S(2)}, u32[]{:S(2)}) %collective-permute-start.7) | collective-permute-done | bytes 135200 | tf_op jit(solution)/shard_map/ppermute | solution.py:258
  38.6 1.3 %shard_map.124 = bf16[1024,128]{1,0:T(8,128)(2,1)} custom-call(f32[512,128]{1,0:T(8,128)S(1)} %get-tuple-element.37.own, s16[528,128]{1,0:T(8,128)(2,1)S(1)} %collective-permute-done.4.ra, s16[528,128]{1,0:T(8,128)(2,1)S(1)} %collective-permute-done.5.rb, s16[528,128]{1,0:T(8,128)(2,1)S(1)} %collective-permute-done.6.rc, ...), custom_call_target="tpu_custom_call" | custom-call | bytes 1048576 | tf_op jit(solution)/shard_map/pallas_call | solution.py:191
  39.8 3.0 %all-to-all-done = bf16[16,64,1024]{2,1,0:T(8,128)(2,1)S(1)} async-done(((bf16[16,64,1024]{2,1,0:T(8,128)(2,1)}), bf16[16,64,1024]{2,1,0:T(8,128)(2,1)S(1)}, u32[]{:S(2)}, u32[]{:S(2)}) %all-to-all-start) | async-done | bytes 2097184 | tf_op jit(solution)/shard_map/all_to_all | solution.py:271
  42.9 2.2 %collective-permute-start.8 = (bf16[16,64,1024]{2,1,0:T(8,128)(2,1)S(1)}, bf16[16,64,1024]{2,1,0:T(8,128)(2,1)}, u32[]{:S(2)}, u32[]{:S(2)}) collective-permute-start(bf16[16,64,1024]{2,1,0:T(8,128)(2,1)S(1)} %all-to-all-done), channel_id=1, source_target_pairs={{0,64},{64,0},{1,65},{65,1},{2,66},{66,2},{3,67},{67,3},{4,68},{68... | collective-permute-start | bytes 6291464 | tf_op jit(solution)/shard_map/ppermute | solution.py:296
  45.0 6.5 %all-to-all-start.1 = ((bf16[32,32,128]{2,1,0:T(8,128)(2,1)}), bf16[32,32,128]{2,1,0:T(8,128)(2,1)S(1)}, u32[]{:S(2)}, u32[]{:S(2)}) async-start(bf16[32,32,128]{2,1,0:T(8,128)(2,1)} %bitcast.6), calls=%async_computation.1 | async-start | bytes 524288 | tf_op jit(solution)/shard_map/all_to_all | solution.py:295
  51.5 1.9 %shard_map.125.refs_0_ = bf16[2,2,512,1024]{3,2,1,0:T(8,128)(2,1)} custom-call(s32[1]{0:T(128)} %bitcast.2.place, bf16[2,512,1024]{2,1,0:T(8,128)(2,1)S(1)} %bitcast.11), custom_call_target="tpu_custom_call" | custom-call | bytes 4194304 | tf_op jit(solution)/shard_map/pallas_call | solution.py:240
  53.4 0.0 collective-permute-done.8
  53.4 3.8 %shard_map.126 = bf16[2,2,512,1024]{3,2,1,0:T(8,128)(2,1)} custom-call(s32[1]{0:T(128)S(6)} %sub.3.place, bf16[2,512,1024]{2,1,0:T(8,128)(2,1)} %bitcast.4.half, bf16[2,2,512,1024]{3,2,1,0:T(8,128)(2,1)} %shard_map.125.refs_0_), custom_call_target="tpu_custom_call", output_to_operand_aliasing={{}: (2, {})} | custom-call | bytes 4194304 | tf_op jit(solution)/shard_map/pallas_call | solution.py:240
  57.2 3.4 %all-to-all-done.1 = bf16[32,32,128]{2,1,0:T(8,128)(2,1)S(1)} async-done(((bf16[32,32,128]{2,1,0:T(8,128)(2,1)}), bf16[32,32,128]{2,1,0:T(8,128)(2,1)S(1)}, u32[]{:S(2)}, u32[]{:S(2)}) %all-to-all-start.1) | async-done | bytes 262176 | tf_op jit(solution)/shard_map/all_to_all | solution.py:295
  60.6 0.7 %copy.17 = bf16[1,32,32,128]{3,2,1,0:T(8,128)(2,1)} copy(bf16[1,32,32,128]{3,2,1,0:T(8,128)(2,1)S(1)} %bitcast.14) | data formatting | bytes 524288
Async XLA Ops:
  4.3 38.6 %all-to-all-start = ((bf16[16,64,1024]{2,1,0:T(8,128)(2,1)}), bf16[16,64,1024]{2,1,0:T(8,128)(2,1)S(1)}, u32[]{:S(2)}, u32[]{:S(2)}) async-start(bf16[16,64,1024]{2,1,0:T(8,128)(2,1)} %shard_map.122), calls=%async_computation | async-start | bytes 4194304 | tf_op jit(solution)/shard_map/all_to_all | solution.py:271
  11.9 21.4 %copy-start = (s32[512,1]{0,1:T(1,128)S(1)}, s32[512,1]{0,1:T(1,128)}, u32[]{:S(2)}) copy-start(s32[512,1]{0,1:T(1,128)} %param.15) | copy-start | bytes 6148
  16.5 12.9 %collective-permute-start = (s16[528,128]{1,0:T(8,128)(2,1)S(1)}, s16[528,128]{1,0:T(8,128)(2,1)S(1)}, u32[]{:S(2)}, u32[]{:S(2)}) collective-permute-start(s16[528,128]{1,0:T(8,128)(2,1)S(1)} %get-tuple-element.25), channel_id=1, source_target_pairs={{0,1},{1,2},{2,3},{3,4},{4,5},{5,6},{6,7},{7,0},{8,9},{9,10},{10,1... | collective-permute-start | bytes 405512 | tf_op jit(solution)/shard_map/ppermute | solution.py:258
  18.2 11.2 %collective-permute-start.2 = (s16[528,128]{1,0:T(8,128)(2,1)S(1)}, s16[528,128]{1,0:T(8,128)(2,1)S(1)}, u32[]{:S(2)}, u32[]{:S(2)}) collective-permute-start(s16[528,128]{1,0:T(8,128)(2,1)S(1)} %get-tuple-element.28), channel_id=1, source_target_pairs={{0,7},{1,0},{2,1},{3,2},{4,3},{5,4},{6,5},{7,6},{8,15},{9,8},{10,9... | collective-permute-start | bytes 405512 | tf_op jit(solution)/shard_map/ppermute | solution.py:258
  22.2 6.6 %collective-permute-start.1 = (s16[272,128]{1,0:T(8,128)(2,1)S(1)}, s16[272,128]{1,0:T(8,128)(2,1)S(1)}, u32[]{:S(2)}, u32[]{:S(2)}) collective-permute-start(s16[272,128]{1,0:T(8,128)(2,1)S(1)} %get-tuple-element.26), channel_id=1, source_target_pairs={{0,2},{1,3},{2,4},{3,5},{4,6},{5,7},{6,0},{7,1},{8,10},{9,11},{10,... | collective-permute-start | bytes 208904 | tf_op jit(solution)/shard_map/ppermute | solution.py:258
  22.2 7.2 %collective-permute-start.3 = (s16[272,128]{1,0:T(8,128)(2,1)S(1)}, s16[272,128]{1,0:T(8,128)(2,1)S(1)}, u32[]{:S(2)}, u32[]{:S(2)}) collective-permute-start(s16[272,128]{1,0:T(8,128)(2,1)S(1)} %get-tuple-element.29), channel_id=1, source_target_pairs={{0,6},{1,7},{2,0},{3,1},{4,2},{5,3},{6,4},{7,5},{8,14},{9,15},{10,... | collective-permute-start | bytes 208904 | tf_op jit(solution)/shard_map/ppermute | solution.py:258
  25.8 10.6 %collective-permute-start.4 = (s16[528,128]{1,0:T(8,128)(2,1)S(1)}, s16[528,128]{1,0:T(8,128)(2,1)S(1)}, u32[]{:S(2)}, u32[]{:S(2)}) collective-permute-start(s16[528,128]{1,0:T(8,128)(2,1)S(1)} %get-tuple-element.38), channel_id=1, source_target_pairs={{0,1},{1,2},{2,3},{3,4},{4,5},{5,6},{6,7},{7,0},{8,9},{9,10},{10,1... | collective-permute-start | bytes 405512 | tf_op jit(solution)/shard_map/ppermute | solution.py:258
  28.8 7.6 %collective-permute-start.5 = (s16[528,128]{1,0:T(8,128)(2,1)S(1)}, s16[528,128]{1,0:T(8,128)(2,1)S(1)}, u32[]{:S(2)}, u32[]{:S(2)}) collective-permute-start(s16[528,128]{1,0:T(8,128)(2,1)S(1)} %get-tuple-element.39), channel_id=1, source_target_pairs={{0,7},{1,0},{2,1},{3,2},{4,3},{5,4},{6,5},{7,6},{8,15},{9,8},{10,9... | collective-permute-start | bytes 405512 | tf_op jit(solution)/shard_map/ppermute | solution.py:258
  29.6 6.8 %collective-permute-start.6 = (s16[528,128]{1,0:T(8,128)(2,1)S(1)}, s16[528,128]{1,0:T(8,128)(2,1)S(1)}, u32[]{:S(2)}, u32[]{:S(2)}) collective-permute-start(s16[528,128]{1,0:T(8,128)(2,1)S(1)} %get-tuple-element.30), channel_id=1, source_target_pairs={{0,2},{1,3},{2,4},{3,5},{4,6},{5,7},{6,0},{7,1},{8,10},{9,11},{10,... | collective-permute-start | bytes 405512 | tf_op jit(solution)/shard_map/ppermute | solution.py:258
  32.7 5.9 %collective-permute-start.7 = (s16[528,128]{1,0:T(8,128)(2,1)S(1)}, s16[528,128]{1,0:T(8,128)(2,1)S(1)}, u32[]{:S(2)}, u32[]{:S(2)}) collective-permute-start(s16[528,128]{1,0:T(8,128)(2,1)S(1)} %get-tuple-element.31), channel_id=1, source_target_pairs={{0,6},{1,7},{2,0},{3,1},{4,2},{5,3},{6,4},{7,5},{8,14},{9,15},{10,... | collective-permute-start | bytes 405512 | tf_op jit(solution)/shard_map/ppermute | solution.py:258
  42.9 10.5 %collective-permute-start.8 = (bf16[16,64,1024]{2,1,0:T(8,128)(2,1)S(1)}, bf16[16,64,1024]{2,1,0:T(8,128)(2,1)}, u32[]{:S(2)}, u32[]{:S(2)}) collective-permute-start(bf16[16,64,1024]{2,1,0:T(8,128)(2,1)S(1)} %all-to-all-done), channel_id=1, source_target_pairs={{0,64},{64,0},{1,65},{65,1},{2,66},{66,2},{3,67},{67,3},{4,68},{68... | collective-permute-start | bytes 6291464 | tf_op jit(solution)/shard_map/ppermute | solution.py:296
  45.0 15.5 %all-to-all-start.1 = ((bf16[32,32,128]{2,1,0:T(8,128)(2,1)}), bf16[32,32,128]{2,1,0:T(8,128)(2,1)S(1)}, u32[]{:S(2)}, u32[]{:S(2)}) async-start(bf16[32,32,128]{2,1,0:T(8,128)(2,1)} %bitcast.6), calls=%async_computation.1 | async-start | bytes 524288 | tf_op jit(solution)/shard_map/all_to_all | solution.py:295

commit v13 on v12

--- a/solution.py
+++ b/solution.py
@@ -275,9 +275,11 @@
     )
     r3, r5 = along_tp(q3, 1), along_tp(q5, -1)
     r4a, r4b = along_tp(q4a, 2), along_tp(q4b, -2)
-    r1, r7 = along_tp(q1, 1), along_tp(q7, -1)
+    r1 = along_tp(q1, 1)
     q2, q6 = local_call(merge_kernel, [code(count), code(count)], p2, r3, r4a, p6, r5, r4b)
     r2, r6 = along_tp(q2, 2), along_tp(q6, -2)
+    q7 = lax.optimization_barrier((q7, q2))[0]
+    r7 = along_tp(q7, -1)
     late = lax.optimization_barrier((master, q2, q6))[0]
     new_master, new_moment, new_second = updated(step_count, late, moment, second, gradient)
     p0 = lax.optimization_barrier((p0, new_master))[0]

time: 61.6 us -> 62.2 us (level)
  waiting for transfers between devices: 11.6 us -> 12.6 us
    all_to_all x1, waiting for transfers between devices: 3.03 us -> 3.75 us  [local(): lax.all_to_all(spread, CHIPS, split_axis=0, concat_axis=0, tiled=True)]
    ppermute x8, starting transfers between devices: 13.5 us -> 12.8 us  [along_tp(): lax.ppermute(value, 'tp', [(i, (i + step) % size) for i in range(size)])]
  transfers between devices with their start and end apart: 11 -> 11, of which waited for: 4 -> 6; matrix products, arithmetic and copies ran while one was open for 0% -> 0% of each run, Pallas kernels for 24% -> 24%
where the time goes in v13:
time: 62.2 us; the launch traced here: 61.8 us
  starting transfers between devices  29.3 us (47%)
  Pallas kernels  17.8 us (29%)
  waiting for transfers between devices  12.6 us (20%)
  between operations  1.38 us (2%)
  local copies, waits for them, and re-layouts  0.71 us (1%)
    ppermute x8, starting transfers between devices, along_tp(): lax.ppermute(value, 'tp', [(i, (i + step) % size) for i in range(size)])  12.8 us
    all_to_all x1, starting transfers between devices, local(): lax.all_to_all(spread, CHIPS, split_axis=0, concat_axis=0, tiled=True)  7.6 us
    all_to_all x1, starting transfers between devices, local(): lax.all_to_all(placed, PLANE, split_axis=0, concat_axis=0, tiled=True)  7.02 us
    pallas_call x2, Pallas kernels, set_half(): pl.pallas_call(half_kernel, out_shape=jax.ShapeDtypeStruct((lanes, 2, row...  5.64 us
    pallas_call x2, Pallas kernels, updated(): pl.pallas_call(update_kernel, out_shape=outs, in_specs=[anywhere] * 5, ou...  5.44 us
    ppermute x8, waiting for transfers between devices, along_tp(): lax.ppermute(value, 'tp', [(i, (i + step) % size) for i in range(size)])  5.4 us
    pallas_call x1, Pallas kernels, products(): pl.pallas_call(functools.partial(loading, steps, places, kernel), out_sha...  4.56 us
    all_to_all x1, waiting for transfers between devices, local(): lax.all_to_all(spread, CHIPS, split_axis=0, concat_axis=0, tiled=True)  3.75 us
  transfers between devices with their start and end apart: 11, of which 6 were waited for; matrix products, arithmetic and copies ran while one was open for 0% of the time, Pallas kernels for 24%

profile of v13, /device:TPU:1, one launch (start us, length us, event | category | flops | bytes accessed | tf_op | source)
XLA Modules:
  0.0 61.8 jit_solution(14973483511186291704)
XLA Ops:
  1.3 3.0 %shard_map.122 = bf16[16,64,1024]{2,1,0:T(8,128)(2,1)} custom-call(s32[1,1]{1,0:T(1,128)} %bitcast.10.step_h, f32[64,1024]{1,0:T(8,128)} %master_h.2, f32[64,1024]{1,0:T(8,128)} %moment_h.3, f32[64,1024]{1,0:T(8,128)} %second_h.3, f32[64,1024]{1,0:T(8,128)} %gradient_h.3), custom_call_target="tpu_custom_call" | custom-call | flops 1966080 | bytes 1835008 | tf_op jit(solution)/shard_map/pallas_call | solution.py:97
  4.3 7.6 %all-to-all-start = ((bf16[16,64,1024]{2,1,0:T(8,128)(2,1)}), bf16[16,64,1024]{2,1,0:T(8,128)(2,1)S(1)}, u32[]{:S(2)}, u32[]{:S(2)}) async-start(bf16[16,64,1024]{2,1,0:T(8,128)(2,1)} %shard_map.122), calls=%async_computation | async-start | bytes 4194304 | tf_op jit(solution)/shard_map/all_to_all | solution.py:271
  11.9 0.0 copy-start
  11.9 4.6 %shard_map.119 = (s16[528,128]{1,0:T(8,128)(2,1)S(1)}, s16[528,128]{1,0:T(8,128)(2,1)S(1)}, s16[272,128]{1,0:T(8,128)(2,1)S(1)}, s16[272,128]{1,0:T(8,128)(2,1)S...) custom-call(s32[1]{0:T(128)} %bitcast.1.me, ...), custom_call_target="tpu_custom_call" | custom-call | flops 2147483648 | bytes 6291456 | tf_op jit(solution)/shard_map/pallas_call | solution.py:169
  16.5 1.7 %collective-permute-start = (s16[528,128]{1,0:T(8,128)(2,1)S(1)}, s16[528,128]{1,0:T(8,128)(2,1)S(1)}, u32[]{:S(2)}, u32[]{:S(2)}) collective-permute-start(s16[528,128]{1,0:T(8,128)(2,1)S(1)} %get-tuple-element.26), channel_id=1, source_target_pairs={{0,1},{1,2},{2,3},{3,4},{4,5},{5,6},{6,7},{7,0},{8,9},{9,10},{10,1... | collective-permute-start | bytes 405512 | tf_op jit(solution)/shard_map/ppermute | solution.py:258
  18.2 4.0 %collective-permute-start.2 = (s16[528,128]{1,0:T(8,128)(2,1)S(1)}, s16[528,128]{1,0:T(8,128)(2,1)S(1)}, u32[]{:S(2)}, u32[]{:S(2)}) collective-permute-start(s16[528,128]{1,0:T(8,128)(2,1)S(1)} %get-tuple-element.29), channel_id=1, source_target_pairs={{0,7},{1,0},{2,1},{3,2},{4,3},{5,4},{6,5},{7,6},{8,15},{9,8},{10,9... | collective-permute-start | bytes 405512 | tf_op jit(solution)/shard_map/ppermute | solution.py:258
  22.2 0.0 collective-permute-start.1
  22.2 3.6 %collective-permute-start.3 = (s16[272,128]{1,0:T(8,128)(2,1)S(1)}, s16[272,128]{1,0:T(8,128)(2,1)S(1)}, u32[]{:S(2)}, u32[]{:S(2)}) collective-permute-start(s16[272,128]{1,0:T(8,128)(2,1)S(1)} %get-tuple-element.30), channel_id=1, source_target_pairs={{0,6},{1,7},{2,0},{3,1},{4,2},{5,3},{6,4},{7,5},{8,14},{9,15},{10,... | collective-permute-start | bytes 208904 | tf_op jit(solution)/shard_map/ppermute | solution.py:258
  25.8 0.0 collective-permute-start.4
  25.8 3.0 %collective-permute-done.1.far_a = s16[272,128]{1,0:T(8,128)(2,1)S(1)} collective-permute-done((s16[272,128]{1,0:T(8,128)(2,1)S(1)}, s16[272,128]{1,0:T(8,128)(2,1)S(1)}, u32[]{:S(2)}, u32[]{:S(2)}) %collective-permute-start.1) | collective-permute-done | bytes 69664 | tf_op jit(solution)/shard_map/ppermute | solution.py:258
  28.8 0.2 collective-permute-done.3.far_b
  29.0 0.0 collective-permute-done.next_a
  29.0 0.0 collective-permute-done.2.next_b
  29.0 0.3 shard_map.120
  29.3 0.4 collective-permute-start.5
  29.7 2.0 %collective-permute-start.7 = (s16[528,128]{1,0:T(8,128)(2,1)S(1)}, s16[528,128]{1,0:T(8,128)(2,1)S(1)}, u32[]{:S(2)}, u32[]{:S(2)}) collective-permute-start(s16[528,128]{1,0:T(8,128)(2,1)S(1)} %get-tuple-element.32), channel_id=1, source_target_pairs={{0,6},{1,7},{2,0},{3,1},{4,2},{5,3},{6,4},{7,5},{8,14},{9,15},{10,... | collective-permute-start | bytes 405512 | tf_op jit(solution)/shard_map/ppermute | solution.py:258
  31.7 1.2 %collective-permute-start.6 = (s16[528,128]{1,0:T(8,128)(2,1)S(1)}, s16[528,128]{1,0:T(8,128)(2,1)S(1)}, u32[]{:S(2)}, u32[]{:S(2)}) collective-permute-start(s16[528,128]{1,0:T(8,128)(2,1)S(1)} %get-tuple-element.31), channel_id=1, source_target_pairs={{0,2},{1,3},{2,4},{3,5},{4,6},{5,7},{6,0},{7,1},{8,10},{9,11},{10,... | collective-permute-start | bytes 405512 | tf_op jit(solution)/shard_map/ppermute | solution.py:258
  32.8 0.0 copy-done
  32.8 0.6 %shard_map.123.selector = bf16[1024,512]{1,0:T(8,128)(2,1)S(1)} custom-call(s32[1,512]{1,0:T(1,128)S(1)} %bitcast.12), custom_call_target="tpu_custom_call" | custom-call | bytes 1048576 | tf_op jit(solution)/shard_map/pallas_call | solution.py:191
  33.5 2.4 %shard_map.121 = (f32[64,1024]{1,0:T(8,128)}, f32[64,1024]{1,0:T(8,128)}, f32[64,1024]{1,0:T(8,128)}) custom-call(s32[1,1]{1,0:T(1,128)} %bitcast.9.step_h, f32[64,1024]{1,0:T(8,128)} %master_h.2, f32[64,1024]{1,0:T(8,128)} %moment_h.3, f32[64,1024]{1,0:T(8,128)} %second_h.3, f32[64,1024]{1,0:T(8,128)} %gradient_h.3), custom_call_target="tpu_custom_call" | custom-call | flops 1966080 | bytes 1835008 | tf_op jit(solution)/shard_map/pallas_call | solution.py:97
  35.9 0.0 collective-permute-done.4.ra
  36.0 0.0 collective-permute-done.5.rb
  36.0 1.7 %collective-permute-done.7.rd = s16[528,128]{1,0:T(8,128)(2,1)S(1)} collective-permute-done((s16[528,128]{1,0:T(8,128)(2,1)S(1)}, s16[528,128]{1,0:T(8,128)(2,1)S(1)}, u32[]{:S(2)}, u32[]{:S(2)}) %collective-permute-start.7) | collective-permute-done | bytes 135200 | tf_op jit(solution)/shard_map/ppermute | solution.py:258
  37.7 0.5 collective-permute-done.6.rc
  38.1 1.3 %shard_map.124 = bf16[1024,128]{1,0:T(8,128)(2,1)} custom-call(f32[512,128]{1,0:T(8,128)S(1)} %get-tuple-element.38.own, s16[528,128]{1,0:T(8,128)(2,1)S(1)} %collective-permute-done.4.ra, s16[528,128]{1,0:T(8,128)(2,1)S(1)} %collective-permute-done.5.rb, s16[528,128]{1,0:T(8,128)(2,1)S(1)} %collective-permute-done.6.rc, ...), custom_call_target="tpu_custom_call" | custom-call | bytes 1048576 | tf_op jit(solution)/shard_map/pallas_call | solution.py:191
  39.4 3.7 %all-to-all-done = bf16[16,64,1024]{2,1,0:T(8,128)(2,1)S(1)} async-done(((bf16[16,64,1024]{2,1,0:T(8,128)(2,1)}), bf16[16,64,1024]{2,1,0:T(8,128)(2,1)S(1)}, u32[]{:S(2)}, u32[]{:S(2)}) %all-to-all-start) | async-done | bytes 2097184 | tf_op jit(solution)/shard_map/all_to_all | solution.py:271
  43.2 1.9 %collective-permute-start.8 = (bf16[16,64,1024]{2,1,0:T(8,128)(2,1)S(1)}, bf16[16,64,1024]{2,1,0:T(8,128)(2,1)}, u32[]{:S(2)}, u32[]{:S(2)}) collective-permute-start(bf16[16,64,1024]{2,1,0:T(8,128)(2,1)S(1)} %all-to-all-done), channel_id=1, source_target_pairs={{0,64},{64,0},{1,65},{65,1},{2,66},{66,2},{3,67},{67,3},{4,68},{68... | collective-permute-start | bytes 6291464 | tf_op jit(solution)/shard_map/ppermute | solution.py:298
  45.0 7.0 %all-to-all-start.1 = ((bf16[32,32,128]{2,1,0:T(8,128)(2,1)}), bf16[32,32,128]{2,1,0:T(8,128)(2,1)S(1)}, u32[]{:S(2)}, u32[]{:S(2)}) async-start(bf16[32,32,128]{2,1,0:T(8,128)(2,1)} %bitcast.6), calls=%async_computation.1 | async-start | bytes 524288 | tf_op jit(solution)/shard_map/all_to_all | solution.py:297
  52.1 1.9 %shard_map.125.refs_0_ = bf16[2,2,512,1024]{3,2,1,0:T(8,128)(2,1)} custom-call(s32[1]{0:T(128)} %bitcast.2.place, bf16[2,512,1024]{2,1,0:T(8,128)(2,1)S(1)} %bitcast.11), custom_call_target="tpu_custom_call" | custom-call | bytes 4194304 | tf_op jit(solution)/shard_map/pallas_call | solution.py:240
  53.9 0.0 collective-permute-done.8
  53.9 3.8 %shard_map.126 = bf16[2,2,512,1024]{3,2,1,0:T(8,128)(2,1)} custom-call(s32[1]{0:T(128)S(6)} %sub.3.place, bf16[2,512,1024]{2,1,0:T(8,128)(2,1)} %bitcast.4.half, bf16[2,2,512,1024]{3,2,1,0:T(8,128)(2,1)} %shard_map.125.refs_0_), custom_call_target="tpu_custom_call", output_to_operand_aliasing={{}: (2, {})} | custom-call | bytes 4194304 | tf_op jit(solution)/shard_map/pallas_call | solution.py:240
  57.7 3.4 %all-to-all-done.1 = bf16[32,32,128]{2,1,0:T(8,128)(2,1)S(1)} async-done(((bf16[32,32,128]{2,1,0:T(8,128)(2,1)}), bf16[32,32,128]{2,1,0:T(8,128)(2,1)S(1)}, u32[]{:S(2)}, u32[]{:S(2)}) %all-to-all-start.1) | async-done | bytes 262176 | tf_op jit(solution)/shard_map/all_to_all | solution.py:297
  61.1 0.7 %copy.17 = bf16[1,32,32,128]{3,2,1,0:T(8,128)(2,1)} copy(bf16[1,32,32,128]{3,2,1,0:T(8,128)(2,1)S(1)} %bitcast.14) | data formatting | bytes 524288
Async XLA Ops:
  4.3 38.9 %all-to-all-start = ((bf16[16,64,1024]{2,1,0:T(8,128)(2,1)}), bf16[16,64,1024]{2,1,0:T(8,128)(2,1)S(1)}, u32[]{:S(2)}, u32[]{:S(2)}) async-start(bf16[16,64,1024]{2,1,0:T(8,128)(2,1)} %shard_map.122), calls=%async_computation | async-start | bytes 4194304 | tf_op jit(solution)/shard_map/all_to_all | solution.py:271
  11.9 20.9 %copy-start = (s32[512,1]{0,1:T(1,128)S(1)}, s32[512,1]{0,1:T(1,128)}, u32[]{:S(2)}) copy-start(s32[512,1]{0,1:T(1,128)} %param.15) | copy-start | bytes 6148
  16.5 12.5 %collective-permute-start = (s16[528,128]{1,0:T(8,128)(2,1)S(1)}, s16[528,128]{1,0:T(8,128)(2,1)S(1)}, u32[]{:S(2)}, u32[]{:S(2)}) collective-permute-start(s16[528,128]{1,0:T(8,128)(2,1)S(1)} %get-tuple-element.26), channel_id=1, source_target_pairs={{0,1},{1,2},{2,3},{3,4},{4,5},{5,6},{6,7},{7,0},{8,9},{9,10},{10,1... | collective-permute-start | bytes 405512 | tf_op jit(solution)/shard_map/ppermute | solution.py:258
  18.2 10.8 %collective-permute-start.2 = (s16[528,128]{1,0:T(8,128)(2,1)S(1)}, s16[528,128]{1,0:T(8,128)(2,1)S(1)}, u32[]{:S(2)}, u32[]{:S(2)}) collective-permute-start(s16[528,128]{1,0:T(8,128)(2,1)S(1)} %get-tuple-element.29), channel_id=1, source_target_pairs={{0,7},{1,0},{2,1},{3,2},{4,3},{5,4},{6,5},{7,6},{8,15},{9,8},{10,9... | collective-permute-start | bytes 405512 | tf_op jit(solution)/shard_map/ppermute | solution.py:258
  22.2 6.6 %collective-permute-start.1 = (s16[272,128]{1,0:T(8,128)(2,1)S(1)}, s16[272,128]{1,0:T(8,128)(2,1)S(1)}, u32[]{:S(2)}, u32[]{:S(2)}) collective-permute-start(s16[272,128]{1,0:T(8,128)(2,1)S(1)} %get-tuple-element.27), channel_id=1, source_target_pairs={{0,2},{1,3},{2,4},{3,5},{4,6},{5,7},{6,0},{7,1},{8,10},{9,11},{10,... | collective-permute-start | bytes 208904 | tf_op jit(solution)/shard_map/ppermute | solution.py:258
  22.2 6.8 %collective-permute-start.3 = (s16[272,128]{1,0:T(8,128)(2,1)S(1)}, s16[272,128]{1,0:T(8,128)(2,1)S(1)}, u32[]{:S(2)}, u32[]{:S(2)}) collective-permute-start(s16[272,128]{1,0:T(8,128)(2,1)S(1)} %get-tuple-element.30), channel_id=1, source_target_pairs={{0,6},{1,7},{2,0},{3,1},{4,2},{5,3},{6,4},{7,5},{8,14},{9,15},{10,... | collective-permute-start | bytes 208904 | tf_op jit(solution)/shard_map/ppermute | solution.py:258
  25.8 10.2 %collective-permute-start.4 = (s16[528,128]{1,0:T(8,128)(2,1)S(1)}, s16[528,128]{1,0:T(8,128)(2,1)S(1)}, u32[]{:S(2)}, u32[]{:S(2)}) collective-permute-start(s16[528,128]{1,0:T(8,128)(2,1)S(1)} %get-tuple-element.39), channel_id=1, source_target_pairs={{0,1},{1,2},{2,3},{3,4},{4,5},{5,6},{6,7},{7,0},{8,9},{9,10},{10,1... | collective-permute-start | bytes 405512 | tf_op jit(solution)/shard_map/ppermute | solution.py:258
  29.3 6.7 %collective-permute-start.5 = (s16[528,128]{1,0:T(8,128)(2,1)S(1)}, s16[528,128]{1,0:T(8,128)(2,1)S(1)}, u32[]{:S(2)}, u32[]{:S(2)}) collective-permute-start(s16[528,128]{1,0:T(8,128)(2,1)S(1)} %get-tuple-element.41), channel_id=1, source_target_pairs={{0,7},{1,0},{2,1},{3,2},{4,3},{5,4},{6,5},{7,6},{8,15},{9,8},{10,9... | collective-permute-start | bytes 405512 | tf_op jit(solution)/shard_map/ppermute | solution.py:258
  29.7 8.0 %collective-permute-start.7 = (s16[528,128]{1,0:T(8,128)(2,1)S(1)}, s16[528,128]{1,0:T(8,128)(2,1)S(1)}, u32[]{:S(2)}, u32[]{:S(2)}) collective-permute-start(s16[528,128]{1,0:T(8,128)(2,1)S(1)} %get-tuple-element.32), channel_id=1, source_target_pairs={{0,6},{1,7},{2,0},{3,1},{4,2},{5,3},{6,4},{7,5},{8,14},{9,15},{10,... | collective-permute-start | bytes 405512 | tf_op jit(solution)/shard_map/ppermute | solution.py:258
  31.7 6.4 %collective-permute-start.6 = (s16[528,128]{1,0:T(8,128)(2,1)S(1)}, s16[528,128]{1,0:T(8,128)(2,1)S(1)}, u32[]{:S(2)}, u32[]{:S(2)}) collective-permute-start(s16[528,128]{1,0:T(8,128)(2,1)S(1)} %get-tuple-element.31), channel_id=1, source_target_pairs={{0,2},{1,3},{2,4},{3,5},{4,6},{5,7},{6,0},{7,1},{8,10},{9,11},{10,... | collective-permute-start | bytes 405512 | tf_op jit(solution)/shard_map/ppermute | solution.py:258
  43.2 10.8 %collective-permute-start.8 = (bf16[16,64,1024]{2,1,0:T(8,128)(2,1)S(1)}, bf16[16,64,1024]{2,1,0:T(8,128)(2,1)}, u32[]{:S(2)}, u32[]{:S(2)}) collective-permute-start(bf16[16,64,1024]{2,1,0:T(8,128)(2,1)S(1)} %all-to-all-done), channel_id=1, source_target_pairs={{0,64},{64,0},{1,65},{65,1},{2,66},{66,2},{3,67},{67,3},{4,68},{68... | collective-permute-start | bytes 6291464 | tf_op jit(solution)/shard_map/ppermute | solution.py:298
  45.0 16.1 %all-to-all-start.1 = ((bf16[32,32,128]{2,1,0:T(8,128)(2,1)}), bf16[32,32,128]{2,1,0:T(8,128)(2,1)S(1)}, u32[]{:S(2)}, u32[]{:S(2)}) async-start(bf16[32,32,128]{2,1,0:T(8,128)(2,1)} %bitcast.6), calls=%async_computation.1 | async-start | bytes 524288 | tf_op jit(solution)/shard_map/all_to_all | solution.py:297

commit v14 on v12

--- a/solution.py
+++ b/solution.py
@@ -275,9 +275,10 @@
     )
     r3, r5 = along_tp(q3, 1), along_tp(q5, -1)
     r4a, r4b = along_tp(q4a, 2), along_tp(q4b, -2)
-    r1, r7 = along_tp(q1, 1), along_tp(q7, -1)
     q2, q6 = local_call(merge_kernel, [code(count), code(count)], p2, r3, r4a, p6, r5, r4b)
     r2, r6 = along_tp(q2, 2), along_tp(q6, -2)
+    q1, q7, _ = lax.optimization_barrier((q1, q7, q2))
+    r1, r7 = along_tp(q1, 1), along_tp(q7, -1)
     late = lax.optimization_barrier((master, q2, q6))[0]
     new_master, new_moment, new_second = updated(step_count, late, moment, second, gradient)
     p0 = lax.optimization_barrier((p0, new_master))[0]

time: 61.6 us -> 63 us (1.023)
  starting transfers between devices: 29.7 us -> 31.7 us
    all_to_all x1, waiting for transfers between devices: 3.03 us -> 0.01 us  [local(): lax.all_to_all(spread, CHIPS, split_axis=0, concat_axis=0, tiled=True)]
    ppermute x8, waiting for transfers between devices: 5.15 us -> 7.58 us  [along_tp(): lax.ppermute(value, 'tp', [(i, (i + step) % size) for i in range(size)])]
    ppermute x8, starting transfers between devices: 13.5 us -> 14.4 us  [along_tp(): lax.ppermute(value, 'tp', [(i, (i + step) % size) for i in range(size)])]
    all_to_all x1, starting transfers between devices: 6.48 us -> 7.15 us  [local(): lax.all_to_all(placed, PLANE, split_axis=0, concat_axis=0, tiled=True)]
where the time goes in v14:
time: 63 us; the launch traced here: 62.7 us
  starting transfers between devices  31.7 us (50%)
  Pallas kernels  17.8 us (28%)
  waiting for transfers between devices  11 us (17%)
  between operations  1.38 us (2%)
  local copies, waits for them, and re-layouts  0.71 us (1%)
    ppermute x8, starting transfers between devices, along_tp(): lax.ppermute(value, 'tp', [(i, (i + step) % size) for i in range(size)])  14.4 us
    all_to_all x1, starting transfers between devices, local(): lax.all_to_all(spread, CHIPS, split_axis=0, concat_axis=0, tiled=True)  7.6 us
    ppermute x8, waiting for transfers between devices, along_tp(): lax.ppermute(value, 'tp', [(i, (i + step) % size) for i in range(size)])  7.58 us
    all_to_all x1, starting transfers between devices, local(): lax.all_to_all(placed, PLANE, split_axis=0, concat_axis=0, tiled=True)  7.15 us
    pallas_call x2, Pallas kernels, set_half(): pl.pallas_call(half_kernel, out_shape=jax.ShapeDtypeStruct((lanes, 2, row...  5.64 us
    pallas_call x2, Pallas kernels, updated(): pl.pallas_call(update_kernel, out_shape=outs, in_specs=[anywhere] * 5, ou...  5.44 us
    pallas_call x1, Pallas kernels, products(): pl.pallas_call(functools.partial(loading, steps, places, kernel), out_sha...  4.56 us
    all_to_all x1, waiting for transfers between devices, local(): lax.all_to_all(placed, PLANE, split_axis=0, concat_axis=0, tiled=True)  3.41 us
  transfers between devices with their start and end apart: 11, of which 4 were waited for; matrix products, arithmetic and copies ran while one was open for 0% of the time, Pallas kernels for 24%

profile of v14, /device:TPU:1, one launch (start us, length us, event | category | flops | bytes accessed | tf_op | source)
XLA Modules:
  0.0 62.7 jit_solution(9227728635991461157)
XLA Ops:
  1.3 3.0 %shard_map.122 = bf16[16,64,1024]{2,1,0:T(8,128)(2,1)} custom-call(s32[1,1]{1,0:T(1,128)} %bitcast.10.step_h, f32[64,1024]{1,0:T(8,128)} %master_h.2, f32[64,1024]{1,0:T(8,128)} %moment_h.3, f32[64,1024]{1,0:T(8,128)} %second_h.3, f32[64,1024]{1,0:T(8,128)} %gradient_h.3), custom_call_target="tpu_custom_call" | custom-call | flops 1966080 | bytes 1835008 | tf_op jit(solution)/shard_map/pallas_call | solution.py:97
  4.3 7.6 %all-to-all-start = ((bf16[16,64,1024]{2,1,0:T(8,128)(2,1)}), bf16[16,64,1024]{2,1,0:T(8,128)(2,1)S(1)}, u32[]{:S(2)}, u32[]{:S(2)}) async-start(bf16[16,64,1024]{2,1,0:T(8,128)(2,1)} %shard_map.122), calls=%async_computation | async-start | bytes 4194304 | tf_op jit(solution)/shard_map/all_to_all | solution.py:271
  11.9 0.0 copy-start
  11.9 4.6 %shard_map.119 = (s16[528,128]{1,0:T(8,128)(2,1)S(1)}, s16[528,128]{1,0:T(8,128)(2,1)S(1)}, s16[272,128]{1,0:T(8,128)(2,1)S(1)}, s16[272,128]{1,0:T(8,128)(2,1)S...) custom-call(s32[1]{0:T(128)} %bitcast.1.me, ...), custom_call_target="tpu_custom_call" | custom-call | flops 2147483648 | bytes 6291456 | tf_op jit(solution)/shard_map/pallas_call | solution.py:169
  16.5 1.7 %collective-permute-start = (s16[528,128]{1,0:T(8,128)(2,1)S(1)}, s16[528,128]{1,0:T(8,128)(2,1)S(1)}, u32[]{:S(2)}, u32[]{:S(2)}) collective-permute-start(s16[528,128]{1,0:T(8,128)(2,1)S(1)} %get-tuple-element.27), channel_id=1, source_target_pairs={{0,1},{1,2},{2,3},{3,4},{4,5},{5,6},{6,7},{7,0},{8,9},{9,10},{10,1... | collective-permute-start | bytes 405512 | tf_op jit(solution)/shard_map/ppermute | solution.py:258
  18.2 4.0 %collective-permute-start.2 = (s16[528,128]{1,0:T(8,128)(2,1)S(1)}, s16[528,128]{1,0:T(8,128)(2,1)S(1)}, u32[]{:S(2)}, u32[]{:S(2)}) collective-permute-start(s16[528,128]{1,0:T(8,128)(2,1)S(1)} %get-tuple-element.30), channel_id=1, source_target_pairs={{0,7},{1,0},{2,1},{3,2},{4,3},{5,4},{6,5},{7,6},{8,15},{9,8},{10,9... | collective-permute-start | bytes 405512 | tf_op jit(solution)/shard_map/ppermute | solution.py:258
  22.2 0.0 collective-permute-start.1
  22.2 3.6 %collective-permute-start.3 = (s16[272,128]{1,0:T(8,128)(2,1)S(1)}, s16[272,128]{1,0:T(8,128)(2,1)S(1)}, u32[]{:S(2)}, u32[]{:S(2)}) collective-permute-start(s16[272,128]{1,0:T(8,128)(2,1)S(1)} %get-tuple-element.31), channel_id=1, source_target_pairs={{0,6},{1,7},{2,0},{3,1},{4,2},{5,3},{6,4},{7,5},{8,14},{9,15},{10,... | collective-permute-start | bytes 208904 | tf_op jit(solution)/shard_map/ppermute | solution.py:258
  25.8 3.0 %collective-permute-done.1.far_a = s16[272,128]{1,0:T(8,128)(2,1)S(1)} collective-permute-done((s16[272,128]{1,0:T(8,128)(2,1)S(1)}, s16[272,128]{1,0:T(8,128)(2,1)S(1)}, u32[]{:S(2)}, u32[]{:S(2)}) %collective-permute-start.1) | collective-permute-done | bytes 69664 | tf_op jit(solution)/shard_map/ppermute | solution.py:258
  28.8 0.2 collective-permute-done.3.far_b
  29.0 0.0 collective-permute-done.next_a
  29.0 0.0 collective-permute-done.2.next_b
  29.0 0.3 shard_map.120
  29.3 0.1 collective-permute-start.4
  29.4 2.7 %collective-permute-start.5 = (s16[528,128]{1,0:T(8,128)(2,1)S(1)}, s16[528,128]{1,0:T(8,128)(2,1)S(1)}, u32[]{:S(2)}, u32[]{:S(2)}) collective-permute-start(s16[528,128]{1,0:T(8,128)(2,1)S(1)} %get-tuple-element.43), channel_id=1, source_target_pairs={{0,7},{1,0},{2,1},{3,2},{4,3},{5,4},{6,5},{7,6},{8,15},{9,8},{10,9... | collective-permute-start | bytes 405512 | tf_op jit(solution)/shard_map/ppermute | solution.py:258
  32.0 1.0 %collective-permute-start.7 = (s16[528,128]{1,0:T(8,128)(2,1)S(1)}, s16[528,128]{1,0:T(8,128)(2,1)S(1)}, u32[]{:S(2)}, u32[]{:S(2)}) collective-permute-start(s16[528,128]{1,0:T(8,128)(2,1)S(1)} %get-tuple-element.33), channel_id=1, source_target_pairs={{0,6},{1,7},{2,0},{3,1},{4,2},{5,3},{6,4},{7,5},{8,14},{9,15},{10,... | collective-permute-start | bytes 405512 | tf_op jit(solution)/shard_map/ppermute | solution.py:258
  33.1 1.3 %collective-permute-start.6 = (s16[528,128]{1,0:T(8,128)(2,1)S(1)}, s16[528,128]{1,0:T(8,128)(2,1)S(1)}, u32[]{:S(2)}, u32[]{:S(2)}) collective-permute-start(s16[528,128]{1,0:T(8,128)(2,1)S(1)} %get-tuple-element.32), channel_id=1, source_target_pairs={{0,2},{1,3},{2,4},{3,5},{4,6},{5,7},{6,0},{7,1},{8,10},{9,11},{10,... | collective-permute-start | bytes 405512 | tf_op jit(solution)/shard_map/ppermute | solution.py:258
  34.4 0.0 copy-done
  34.4 0.6 %shard_map.123.selector = bf16[1024,512]{1,0:T(8,128)(2,1)S(1)} custom-call(s32[1,512]{1,0:T(1,128)S(1)} %bitcast.12), custom_call_target="tpu_custom_call" | custom-call | bytes 1048576 | tf_op jit(solution)/shard_map/pallas_call | solution.py:191
  35.1 2.4 %shard_map.121 = (f32[64,1024]{1,0:T(8,128)}, f32[64,1024]{1,0:T(8,128)}, f32[64,1024]{1,0:T(8,128)}) custom-call(s32[1,1]{1,0:T(1,128)} %bitcast.9.step_h, f32[64,1024]{1,0:T(8,128)} %master_h.2, f32[64,1024]{1,0:T(8,128)} %moment_h.3, f32[64,1024]{1,0:T(8,128)} %second_h.3, f32[64,1024]{1,0:T(8,128)} %gradient_h.3), custom_call_target="tpu_custom_call" | custom-call | flops 1966080 | bytes 1835008 | tf_op jit(solution)/shard_map/pallas_call | solution.py:97
  37.5 0.0 collective-permute-done.4.ra
  37.5 0.0 collective-permute-done.5.rb
  37.5 4.3 %collective-permute-done.7.rd = s16[528,128]{1,0:T(8,128)(2,1)S(1)} collective-permute-done((s16[528,128]{1,0:T(8,128)(2,1)S(1)}, s16[528,128]{1,0:T(8,128)(2,1)S(1)}, u32[]{:S(2)}, u32[]{:S(2)}) %collective-permute-start.7) | collective-permute-done | bytes 135200 | tf_op jit(solution)/shard_map/ppermute | solution.py:258
  41.9 0.0 collective-permute-done.6.rc
  41.9 1.3 %shard_map.124 = bf16[1024,128]{1,0:T(8,128)(2,1)} custom-call(f32[512,128]{1,0:T(8,128)S(1)} %get-tuple-element.39.own, s16[528,128]{1,0:T(8,128)(2,1)S(1)} %collective-permute-done.4.ra, s16[528,128]{1,0:T(8,128)(2,1)S(1)} %collective-permute-done.5.rb, s16[528,128]{1,0:T(8,128)(2,1)S(1)} %collective-permute-done.6.rc, ...), custom_call_target="tpu_custom_call" | custom-call | bytes 1048576 | tf_op jit(solution)/shard_map/pallas_call | solution.py:191
  43.2 0.0 all-to-all-done
  43.2 2.6 %collective-permute-start.8 = (bf16[16,64,1024]{2,1,0:T(8,128)(2,1)S(1)}, bf16[16,64,1024]{2,1,0:T(8,128)(2,1)}, u32[]{:S(2)}, u32[]{:S(2)}) collective-permute-start(bf16[16,64,1024]{2,1,0:T(8,128)(2,1)S(1)} %all-to-all-done), channel_id=1, source_target_pairs={{0,64},{64,0},{1,65},{65,1},{2,66},{66,2},{3,67},{67,3},{4,68},{68... | collective-permute-start | bytes 6291464 | tf_op jit(solution)/shard_map/ppermute | solution.py:297
  45.7 7.1 %all-to-all-start.1 = ((bf16[32,32,128]{2,1,0:T(8,128)(2,1)}), bf16[32,32,128]{2,1,0:T(8,128)(2,1)S(1)}, u32[]{:S(2)}, u32[]{:S(2)}) async-start(bf16[32,32,128]{2,1,0:T(8,128)(2,1)} %bitcast.6), calls=%async_computation.1 | async-start | bytes 524288 | tf_op jit(solution)/shard_map/all_to_all | solution.py:296
  52.9 1.9 %shard_map.125.refs_0_ = bf16[2,2,512,1024]{3,2,1,0:T(8,128)(2,1)} custom-call(s32[1]{0:T(128)} %bitcast.2.place, bf16[2,512,1024]{2,1,0:T(8,128)(2,1)S(1)} %bitcast.11), custom_call_target="tpu_custom_call" | custom-call | bytes 4194304 | tf_op jit(solution)/shard_map/pallas_call | solution.py:240
  54.8 0.0 collective-permute-done.8
  54.8 3.8 %shard_map.126 = bf16[2,2,512,1024]{3,2,1,0:T(8,128)(2,1)} custom-call(s32[1]{0:T(128)S(6)} %sub.3.place, bf16[2,512,1024]{2,1,0:T(8,128)(2,1)} %bitcast.4.half, bf16[2,2,512,1024]{3,2,1,0:T(8,128)(2,1)} %shard_map.125.refs_0_), custom_call_target="tpu_custom_call", output_to_operand_aliasing={{}: (2, {})} | custom-call | bytes 4194304 | tf_op jit(solution)/shard_map/pallas_call | solution.py:240
  58.6 3.4 %all-to-all-done.1 = bf16[32,32,128]{2,1,0:T(8,128)(2,1)S(1)} async-done(((bf16[32,32,128]{2,1,0:T(8,128)(2,1)}), bf16[32,32,128]{2,1,0:T(8,128)(2,1)S(1)}, u32[]{:S(2)}, u32[]{:S(2)}) %all-to-all-start.1) | async-done | bytes 262176 | tf_op jit(solution)/shard_map/all_to_all | solution.py:296
  62.0 0.7 %copy.17 = bf16[1,32,32,128]{3,2,1,0:T(8,128)(2,1)} copy(bf16[1,32,32,128]{3,2,1,0:T(8,128)(2,1)S(1)} %bitcast.14) | data formatting | bytes 524288
Async XLA Ops:
  4.3 38.9 %all-to-all-start = ((bf16[16,64,1024]{2,1,0:T(8,128)(2,1)}), bf16[16,64,1024]{2,1,0:T(8,128)(2,1)S(1)}, u32[]{:S(2)}, u32[]{:S(2)}) async-start(bf16[16,64,1024]{2,1,0:T(8,128)(2,1)} %shard_map.122), calls=%async_computation | async-start | bytes 4194304 | tf_op jit(solution)/shard_map/all_to_all | solution.py:271
  11.9 22.5 %copy-start = (s32[512,1]{0,1:T(1,128)S(1)}, s32[512,1]{0,1:T(1,128)}, u32[]{:S(2)}) copy-start(s32[512,1]{0,1:T(1,128)} %param.15) | copy-start | bytes 6148
  16.5 12.5 %collective-permute-start = (s16[528,128]{1,0:T(8,128)(2,1)S(1)}, s16[528,128]{1,0:T(8,128)(2,1)S(1)}, u32[]{:S(2)}, u32[]{:S(2)}) collective-permute-start(s16[528,128]{1,0:T(8,128)(2,1)S(1)} %get-tuple-element.27), channel_id=1, source_target_pairs={{0,1},{1,2},{2,3},{3,4},{4,5},{5,6},{6,7},{7,0},{8,9},{9,10},{10,1... | collective-permute-start | bytes 405512 | tf_op jit(solution)/shard_map/ppermute | solution.py:258
  18.2 10.8 %collective-permute-start.2 = (s16[528,128]{1,0:T(8,128)(2,1)S(1)}, s16[528,128]{1,0:T(8,128)(2,1)S(1)}, u32[]{:S(2)}, u32[]{:S(2)}) collective-permute-start(s16[528,128]{1,0:T(8,128)(2,1)S(1)} %get-tuple-element.30), channel_id=1, source_target_pairs={{0,7},{1,0},{2,1},{3,2},{4,3},{5,4},{6,5},{7,6},{8,15},{9,8},{10,9... | collective-permute-start | bytes 405512 | tf_op jit(solution)/shard_map/ppermute | solution.py:258
  22.2 6.6 %collective-permute-start.1 = (s16[272,128]{1,0:T(8,128)(2,1)S(1)}, s16[272,128]{1,0:T(8,128)(2,1)S(1)}, u32[]{:S(2)}, u32[]{:S(2)}) collective-permute-start(s16[272,128]{1,0:T(8,128)(2,1)S(1)} %get-tuple-element.28), channel_id=1, source_target_pairs={{0,2},{1,3},{2,4},{3,5},{4,6},{5,7},{6,0},{7,1},{8,10},{9,11},{10,... | collective-permute-start | bytes 208904 | tf_op jit(solution)/shard_map/ppermute | solution.py:258
  22.2 6.8 %collective-permute-start.3 = (s16[272,128]{1,0:T(8,128)(2,1)S(1)}, s16[272,128]{1,0:T(8,128)(2,1)S(1)}, u32[]{:S(2)}, u32[]{:S(2)}) collective-permute-start(s16[272,128]{1,0:T(8,128)(2,1)S(1)} %get-tuple-element.31), channel_id=1, source_target_pairs={{0,6},{1,7},{2,0},{3,1},{4,2},{5,3},{6,4},{7,5},{8,14},{9,15},{10,... | collective-permute-start | bytes 208904 | tf_op jit(solution)/shard_map/ppermute | solution.py:258
  29.3 8.2 %collective-permute-start.4 = (s16[528,128]{1,0:T(8,128)(2,1)S(1)}, s16[528,128]{1,0:T(8,128)(2,1)S(1)}, u32[]{:S(2)}, u32[]{:S(2)}) collective-permute-start(s16[528,128]{1,0:T(8,128)(2,1)S(1)} %get-tuple-element.42), channel_id=1, source_target_pairs={{0,1},{1,2},{2,3},{3,4},{4,5},{5,6},{6,7},{7,0},{8,9},{9,10},{10,1... | collective-permute-start | bytes 405512 | tf_op jit(solution)/shard_map/ppermute | solution.py:258
  29.4 8.1 %collective-permute-start.5 = (s16[528,128]{1,0:T(8,128)(2,1)S(1)}, s16[528,128]{1,0:T(8,128)(2,1)S(1)}, u32[]{:S(2)}, u32[]{:S(2)}) collective-permute-start(s16[528,128]{1,0:T(8,128)(2,1)S(1)} %get-tuple-element.43), channel_id=1, source_target_pairs={{0,7},{1,0},{2,1},{3,2},{4,3},{5,4},{6,5},{7,6},{8,15},{9,8},{10,9... | collective-permute-start | bytes 405512 | tf_op jit(solution)/shard_map/ppermute | solution.py:258
  32.0 9.8 %collective-permute-start.7 = (s16[528,128]{1,0:T(8,128)(2,1)S(1)}, s16[528,128]{1,0:T(8,128)(2,1)S(1)}, u32[]{:S(2)}, u32[]{:S(2)}) collective-permute-start(s16[528,128]{1,0:T(8,128)(2,1)S(1)} %get-tuple-element.33), channel_id=1, source_target_pairs={{0,6},{1,7},{2,0},{3,1},{4,2},{5,3},{6,4},{7,5},{8,14},{9,15},{10,... | collective-permute-start | bytes 405512 | tf_op jit(solution)/shard_map/ppermute | solution.py:258
  33.1 8.8 %collective-permute-start.6 = (s16[528,128]{1,0:T(8,128)(2,1)S(1)}, s16[528,128]{1,0:T(8,128)(2,1)S(1)}, u32[]{:S(2)}, u32[]{:S(2)}) collective-permute-start(s16[528,128]{1,0:T(8,128)(2,1)S(1)} %get-tuple-element.32), channel_id=1, source_target_pairs={{0,2},{1,3},{2,4},{3,5},{4,6},{5,7},{6,0},{7,1},{8,10},{9,11},{10,... | collective-permute-start | bytes 405512 | tf_op jit(solution)/shard_map/ppermute | solution.py:258
  43.2 11.6 %collective-permute-start.8 = (bf16[16,64,1024]{2,1,0:T(8,128)(2,1)S(1)}, bf16[16,64,1024]{2,1,0:T(8,128)(2,1)}, u32[]{:S(2)}, u32[]{:S(2)}) collective-permute-start(bf16[16,64,1024]{2,1,0:T(8,128)(2,1)S(1)} %all-to-all-done), channel_id=1, source_target_pairs={{0,64},{64,0},{1,65},{65,1},{2,66},{66,2},{3,67},{67,3},{4,68},{68... | collective-permute-start | bytes 6291464 | tf_op jit(solution)/shard_map/ppermute | solution.py:297
  45.7 16.2 %all-to-all-start.1 = ((bf16[32,32,128]{2,1,0:T(8,128)(2,1)}), bf16[32,32,128]{2,1,0:T(8,128)(2,1)S(1)}, u32[]{:S(2)}, u32[]{:S(2)}) async-start(bf16[32,32,128]{2,1,0:T(8,128)(2,1)} %bitcast.6), calls=%async_computation.1 | async-start | bytes 524288 | tf_op jit(solution)/shard_map/all_to_all | solution.py:296
